TPU v7x, 32 devices: a whole 2x2x4 slice. The times are simulated.
32 devices in a mesh: recv: 4 (over z), src: 8 (over y, x, core).
Axes of the slice: x: 2, y: 2, z: 4, core: 2. Of those that a mesh axis runs over, the one named last changes fastest.
Arguments:
- log_rate: float32 [65536], P(('recv', 'src')), may hold values from -2.5 to 2.5
- log_state: float32 [65536], P(('recv', 'src')), may hold values from -1 to 1.5
- a_sigma: float32 [65536], P(('recv', 'src')), may hold values from 1 to 4
- b_sigma: float32 [65536], P(('recv', 'src')), may hold values from 0.5 to 4
- crit_slip: float32 [65536], P(('recv', 'src')), may hold values from 0.5 to 4
- plate_rate: float32 [65536], P(('recv', 'src')), may hold values from 0.25 to 2
- cluster_order: int32 [32, 2048], P(('recv', 'src')), may hold values from 0 to 2047, each once within a row
- near_tiles: bfloat16 [3072, 128, 128], P(('recv', 'src')), may hold values from -1 to 1
- near_pairs: int32 [2, 3072], P(None, 'recv'), may hold values from 0 to 511, as said below
- far_u: bfloat16 [32768, 32, 128], P(('recv', 'src')), may hold values from -0.59765625 to 0.59765625
- far_v: bfloat16 [32768, 32, 128], P(('recv', 'src')), may hold values from -0.59765625 to 0.59765625
- far_pairs: int32 [2, 32768], P(None, ('recv', 'src')), may hold values from 0 to 511, as said below
- far_ranks: int32 [32768], P(('recv', 'src')), may hold values from 8 to 32
Outputs:
- new_log_rate: float32 [65536], P(('recv', 'src'))
- new_log_state: float32 [65536], P(('recv', 'src'))
Inputs may be any that keep to these rules, and one draw needn't show every extreme that they name: `cluster_order`: each row is a permutation of 0 to 2047. `near_pairs`: the tiles of device g (positions g * 96 onward) have receiver clusters among g's own clusters g * 16 to g * 16 + 15. The source group of a cluster c is (c // 16) % 8; of one device's tiles at most 24 have sources in one source group, and in every recv row one source group gets exactly 24 tiles from every device of that row. `far_pairs`: the blocks held by the device with recv index a and src index b have receiver clusters owned by devices of recv index a and source clusters in source group b.
All inputs are finite; a program needn't handle non-finite values.
Results may differ from a plain program's by a relative error of at most 0.0035.
Values may be sent and summed in bfloat16 or wider, within the bound.
No kernel may reach another device: no remote copies, remote signals or barrier semaphores. Data moves between devices by JAX's collectives and lax.ppermute only.
A program may use at most 128 MiB of HBM per device.

v0:
```python
import jax
import jax.numpy as jnp
from jax import lax
from jax.sharding import PartitionSpec as P

time_step = 0.1
damping = 0.5


def segment_rows(targets, contrib, count):
    wanted = lax.iota(jnp.int32, count)
    indicator = (targets[:, None] == wanted[None, :]).astype(jnp.float32)
    return lax.dot_general(
        indicator,
        contrib,
        (((0,), (0,)), ((), ())),
        precision=lax.Precision.HIGHEST,
        preferred_element_type=jnp.float32,
    )


def one_hot_rows(indices, count):
    return (indices[:, None] == lax.iota(jnp.int32, count)[None, :]).astype(jnp.bfloat16)


def pick_rows(selector, table):
    return jnp.dot(selector, table, preferred_element_type=jnp.float32).astype(jnp.bfloat16)


def on_device(
    log_rate,
    log_state,
    a_sigma,
    b_sigma,
    crit_slip,
    plate_rate,
    cluster_order,
    near_tiles,
    near_pairs,
    far_u,
    far_v,
    far_pairs,
    far_ranks,
):
    src_count = lax.axis_size("src")
    recv_count = lax.axis_size("recv")
    recv_index = lax.axis_index("recv")
    src_index = lax.axis_index("src")
    tile_count = near_tiles.shape[0]
    leaf_size = near_tiles.shape[1]
    elem_count = log_rate.shape[0]
    own_clusters = elem_count // leaf_size
    group_rows = own_clusters * src_count
    source_rows_count = own_clusters * recv_count
    capacity = max(2, 2 * tile_count // src_count)
    slot_count = src_count * capacity
    local_order = cluster_order[0]
    order_hot = (local_order[:, None] == lax.iota(jnp.int32, elem_count)[None, :]).astype(
        jnp.float32
    )
    stacked = jnp.stack([log_rate, log_state, a_sigma, b_sigma, crit_slip, plate_rate], 0)
    ordered = lax.dot_general(
        stacked,
        order_hot,
        (((1,), (1,)), ((), ())),
        precision=lax.Precision.HIGHEST,
        preferred_element_type=jnp.float32,
    )
    speed_log = ordered[0]
    theta_log = ordered[1]
    a_values = ordered[2]
    b_values = ordered[3]
    slip_scale = ordered[4]
    plate_values = ordered[5]
    pair_target = near_pairs[0].reshape(src_count, tile_count)
    pair_source = near_pairs[1].reshape(src_count, tile_count)
    destination = pair_source // own_clusters % src_count
    tile_ids = lax.iota(jnp.int32, tile_count)
    earlier = (destination[:, :, None] == destination[:, None, :]) & (
        tile_ids[None, None, :] < tile_ids[None, :, None]
    )
    slot_rank = jnp.sum(earlier.astype(jnp.int32), axis=2)
    source_col = pair_source // group_rows * own_clusters + pair_source % own_clusters
    target_row = pair_target - recv_index * group_rows
    cap_ids = lax.iota(jnp.int32, capacity)
    matches = (destination == src_index)[:, None, :] & (
        slot_rank[:, None, :] == cap_ids[None, :, None]
    )
    is_valid = jnp.any(matches, axis=2)
    slot_source = jnp.sum(jnp.where(matches, source_col[:, None, :], 0), axis=2).reshape(-1)
    slot_target = jnp.where(
        is_valid, jnp.sum(jnp.where(matches, target_row[:, None, :], 0), axis=2), group_rows
    ).reshape(-1)
    own_slot = destination[src_index] * capacity + slot_rank[src_index]
    far_target = far_pairs[0] - recv_index * group_rows
    far_source = far_pairs[1] // group_rows * own_clusters + far_pairs[1] % own_clusters
    rank_mask = lax.iota(jnp.int32, far_u.shape[1])[None, :] < far_ranks[:, None]
    far_hot = one_hot_rows(far_source, source_rows_count)
    slot_hot = one_hot_rows(slot_source, source_rows_count)
    slot_ids = lax.iota(jnp.int32, slot_count)
    relay_hot = (own_slot[None, :] == slot_ids[:, None]).astype(jnp.bfloat16)
    selected = pick_rows(relay_hot, near_tiles.reshape(tile_count, -1)).reshape(
        slot_count, leaf_size, leaf_size
    )
    relayed = lax.all_to_all(selected, "src", split_axis=0, concat_axis=0, tiled=True)

    def rates(speed_now, theta_now):
        slip_speed = jnp.exp(speed_now)
        deficit = (plate_values - slip_speed).astype(jnp.bfloat16).reshape(own_clusters, leaf_size)
        columns = lax.all_gather(deficit, "recv", axis=0, tiled=True)
        far_rows = pick_rows(far_hot, columns)
        coefficients = jnp.einsum("tkj,tj->tk", far_v, far_rows, preferred_element_type=jnp.float32)
        coefficients = jnp.where(rank_mask, coefficients, 0.0).astype(jnp.bfloat16)
        far_terms = jnp.einsum(
            "tki,tk->ti", far_u, coefficients, preferred_element_type=jnp.float32
        )
        near_terms = jnp.einsum(
            "sij,sj->si", relayed, pick_rows(slot_hot, columns), preferred_element_type=jnp.float32
        )
        all_terms = jnp.concatenate([near_terms, far_terms], 0)
        all_targets = jnp.concatenate([slot_target, far_target], 0)
        whole_sum = lax.psum(
            segment_rows(all_targets, all_terms, group_rows).astype(jnp.bfloat16), "src"
        ).astype(jnp.float32)
        stress = lax.dynamic_slice_in_dim(whole_sum, src_index * own_clusters, own_clusters, 0)
        stress = stress.reshape(-1)
        theta_rate = jnp.exp(-theta_now) - slip_speed / slip_scale
        speed_rate = (stress - b_values * theta_rate) / (a_values + damping * slip_speed)
        return (speed_rate, theta_rate)

    first_p, first_q = rates(speed_log, theta_log)
    second_p, second_q = rates(speed_log + time_step * first_p, theta_log + time_step * first_q)
    new_speed = speed_log + 0.5 * time_step * (first_p + second_p)
    new_theta = theta_log + 0.5 * time_step * (first_q + second_q)
    results = jnp.dot(
        jnp.stack([new_speed, new_theta], 0),
        order_hot,
        precision=lax.Precision.HIGHEST,
        preferred_element_type=jnp.float32,
    )
    return (results[0], results[1])


def solution(mesh):
    return jax.shard_map(
        on_device,
        mesh=mesh,
        in_specs=(
            P(("recv", "src")),
            P(("recv", "src")),
            P(("recv", "src")),
            P(("recv", "src")),
            P(("recv", "src")),
            P(("recv", "src")),
            P(("recv", "src"), None),
            P(("recv", "src"), None, None),
            P(None, "recv"),
            P(("recv", "src"), None, None),
            P(("recv", "src"), None, None),
            P(None, ("recv", "src")),
            P(("recv", "src")),
        ),
        out_specs=(P(("recv", "src")), P(("recv", "src"))),
        check_vma=False,
    )
```

profile of v0, /device:TPU:0, one launch (start us, length us, event | category | flops | bytes accessed | tf_op | source)
XLA Modules:
  0.0 182.0 jit_solution(13465353964437333459)
XLA Ops:
  0.7 0.8 subtract_reduce_fusion
  1.5 0.4 convert_reduce_fusion
  1.9 4.5 %fusion.6 = bf16[24,8,128,128]{3,1,2,0:T(8,128)(2,1)S(1)} fusion(bf16[12,8,128,128]{3,2,1,0:T(8,128)(2,1)} %bitcast.66, s32[96]{0:T(128)S(1)} %fusion.61), kind=kOutput, calls=%fused_computation.8 | convolution fusion | flops 607143936 | bytes 9437568 | tf_op jit(solution)/shard_map/dot_general | solution.py:27
  6.4 4.6 %copy.28 = bf16[24,8,128,128]{3,2,1,0:T(8,128)(2,1)} copy(bf16[24,8,128,128]{3,1,2,0:T(8,128)(2,1)S(1)} %fusion.6) | data formatting | bytes 12582912
  11.0 5.3 %all-to-all-start = ((bf16[192,128,128]{2,1,0:T(8,128)(2,1)}), bf16[192,128,128]{2,1,0:T(8,128)(2,1)}, u32[]{:S(2)}, u32[]{:S(2)}) async-start(bf16[192,128,128]{2,1,0:T(8,128)(2,1)} %bitcast.65), calls=%async_computation | async-start | bytes 12582912 | tf_op jit(solution)/shard_map/all_to_all | solution.py:105
  16.5 0.3 select_reduce_fusion.1
  17.4 7.5 %fusion.1 = f32[6,2048]{1,0:T(8,128)S(1)} fusion(f32[6,2048]{1,0:T(8,128)S(1)} %stack.32, s32[2048]{0:T(1024)S(1)} %bitcast.91), kind=kOutput, calls=%fused_computation.3 | convolution fusion | flops 306184192 | bytes 106496 | tf_op jit(solution)/shard_map/dot_general | solution.py:62
  24.9 14.6 %all_gather.6 = bf16[64,128]{1,0:T(8,128)(2,1)S(1)} all-gather(bf16[16,128]{1,0:T(8,128)(2,1)S(1)} %fusion.45), channel_id=1, replica_groups=mesh['recv'=4,'src'=8] {'recv'}, dimensions={0}, use_global_device_ids=true | all-gather | bytes 20480 | tf_op jit(solution)/shard_map/all_gather | solution.py:110
  39.8 0.3 fusion.9
  40.2 7.8 %fusion.25 = f32[1024,1,32]{2,1,0:T(1,128)S(1)} fusion(bf16[1024,32,128]{2,1,0:T(8,128)(2,1)} %param.23, bf16[1024,128,1]{1,0,2:T(8,128)(2,1)S(1)} %fusion.9), kind=kOutput, calls=%fused_computation.32 | convolution fusion | flops 8388608 | bytes 8781824 | tf_op jit(solution)/shard_map/tkj,tj->tk/dot_general | solution.py:112
  48.2 5.6 %fusion.23 = f32[1024,1,128]{2,1,0:T(1,128)S(1)} fusion(bf16[1024,32,128]{2,1,0:T(8,128)(2,1)} %param.22, bf16[1024,32,1]{1,0,2:T(8,128)(2,1)S(1)} %fusion.29), kind=kOutput, calls=%fused_computation.30 | convolution fusion | flops 8388608 | bytes 8978432 | tf_op jit(solution)/shard_map/tki,tk->ti/dot_general | solution.py:114
  53.8 34.4 %all-to-all-done = bf16[192,128,128]{2,1,0:T(8,128)(2,1)} async-done(((bf16[192,128,128]{2,1,0:T(8,128)(2,1)}), bf16[192,128,128]{2,1,0:T(8,128)(2,1)}, u32[]{:S(2)}, u32[]{:S(2)}) %all-to-all-start) | async-done | bytes 6291488 | tf_op jit(solution)/shard_map/all_to_all | solution.py:105
  88.2 6.1 %fusion.35 = f32[192,1,128]{2,1,0:T(1,128)S(1)} fusion(bf16[192,128,128]{2,1,0:T(8,128)(2,1)} %all-to-all-done, bf16[192,128,1]{1,0,2:T(8,128)(2,1)S(1)} %fusion.11), kind=kOutput, calls=%fused_computation.47 | convolution fusion | flops 6291456 | bytes 6438912 | tf_op jit(solution)/shard_map/sij,sj->si/dot_general | solution.py:117
  94.3 0.9 convolution_convert_fusion.6
  95.3 22.4 %psum.14 = bf16[128,128]{1,0:T(8,128)(2,1)S(1)} all-reduce(bf16[128,128]{1,0:T(8,128)(2,1)S(1)} %convolution_convert_fusion.6), channel_id=1, replica_groups=mesh['recv'=4,'src'=8] {'src'}, use_global_device_ids=true, to_apply=%region_4.5 | all-reduce | flops 16384 | bytes 65536 | tf_op jit(solution)/shard_map/psum | solution.py:122
  117.7 14.3 %all_gather.7 = bf16[64,128]{1,0:T(8,128)(2,1)S(1)} all-gather(bf16[16,128]{1,0:T(8,128)(2,1)S(1)} %subtract_convert_fusion), channel_id=1, replica_groups=mesh['recv'=4,'src'=8] {'recv'}, dimensions={0}, use_global_device_ids=true | all-gather | bytes 20480 | tf_op jit(solution)/shard_map/all_gather | solution.py:110
  132.3 0.3 fusion.10
  132.6 7.8 %fusion.21 = f32[1024,1,32]{2,1,0:T(1,128)S(1)} fusion(bf16[1024,32,128]{2,1,0:T(8,128)(2,1)} %param.23, bf16[1024,128,1]{1,0,2:T(8,128)(2,1)S(1)} %fusion.10), kind=kOutput, calls=%fused_computation.28 | convolution fusion | flops 8388608 | bytes 8781824 | tf_op jit(solution)/shard_map/tkj,tj->tk/dot_general | solution.py:112
  140.6 5.6 %fusion.19 = f32[1024,1,128]{2,1,0:T(1,128)S(1)} fusion(bf16[1024,32,128]{2,1,0:T(8,128)(2,1)} %param.22, bf16[1024,32,1]{1,0,2:T(8,128)(2,1)S(1)} %fusion.30), kind=kOutput, calls=%fused_computation.26 | convolution fusion | flops 8388608 | bytes 8978432 | tf_op jit(solution)/shard_map/tki,tk->ti/dot_general | solution.py:114
  146.3 6.1 %fusion.33 = f32[192,1,128]{2,1,0:T(1,128)S(1)} fusion(bf16[192,128,128]{2,1,0:T(8,128)(2,1)} %all-to-all-done, bf16[192,128,1]{1,0,2:T(8,128)(2,1)S(1)} %fusion.12), kind=kOutput, calls=%fused_computation.45 | convolution fusion | flops 6291456 | bytes 6438912 | tf_op jit(solution)/shard_map/sij,sj->si/dot_general | solution.py:117
  152.4 0.9 convolution_convert_fusion.5
  153.3 22.6 %psum.15 = bf16[128,128]{1,0:T(8,128)(2,1)S(1)} all-reduce(bf16[128,128]{1,0:T(8,128)(2,1)S(1)} %convolution_convert_fusion.5), channel_id=1, replica_groups=mesh['recv'=4,'src'=8] {'src'}, use_global_device_ids=true, to_apply=%region_5.6 | all-reduce | flops 16384 | bytes 65536 | tf_op jit(solution)/shard_map/psum | solution.py:122
  176.1 5.3 %fusion = f32[2,2048]{1,0:T(2,128)S(1)} fusion(s32[2048]{0:T(1024)S(1)} %bitcast.92, f32[1,2048]{1,0:T(1,128)S(1)} %multiply_add_fusion, f32[1,2048]{1,0:T(1,128)S(1)} %get-tuple-element.6), kind=kOutput, calls=%fused_computation.2 | convolution fusion | flops 104861696 | bytes 40960 | tf_op jit(solution)/shard_map/dot_general | solution.py:135
  181.4 0.6 fusion.66
  (44 shorter events, 1.9 us)
Async XLA Ops:
  11.0 6.2 %copy-start.1 = (f32[2048]{0:T(1024)S(1)}, f32[2048]{0:T(1024)}, u32[]{:S(2)}) copy-start(f32[2048]{0:T(1024)} %param.13) | copy-start | bytes 24580
  11.0 6.2 %copy-start.2 = (f32[2048]{0:T(1024)S(1)}, f32[2048]{0:T(1024)}, u32[]{:S(2)}) copy-start(f32[2048]{0:T(1024)} %param.14) | copy-start | bytes 24580
  11.0 6.2 %copy-start.3 = (f32[2048]{0:T(1024)S(1)}, f32[2048]{0:T(1024)}, u32[]{:S(2)}) copy-start(f32[2048]{0:T(1024)} %param.15) | copy-start | bytes 24580
  11.0 6.2 %copy-start.4 = (f32[2048]{0:T(1024)S(1)}, f32[2048]{0:T(1024)}, u32[]{:S(2)}) copy-start(f32[2048]{0:T(1024)} %param.16) | copy-start | bytes 24580
  11.0 6.2 %copy-start.5 = (f32[2048]{0:T(1024)S(1)}, f32[2048]{0:T(1024)}, u32[]{:S(2)}) copy-start(f32[2048]{0:T(1024)} %param.17) | copy-start | bytes 24580
  11.0 6.2 %copy-start.6 = (f32[2048]{0:T(1024)S(1)}, f32[2048]{0:T(1024)}, u32[]{:S(2)}) copy-start(f32[2048]{0:T(1024)} %param.18) | copy-start | bytes 24580
  11.0 6.3 %copy-start.8 = (s32[1,2048]{1,0:T(1,128)S(1)}, s32[1,2048]{1,0:T(1,128)}, u32[]{:S(2)}) copy-start(s32[1,2048]{1,0:T(1,128)} %param.19) | copy-start | bytes 24580
  11.0 28.5 %copy-start.7 = (s32[2,1024]{1,0:T(2,128)S(1)}, s32[2,1024]{1,0:T(2,128)}, u32[]{:S(2)}) copy-start(s32[2,1024]{1,0:T(2,128)} %param.24) | copy-start | bytes 24580
  11.0 77.2 %all-to-all-start = ((bf16[192,128,128]{2,1,0:T(8,128)(2,1)}), bf16[192,128,128]{2,1,0:T(8,128)(2,1)}, u32[]{:S(2)}, u32[]{:S(2)}) async-start(bf16[192,128,128]{2,1,0:T(8,128)(2,1)} %bitcast.65), calls=%async_computation | async-start | bytes 12582912 | tf_op jit(solution)/shard_map/all_to_all | solution.py:105
  16.4 31.6 %copy-start = (s32[1024]{0:T(1024)S(1)}, s32[1024]{0:T(1024)}, u32[]{:S(2)}) copy-start(s32[1024]{0:T(1024)} %param.25) | copy-start | bytes 12292
where the time goes:
time: 183 us; the launch traced here: 182 us
  blocking collectives  73.9 us (40%)
  matrix products  59.4 us (32%)
  waiting for transfers between devices  34.4 us (19%)
  local copies, waits for them, and re-layouts  5.65 us (3%)
  starting transfers between devices  5.31 us (3%)
  other arithmetic  2.53 us (1%)
    psum x2, blocking collectives, rates(): lax.psum(segment_rows(all_targets, all_terms, group_rows).astype(jnp.bflo...  45 us
    all_to_all x1, waiting for transfers between devices, on_device(): lax.all_to_all(selected, 'src', split_axis=0, concat_axis=0, tiled=True)  34.4 us
    all_gather x2, blocking collectives, rates(): columns = lax.all_gather(deficit, 'recv', axis=0, tiled=True)  28.9 us
    dot_general x2, matrix products, rates(): jnp.einsum('tkj,tj->tk', far_v, far_rows, preferred_element_type=jnp.floa...  15.6 us
    dot_general x2, matrix products, rates(): jnp.einsum('sij,sj->si', relayed, pick_rows(slot_hot, columns), preferred...  12.2 us
    dot_general x2, matrix products, rates(): jnp.einsum('tki,tk->ti', far_u, coefficients, preferred_element_type=jnp....  11.3 us
    dot_general x1, matrix products, on_device(): lax.dot_general(stacked, order_hot, (((1,), (1,)), ((), ())), precision=l...  7.52 us
    dot_general x5, matrix products, pick_rows(): jnp.dot(selector, table, preferred_element_type=jnp.float32)  5.55 us
  transfers between devices with their start and end apart: 1, of which 1 were waited for; matrix products, arithmetic and copies ran while one was open for 12% of the time, Pallas kernels for 0%

commit v1 on v0

v1 whole, which is shorter than its diff:
```python
import functools

import jax
import jax.numpy as jnp
from jax import lax
from jax.experimental import pallas as pl
from jax.experimental.pallas import tpu as pltpu
from jax.sharding import PartitionSpec as P

time_step = 0.1
damping = 0.5
f32 = jnp.float32
bf16 = jnp.bfloat16
lanes = 128
chunks = 8
vmem_bytes = 40 * 2**20
by_row = (((1,), (1,)), ((), ()))
in_vmem = pl.BlockSpec(memory_space=pltpu.VMEM)
in_smem = pl.BlockSpec(memory_space=pltpu.SMEM)
anywhere = pl.BlockSpec(memory_space=pl.ANY)


def order_kernel(p_ref, q_ref, a_ref, b_ref, slip_ref, plate_ref, order_ref, own_ref, shared_ref, deficit_ref):
    order = order_ref[...]
    row, lane = order // lanes, order % lanes
    rows = order.shape[0]
    refs = (p_ref, q_ref, a_ref, b_ref, slip_ref, plate_ref)
    sorted_values = [jnp.zeros(order.shape, f32)] * len(refs)
    for r in range(rows):
        here = row == r
        for k, ref in enumerate(refs):
            spread = jnp.broadcast_to(ref[r : r + 1, :], order.shape)
            got = jnp.take_along_axis(spread, lane, axis=1)
            sorted_values[k] = jnp.where(here, got, sorted_values[k])
    p, q, a, b, slip, plate = sorted_values
    speed = jnp.exp(p)
    theta_rate = jnp.exp(-q) - speed / slip
    gain = 1.0 / (a + damping * speed)
    for k, value in enumerate((p, q, a, b, slip, plate, theta_rate, gain)):
        own_ref[k] = value
    shared_ref[0] = p - time_step * b * theta_rate * gain
    shared_ref[1] = time_step * gain
    shared_ref[2] = plate
    deficit_ref[...] = (plate - speed).astype(bf16)


def table_kernel(source_ref, target_ref, rank_ref, source_out, target_out, *, rank):
    per_row = lanes // rank
    group = lanes // per_row
    shape = (group, lanes)
    lane = lax.broadcasted_iota(jnp.int32, shape, 1)
    pick = lax.broadcasted_iota(jnp.int32, shape, 0) * per_row + lane // rank
    for a in range(source_ref.shape[0]):
        def spread(ref):
            return jnp.take_along_axis(jnp.broadcast_to(ref[a : a + 1, :], shape), pick, axis=1)

        where = slice(a * group, (a + 1) * group)
        source_out[where, :] = jnp.where(lane % rank < spread(rank_ref), spread(source_ref), -1)
        target_out[where, :] = spread(target_ref).astype(f32)


def far_part(source_ref, target_ref, deficit_ref, v_buf, u_buf, out_ref, before):
    factor_rows = v_buf.shape[0]
    part = factor_rows // chunks
    source_count = deficit_ref.shape[0]
    target_count = out_ref.shape[0]
    deficit = deficit_ref[...]
    source_ids = lax.broadcasted_iota(jnp.int32, (source_count, lanes), 0)
    target_ids = [
        (lax.broadcasted_iota(jnp.int32, (16, lanes), 0) + 16 * k).astype(f32).astype(bf16)
        for k in range(target_count // 16)
    ]
    out_ref[...] = jnp.zeros_like(out_ref)

    def step(i, _):
        before(i)
        base = pl.multiple_of(i * part, part)
        products = lax.dot_general(
            deficit, v_buf[pl.ds(base, part), :], by_row, preferred_element_type=f32
        )
        spread = []
        for k in range(part // lanes):
            row = i * (part // lanes) + k
            source = source_ref[pl.ds(row, 1), :]
            target = jnp.broadcast_to(target_ref[pl.ds(row, 1), :], (16, lanes)).astype(bf16)
            coef = jnp.sum(
                jnp.where(source_ids == source, products[:, k * lanes : (k + 1) * lanes], 0.0),
                axis=0,
                keepdims=True,
            )
            coef = jnp.broadcast_to(coef, (16, lanes)).astype(bf16)
            spread.append(
                jnp.concatenate(
                    [jnp.where(ids == target, coef, jnp.zeros_like(coef)) for ids in target_ids], 0
                )
            )
        out_ref[...] += jnp.dot(
            jnp.concatenate(spread, 1), u_buf[pl.ds(base, part), :], preferred_element_type=f32
        )
        return 0

    lax.fori_loop(0, chunks, step, 0)


def near_part(source_ref, target_ref, columns_ref, tile_buf, columns_buf, count):
    tile_count = tile_buf.shape[0]
    columns_buf[...] = columns_ref[...].astype(f32)
    ids = lax.broadcasted_iota(jnp.int32, (count, lanes), 0)
    total = jnp.zeros((count, lanes), f32)
    for t in range(tile_count):
        deficit = jnp.broadcast_to(columns_buf[pl.ds(source_ref[t], 1), :], (count, lanes))
        placed = jnp.where(ids == target_ref[t], deficit, 0.0).astype(bf16)
        total += lax.dot_general(placed, tile_buf[t], by_row, preferred_element_type=f32)
    return total


def far_copies(v_hbm, u_hbm, v_buf, u_buf, sems):
    part = v_hbm.shape[0] // chunks

    def copies(i):
        where = pl.ds(pl.multiple_of(i * part, part), part)
        return (
            pltpu.make_async_copy(v_hbm.at[where], v_buf.at[where], sems.at[0, i]),
            pltpu.make_async_copy(u_hbm.at[where], u_buf.at[where], sems.at[1, i]),
        )

    return copies


def both_kernel(
    near_source, near_target, own_row, source_ref, target_ref, deficit_ref, columns_ref, v_hbm, u_hbm, tiles_hbm,
    out_ref, v_buf, u_buf, tile_buf, columns_buf, total_ref, sems, tile_sem,
):
    copies = far_copies(v_hbm, u_hbm, v_buf, u_buf, sems)
    for i in range(chunks):
        for copy in copies(i):
            copy.start()
    tile_copy = pltpu.make_async_copy(tiles_hbm, tile_buf, tile_sem)
    tile_copy.start()

    def before(i):
        for copy in copies(i):
            copy.wait()

    far_part(source_ref, target_ref, deficit_ref, v_buf, u_buf, total_ref, before)
    tile_copy.wait()
    count = out_ref.shape[1]
    near = near_part(near_source, near_target, columns_ref, tile_buf, columns_buf, count)
    own = pl.ds(pl.multiple_of(own_row[0] * count, count), count)
    total_ref[own, :] += near
    out_ref[...] = jnp.broadcast_to(
        total_ref[...].astype(bf16).reshape(1, -1, count, lanes), (out_ref.shape[0] // (total_ref.shape[0] // count), total_ref.shape[0] // count, count, lanes)
    ).reshape(out_ref.shape)


def far_kernel(
    source_ref, target_ref, deficit_ref, v_hbm, u_hbm, out_ref, v_buf, u_buf, total_ref, sems
):
    copies = far_copies(v_hbm, u_hbm, v_buf, u_buf, sems)
    for i in range(chunks):
        for copy in copies(i):
            copy.start()

    def before(i):
        for copy in copies(i):
            copy.wait()

    far_part(source_ref, target_ref, deficit_ref, v_buf, u_buf, total_ref, before)
    out_ref[...] = total_ref[...].astype(bf16)


def near_kernel(near_source, near_target, columns_ref, tile_buf, out_ref, columns_buf):
    out_ref[...] = near_part(
        near_source, near_target, columns_ref, tile_buf, columns_buf, out_ref.shape[0]
    )


def final_kernel(own_ref, first_ref, second_ref, near_ref, order_ref, p_out, q_out):
    p, q, a, b, slip, plate, theta_rate, gain = [own_ref[k] for k in range(8)]
    first_p = (first_ref[...] - b * theta_rate) * gain
    speed = jnp.exp(p + time_step * first_p)
    second_q = jnp.exp(-(q + time_step * theta_rate)) - speed / slip
    stress = jnp.sum(second_ref[...].astype(f32), axis=0) + near_ref[...]
    second_p = (stress - b * second_q) / (a + damping * speed)
    new_p = p + 0.5 * time_step * (first_p + second_p)
    new_q = q + 0.5 * time_step * (theta_rate + second_q)
    pieces = []
    for value in (new_p, new_q):
        for _ in range(3):
            piece = value.astype(bf16).astype(f32)
            value = value - piece
            pieces.append(piece)
    rows = p.shape[0]
    order = order_ref[...]
    row, lane = order // lanes, order % lanes
    row_ids = lax.broadcasted_iota(jnp.int32, (rows, lanes), 0)
    lane_ids = lax.broadcasted_iota(jnp.int32, (lanes, lanes), 0)
    total = jnp.zeros((len(pieces) * rows, lanes), f32)
    for r in range(rows):
        here = row_ids == row[r : r + 1, :]
        placed = jnp.concatenate(
            [jnp.where(here, piece[r : r + 1, :], 0.0) for piece in pieces], 0
        ).astype(bf16)
        spread = jnp.where(lane_ids == lane[r : r + 1, :], 1.0, 0.0).astype(bf16)
        total += lax.dot_general(placed, spread, by_row, preferred_element_type=f32)
    for k, out in enumerate((p_out, q_out)):
        high, mid, low = [total[(3 * k + j) * rows : (3 * k + j + 1) * rows, :] for j in range(3)]
        out[...] = (low + mid) + high


def on_device(
    log_rate,
    log_state,
    a_sigma,
    b_sigma,
    crit_slip,
    plate_rate,
    cluster_order,
    near_tiles,
    near_pairs,
    far_u,
    far_v,
    far_pairs,
    far_ranks,
):
    src_count = lax.axis_size("src")
    recv_count = lax.axis_size("recv")
    device_count = src_count * recv_count
    recv_index = lax.axis_index("recv")
    src_index = lax.axis_index("src")
    tile_count = near_tiles.shape[0]
    own_clusters = log_rate.shape[0] // lanes
    group_rows = own_clusters * src_count
    source_rows = own_clusters * recv_count
    far_count, rank = far_u.shape[:2]
    factor_rows = far_count * rank
    params = pltpu.CompilerParams(vmem_limit_bytes=vmem_bytes)
    whole = (own_clusters, lanes)

    order = cluster_order.reshape(whole)
    own, shared, deficit = pl.pallas_call(
        order_kernel,
        out_shape=(
            jax.ShapeDtypeStruct((8,) + whole, f32),
            jax.ShapeDtypeStruct((3,) + whole, f32),
            jax.ShapeDtypeStruct(whole, bf16),
        ),
    )(*[x.reshape(whole) for x in (log_rate, log_state, a_sigma, b_sigma, crit_slip, plate_rate)], order)

    columns = lax.all_to_all(
        jnp.broadcast_to(deficit[None], (device_count,) + whole),
        ("recv", "src"), split_axis=0, concat_axis=0, tiled=True,
    )
    shared_columns = lax.all_gather(shared, "recv", axis=1, tiled=True)

    near_own = lax.dynamic_slice_in_dim(near_pairs, src_index * tile_count, tile_count, 1)
    near_target = near_own[0] - (recv_index * group_rows + src_index * own_clusters)
    near_source = near_own[1]
    far_target = far_pairs[0] - recv_index * group_rows
    far_source = far_pairs[1] // group_rows * own_clusters + far_pairs[1] % own_clusters
    table = (factor_rows // lanes, lanes)
    source_table, target_table = pl.pallas_call(
        functools.partial(table_kernel, rank=rank),
        out_shape=(jax.ShapeDtypeStruct(table, jnp.int32), jax.ShapeDtypeStruct(table, f32)),
    )(*[x.reshape(far_count // lanes, lanes) for x in (far_source, far_target, far_ranks)])

    v_rows = far_v.reshape(factor_rows, lanes)
    u_rows = far_u.reshape(factor_rows, lanes)
    far_scratch = [
        pltpu.VMEM(v_rows.shape, bf16),
        pltpu.VMEM(u_rows.shape, bf16),
    ]
    total_scratch = pltpu.VMEM((group_rows, lanes), f32)
    columns_scratch = pltpu.VMEM((own_clusters * device_count, lanes), f32)
    far_sems = pltpu.SemaphoreType.DMA((2, chunks))

    group_columns = lax.dynamic_index_in_dim(
        columns.reshape((recv_count, src_count) + whole), src_index, 1, keepdims=False
    ).reshape(source_rows, lanes)
    partial = pl.pallas_call(
        both_kernel,
        in_specs=[in_smem] * 3 + [in_vmem] * 4 + [anywhere] * 3,
        out_specs=in_vmem,
        out_shape=jax.ShapeDtypeStruct((device_count,) + whole, bf16),
        scratch_shapes=far_scratch
        + [pltpu.VMEM(near_tiles.shape, bf16), columns_scratch, total_scratch, far_sems, pltpu.SemaphoreType.DMA],
        compiler_params=params,
    )(
        near_source, near_target, src_index.reshape(1), source_table, target_table,
        group_columns, columns.reshape(-1, lanes), v_rows, u_rows, near_tiles,
    )
    stress_parts = lax.all_to_all(
        partial, ("recv", "src"), split_axis=0, concat_axis=0, tiled=True
    )
    first_stress = jnp.sum(
        stress_parts.reshape((recv_count, src_count) + whole).astype(f32), axis=1
    )
    second_deficit = (
        shared_columns[2]
        - jnp.exp(shared_columns[0] + shared_columns[1] * first_stress.reshape(-1, lanes))
    ).astype(bf16)
    own_stress = lax.dynamic_index_in_dim(first_stress, recv_index, 0, keepdims=False)

    by_group = lax.all_gather(second_deficit.reshape((1, recv_count) + whole), "src", axis=0, tiled=True)
    second_columns = by_group.transpose(1, 0, 2, 3).reshape(-1, lanes)
    far_second = pl.pallas_call(
        far_kernel,
        in_specs=[in_vmem] * 3 + [anywhere] * 2,
        out_specs=in_vmem,
        out_shape=jax.ShapeDtypeStruct((group_rows, lanes), bf16),
        scratch_shapes=far_scratch + [total_scratch, far_sems],
        compiler_params=params,
    )(source_table, target_table, second_deficit, v_rows, u_rows)
    second_parts = lax.all_to_all(far_second, "src", split_axis=0, concat_axis=0, tiled=True)
    near_second = pl.pallas_call(
        near_kernel,
        in_specs=[in_smem] * 2 + [in_vmem] * 2,
        out_specs=in_vmem,
        out_shape=jax.ShapeDtypeStruct(whole, f32),
        scratch_shapes=[columns_scratch],
        compiler_params=params,
    )(near_source, near_target, second_columns, near_tiles)
    new_p, new_q = pl.pallas_call(
        final_kernel,
        out_shape=(jax.ShapeDtypeStruct(whole, f32), jax.ShapeDtypeStruct(whole, f32)),
    )(own, own_stress, second_parts.reshape((src_count,) + whole), near_second, order)
    return new_p.reshape(-1), new_q.reshape(-1)


def solution(mesh):
    return jax.shard_map(
        on_device,
        mesh=mesh,
        in_specs=(
            P(("recv", "src")),
            P(("recv", "src")),
            P(("recv", "src")),
            P(("recv", "src")),
            P(("recv", "src")),
            P(("recv", "src")),
            P(("recv", "src"), None),
            P(("recv", "src"), None, None),
            P(None, "recv"),
            P(("recv", "src"), None, None),
            P(("recv", "src"), None, None),
            P(None, ("recv", "src")),
            P(("recv", "src")),
        ),
        out_specs=(P(("recv", "src")), P(("recv", "src"))),
        check_vma=False,
    )
```

time: 183 us -> 86.1 us (0.47)
  matrix products: 59.4 us -> 0 us
  blocking collectives: 73.9 us -> 24 us
  waiting for transfers between devices: 34.4 us -> 4.43 us
  Pallas kernels: 0 us -> 26.8 us
  starting transfers between devices: 5.31 us -> 13.6 us
  local copies, waits for them, and re-layouts: 5.65 us -> 13.8 us
    dot_general x15 -> x0, matrix products: 59.4 us -> none  [the longest x2 15.6 us: rates(): jnp.einsum('tkj,tj->tk', far_v, far_rows, preferred_element_type=jnp.floa...]
    psum x2 -> x0, blocking collectives: 45 us -> none  [rates(): lax.psum(segment_rows(all_targets, all_terms, group_rows).astype(jnp.bflo...]
    all_to_all x1 -> x3, waiting for transfers between devices: 34.4 us -> 4.43 us  [the longest x1 4.43 us: on_device(): lax.all_to_all(jnp.broadcast_to(deficit[None], (device_count,) + whole),...]
    pallas_call x0 -> x6, Pallas kernels: none -> 26.8 us  [the longest x1 10.7 us: on_device(): pl.pallas_call(both_kernel, in_specs=[in_smem] * 3 + [in_vmem] * 4 + [any...]
    all_to_all x1 -> x3, starting transfers between devices: 5.31 us -> 13.6 us  [the longest x1 7.3 us: on_device(): lax.all_to_all(jnp.broadcast_to(deficit[None], (device_count,) + whole),...]
    unnamed x19 -> x24, local copies, waits for them, and re-layouts: 4.62 us -> 11.7 us
    all_gather x2, blocking collectives: 28.9 us -> 24 us  [the longest x1 14.3 us: on_device(): shared_columns = lax.all_gather(shared, 'recv', axis=1, tiled=True)]
  transfers between devices with their start and end apart: 1 -> 3, of which waited for: 1 -> 1; matrix products, arithmetic and copies ran while one was open for 12% -> 2% of each run, Pallas kernels for 0% -> 5%
where the time goes in v1:
time: 86.1 us; the launch traced here: 85.4 us
  Pallas kernels  26.8 us (31%)
  blocking collectives  24 us (28%)
  local copies, waits for them, and re-layouts  13.8 us (16%)
  starting transfers between devices  13.6 us (16%)
  waiting for transfers between devices  4.43 us (5%)
  other arithmetic  2.04 us (2%)
    all_gather x1, blocking collectives, on_device(): shared_columns = lax.all_gather(shared, 'recv', axis=1, tiled=True)  14.3 us
    unnamed x24, local copies, waits for them, and re-layouts  11.7 us
    pallas_call x1, Pallas kernels, on_device(): pl.pallas_call(both_kernel, in_specs=[in_smem] * 3 + [in_vmem] * 4 + [any...  10.7 us
    all_gather x1, blocking collectives, on_device(): lax.all_gather(second_deficit.reshape((1, recv_count) + whole), 'src', ax...  9.73 us
    pallas_call x1, Pallas kernels, on_device(): pl.pallas_call(far_kernel, in_specs=[in_vmem] * 3 + [anywhere] * 2, out_s...  8.48 us
    all_to_all x1, starting transfers between devices, on_device(): lax.all_to_all(jnp.broadcast_to(deficit[None], (device_count,) + whole),...  7.3 us
    all_to_all x1, waiting for transfers between devices, on_device(): lax.all_to_all(jnp.broadcast_to(deficit[None], (device_count,) + whole),...  4.43 us
    all_to_all x1, starting transfers between devices, on_device(): lax.all_to_all(far_second, 'src', split_axis=0, concat_axis=0, tiled=True)  3.73 us
  transfers between devices with their start and end apart: 3, of which 1 were waited for; matrix products, arithmetic and copies ran while one was open for 2% of the time, Pallas kernels for 5%

profile of v1, /device:TPU:0, one launch (start us, length us, event | category | flops | bytes accessed | tf_op | source)
XLA Modules:
  0.0 85.4 jit_solution(6520120554464186433)
XLA Ops:
  0.6 1.7 %shard_map.140 = (f32[8,16,128]{2,1,0:T(8,128)}, f32[3,16,128]{2,1,0:T(8,128)}, bf16[16,128]{1,0:T(8,128)(2,1)}) custom-call(f32[16,128]{1,0:T(8,128)} %bitcast.77, f32[16,128]{1,0:T(8,128)} %bitcast.78, f32[16,128]{1,0:T(8,128)} %bitcast.79, f32[16,128]{1,0:T(8,128)} %bitcast.80, f32[16,128]{1,0:T(8,128)} %bitcast.81, f32[16,128]{1,0:T(8,128)} %bitcast.82, ...), custom_call_target="tpu_custom_call" | custom-call | tf_op jit(solution)/shard_map/pallas_call | solution.py:241
  2.4 1.4 %broadcast_in_dim.2 = bf16[32,16,128]{2,1,0:T(8,128)(2,1)} broadcast(bf16[16,128]{1,0:T(8,128)(2,1)} %get-tuple-element.12), dimensions={1,2} | broadcast | bytes 135168 | tf_op jit(solution)/shard_map/broadcast_in_dim | solution.py:251
  3.7 7.3 %all-to-all-start = ((bf16[32,16,128]{2,1,0:T(8,128)(2,1)}), bf16[32,16,128]{2,1,0:T(8,128)(2,1)S(1)}, u32[]{:S(2)}, u32[]{:S(2)}) async-start(bf16[32,16,128]{2,1,0:T(8,128)(2,1)} %broadcast_in_dim.2), calls=%async_computation | async-start | bytes 262144 | tf_op jit(solution)/shard_map/all_to_all | solution.py:250
  11.0 1.4 %slice_subtract_fusion = (s32[1,1024]{1,0:T(1,128)}, s32[1,1024]{1,0:T(1,128)S(1)}) fusion(s32[2,1024]{1,0:T(2,128)} %param.24, s32[]{:T(128)S(6)} %mul.30), kind=kLoop, calls=%fused_computation.21 | loop fusion | flops 1024 | bytes 16388 | tf_op jit(solution)/shard_map/sub | solution.py:259
  12.4 0.6 fusion.10.source_ref
  13.0 0.1 constant_dynamic-slice_fusion.1
  13.1 1.7 %shard_map.141 = (s32[256,128]{1,0:T(8,128)}, f32[256,128]{1,0:T(8,128)}) custom-call(s32[8,128]{1,0:T(8,128)} %fusion.10.source_ref, s32[8,128]{1,0:T(8,128)} %bitcast.75, s32[8,128]{1,0:T(8,128)} %bitcast.83), custom_call_target="tpu_custom_call" | custom-call | tf_op jit(solution)/shard_map/pallas_call | solution.py:262
  14.8 4.4 %all-to-all-done = bf16[32,16,128]{2,1,0:T(8,128)(2,1)S(1)} async-done(((bf16[32,16,128]{2,1,0:T(8,128)(2,1)}), bf16[32,16,128]{2,1,0:T(8,128)(2,1)S(1)}, u32[]{:S(2)}, u32[]{:S(2)}) %all-to-all-start) | async-done | bytes 131104 | tf_op jit(solution)/shard_map/all_to_all | solution.py:250
  19.3 3.4 %copy-done.1 = bf16[1024,32,128]{2,1,0:T(8,128)(2,1)S(1)} copy-done((bf16[1024,32,128]{2,1,0:T(8,128)(2,1)S(1)}, bf16[1024,32,128]{2,1,0:T(8,128)(2,1)}, u32[]{:S(2)}) %copy-start.1) | copy-done | bytes 8388632
  22.7 1.9 %copy-done.3 = bf16[96,128,128]{2,1,0:T(8,128)(2,1)S(1)} copy-done((bf16[96,128,128]{2,1,0:T(8,128)(2,1)S(1)}, bf16[96,128,128]{2,1,0:T(8,128)(2,1)}, u32[]{:S(2)}) %copy-start.3) | copy-done | bytes 3145752
  24.5 0.9 %copy-done.5 = s32[256,128]{1,0:T(8,128)S(1)} copy-done((s32[256,128]{1,0:T(8,128)S(1)}, s32[256,128]{1,0:T(8,128)}, u32[]{:S(2)}) %copy-start.5) | copy-done | bytes 131096
  25.4 0.9 %copy-done.7 = f32[256,128]{1,0:T(8,128)S(1)} copy-done((f32[256,128]{1,0:T(8,128)S(1)}, f32[256,128]{1,0:T(8,128)}, u32[]{:S(2)}) %copy-start.7) | copy-done | bytes 131096
  26.4 10.7 %shard_map.142 = bf16[32,16,128]{2,1,0:T(8,128)(2,1)} custom-call(s32[96]{0:T(128)S(1)} %get-tuple-element.22.near_source, s32[96]{0:T(128)S(1)} %get-tuple-element.21.near_target, s32[1]{0:T(128)} %bitcast.9.own_row, s32[256,128]{1,0:T(8,128)S(1)} %copy-done.5, f32[256,128]{1,0:T(8,128)S(1)} %copy-done.7, bf16[64,128]{1,0:T(8,128)(2,1)S(1)} %bitcast.66, ...), custom_call_target="tpu_custom_call" | custom-call | tf_op jit(solution)/shard_map/pallas_call | solution.py:280
  37.0 2.6 %all-to-all-start.1 = ((bf16[32,16,128]{2,1,0:T(8,128)(2,1)}), bf16[32,16,128]{2,1,0:T(8,128)(2,1)S(1)}, u32[]{:S(2)}, u32[]{:S(2)}) async-start(bf16[32,16,128]{2,1,0:T(8,128)(2,1)} %shard_map.142), calls=%async_computation.1 | async-start | bytes 262144 | tf_op jit(solution)/shard_map/all_to_all | solution.py:292
  39.6 14.3 %all_gather.6 = f32[3,64,128]{2,1,0:T(8,128)S(1)} all-gather(f32[3,16,128]{2,1,0:T(8,128)S(1)} %copy-done.11), channel_id=1, replica_groups=mesh['recv'=4,'src'=8] {'recv'}, dimensions={1}, use_global_device_ids=true | all-gather | bytes 122880 | tf_op jit(solution)/shard_map/all_gather | solution.py:254
  54.0 0.6 dynamic-slice_bitcast_fusion.first_ref
  54.6 3.4 %copy-done.2 = bf16[1024,32,128]{2,1,0:T(8,128)(2,1)S(1)} copy-done((bf16[1024,32,128]{2,1,0:T(8,128)(2,1)S(1)}, bf16[1024,32,128]{2,1,0:T(8,128)(2,1)}, u32[]{:S(2)}) %copy-start.2) | copy-done | bytes 8388632
  58.0 8.5 %shard_map.143 = bf16[128,128]{1,0:T(8,128)(2,1)} custom-call(s32[256,128]{1,0:T(8,128)S(1)} %copy-done.6, f32[256,128]{1,0:T(8,128)S(1)} %copy-done.8, bf16[64,128]{1,0:T(8,128)(2,1)S(1)} %fusion.7.deficit_ref, bf16[32768,128]{1,0:T(8,128)(2,1)S(1)} %bitcast.62, bf16[32768,128]{1,0:T(8,128)(2,1)} %bitcast.68), custom_call_target="tpu_custom_call" | custom-call | tf_op jit(solution)/shard_map/pallas_call | solution.py:306
  66.5 3.7 %all-to-all-start.2 = ((bf16[8,16,128]{2,1,0:T(8,128)(2,1)}), bf16[8,16,128]{2,1,0:T(8,128)(2,1)S(1)}, u32[]{:S(2)}, u32[]{:S(2)}) async-start(bf16[8,16,128]{2,1,0:T(8,128)(2,1)} %bitcast.24), calls=%async_computation.2 | async-start | bytes 65536 | tf_op jit(solution)/shard_map/all_to_all | solution.py:314
  70.2 9.7 %all_gather.7 = bf16[8,4,16,128]{3,2,1,0:T(8,128)(2,1)S(1)} all-gather(bf16[1,4,16,128]{3,2,1,0:T(8,128)(2,1)S(1)} %fusion.3), channel_id=1, replica_groups=mesh['recv'=4,'src'=8] {'src'}, dimensions={0}, use_global_device_ids=true | all-gather | bytes 147456 | tf_op jit(solution)/shard_map/all_gather | solution.py:304
  80.0 2.2 %shard_map.144.near_ref = f32[16,128]{1,0:T(8,128)S(1)} custom-call(s32[96]{0:T(128)S(1)} %get-tuple-element.22.near_source, s32[96]{0:T(128)S(1)} %get-tuple-element.21.near_target, bf16[512,128]{1,0:T(8,128)(2,1)S(1)} %bitcast.65, bf16[96,128,128]{2,1,0:T(8,128)(2,1)S(1)} %copy-done.4), custom_call_target="tpu_custom_call" | custom-call | tf_op jit(solution)/shard_map/pallas_call | solution.py:315
  82.2 0.6 copy-done.9
  82.9 0.6 copy-done.10
  83.5 2.0 %shard_map.145 = (f32[16,128]{1,0:T(8,128)}, f32[16,128]{1,0:T(8,128)}) custom-call(f32[8,16,128]{2,1,0:T(8,128)} %get-tuple-element.9.own_ref, f32[16,128]{1,0:T(8,128)} %dynamic-slice_bitcast_fusion.first_ref, bf16[8,16,128]{2,1,0:T(8,128)(2,1)} %copy-done.10, f32[16,128]{1,0:T(8,128)} %copy-done.9, s32[16,128]{1,0:T(8,128)} %bitcast.74), custom_call_target="tpu_custom_call" | custom-call | tf_op jit(solution)/shard_map/pallas_call | solution.py:323
  (26 shorter events, 0.1 us)
Async XLA Ops:
  0.6 12.4 %copy-start = (s32[2,768]{1,0:T(2,128)S(1)}, s32[2,768]{1,0:T(2,128)}, u32[]{:S(2)}) copy-start(s32[2,768]{1,0:T(2,128)} %param.21) | copy-start | bytes 18436
  3.7 15.5 %all-to-all-start = ((bf16[32,16,128]{2,1,0:T(8,128)(2,1)}), bf16[32,16,128]{2,1,0:T(8,128)(2,1)S(1)}, u32[]{:S(2)}, u32[]{:S(2)}) async-start(bf16[32,16,128]{2,1,0:T(8,128)(2,1)} %broadcast_in_dim.2), calls=%async_computation | async-start | bytes 262144 | tf_op jit(solution)/shard_map/all_to_all | solution.py:250
  19.3 3.4 %copy-start.1 = (bf16[1024,32,128]{2,1,0:T(8,128)(2,1)S(1)}, bf16[1024,32,128]{2,1,0:T(8,128)(2,1)}, u32[]{:S(2)}) copy-start(bf16[1024,32,128]{2,1,0:T(8,128)(2,1)} %param.23) | copy-start | bytes 25165828
  22.6 1.9 %copy-start.3 = (bf16[96,128,128]{2,1,0:T(8,128)(2,1)S(1)}, bf16[96,128,128]{2,1,0:T(8,128)(2,1)}, u32[]{:S(2)}) copy-start(bf16[96,128,128]{2,1,0:T(8,128)(2,1)} %tile_buf.1) | copy-start | bytes 9437188
  24.5 0.9 %copy-start.5 = (s32[256,128]{1,0:T(8,128)S(1)}, s32[256,128]{1,0:T(8,128)}, u32[]{:S(2)}) copy-start(s32[256,128]{1,0:T(8,128)} %get-tuple-element.10.source_ref) | copy-start | bytes 393220
  25.4 0.9 %copy-start.7 = (f32[256,128]{1,0:T(8,128)S(1)}, f32[256,128]{1,0:T(8,128)}, u32[]{:S(2)}) copy-start(f32[256,128]{1,0:T(8,128)} %get-tuple-element.11.target_ref) | copy-start | bytes 393220
  26.3 13.3 %copy-start.11 = (f32[3,16,128]{2,1,0:T(8,128)S(1)}, f32[3,16,128]{2,1,0:T(8,128)}, u32[]{:S(2)}) copy-start(f32[3,16,128]{2,1,0:T(8,128)} %get-tuple-element.13) | copy-start | bytes 73732
  26.4 28.2 %copy-start.6 = (s32[256,128]{1,0:T(8,128)S(1)}, s32[256,128]{1,0:T(8,128)}, u32[]{:S(2)}) copy-start(s32[256,128]{1,0:T(8,128)} %get-tuple-element.10.source_ref) | copy-start | bytes 393220
  26.4 28.2 %copy-start.8 = (f32[256,128]{1,0:T(8,128)S(1)}, f32[256,128]{1,0:T(8,128)}, u32[]{:S(2)}) copy-start(f32[256,128]{1,0:T(8,128)} %get-tuple-element.11.target_ref) | copy-start | bytes 393220
  37.0 16.9 %all-to-all-start.1 = ((bf16[32,16,128]{2,1,0:T(8,128)(2,1)}), bf16[32,16,128]{2,1,0:T(8,128)(2,1)S(1)}, u32[]{:S(2)}, u32[]{:S(2)}) async-start(bf16[32,16,128]{2,1,0:T(8,128)(2,1)} %shard_map.142), calls=%async_computation.1 | async-start | bytes 262144 | tf_op jit(solution)/shard_map/all_to_all | solution.py:292
  54.6 3.4 %copy-start.2 = (bf16[1024,32,128]{2,1,0:T(8,128)(2,1)S(1)}, bf16[1024,32,128]{2,1,0:T(8,128)(2,1)}, u32[]{:S(2)}) copy-start(bf16[1024,32,128]{2,1,0:T(8,128)(2,1)} %param.23) | copy-start | bytes 25165828
  58.0 22.0 %copy-start.4 = (bf16[96,128,128]{2,1,0:T(8,128)(2,1)S(1)}, bf16[96,128,128]{2,1,0:T(8,128)(2,1)}, u32[]{:S(2)}) copy-start(bf16[96,128,128]{2,1,0:T(8,128)(2,1)} %tile_buf.1) | copy-start | bytes 9437188
  66.5 16.4 %all-to-all-start.2 = ((bf16[8,16,128]{2,1,0:T(8,128)(2,1)}), bf16[8,16,128]{2,1,0:T(8,128)(2,1)S(1)}, u32[]{:S(2)}, u32[]{:S(2)}) async-start(bf16[8,16,128]{2,1,0:T(8,128)(2,1)} %bitcast.24), calls=%async_computation.2 | async-start | bytes 65536 | tf_op jit(solution)/shard_map/all_to_all | solution.py:314
  82.2 0.6 copy-start.9
  82.9 0.6 copy-start.10

commit v2 on v1

--- a/solution.py
+++ b/solution.py
@@ -13,14 +13,15 @@
 bf16 = jnp.bfloat16
 lanes = 128
 chunks = 8
-vmem_bytes = 40 * 2**20
+vmem_bytes = 8 * 2**20
+far_vmem_bytes = 58 * 2**20
 by_row = (((1,), (1,)), ((), ()))
 in_vmem = pl.BlockSpec(memory_space=pltpu.VMEM)
+in_hbm = pl.BlockSpec(memory_space=pl.ANY)
 in_smem = pl.BlockSpec(memory_space=pltpu.SMEM)
-anywhere = pl.BlockSpec(memory_space=pl.ANY)
-
-
-def order_kernel(p_ref, q_ref, a_ref, b_ref, slip_ref, plate_ref, order_ref, own_ref, shared_ref, deficit_ref):
+
+
+def order_kernel(p_ref, q_ref, a_ref, b_ref, slip_ref, plate_ref, order_ref, own_ref, shared_ref):
     order = order_ref[...]
     row, lane = order // lanes, order % lanes
     rows = order.shape[0]
@@ -41,7 +42,7 @@
     shared_ref[0] = p - time_step * b * theta_rate * gain
     shared_ref[1] = time_step * gain
     shared_ref[2] = plate
-    deficit_ref[...] = (plate - speed).astype(bf16)
+    shared_ref[3] = (plate - speed).astype(bf16).astype(f32)
 
 
 def table_kernel(source_ref, target_ref, rank_ref, source_out, target_out, *, rank):
@@ -114,7 +115,7 @@
     return total
 
 
-def far_copies(v_hbm, u_hbm, v_buf, u_buf, sems):
+def far_stream(source_ref, target_ref, deficit_ref, v_hbm, u_hbm, out_ref, v_buf, u_buf, sems):
     part = v_hbm.shape[0] // chunks
 
     def copies(i):
@@ -124,55 +125,72 @@
             pltpu.make_async_copy(u_hbm.at[where], u_buf.at[where], sems.at[1, i]),
         )
 
-    return copies
-
-
-def both_kernel(
-    near_source, near_target, own_row, source_ref, target_ref, deficit_ref, columns_ref, v_hbm, u_hbm, tiles_hbm,
-    out_ref, v_buf, u_buf, tile_buf, columns_buf, total_ref, sems, tile_sem,
-):
-    copies = far_copies(v_hbm, u_hbm, v_buf, u_buf, sems)
     for i in range(chunks):
         for copy in copies(i):
             copy.start()
-    tile_copy = pltpu.make_async_copy(tiles_hbm, tile_buf, tile_sem)
-    tile_copy.start()
 
     def before(i):
         for copy in copies(i):
             copy.wait()
 
-    far_part(source_ref, target_ref, deficit_ref, v_buf, u_buf, total_ref, before)
-    tile_copy.wait()
+    far_part(source_ref, target_ref, deficit_ref, v_buf, u_buf, out_ref, before)
+
+
+def far_kernel(source_ref, target_ref, deficit_ref, v_hbm, u_hbm, out_ref, v_buf, u_buf, sems):
+    far_stream(source_ref, target_ref, deficit_ref, v_hbm, u_hbm, out_ref, v_buf, u_buf, sems)
+
+
+def far_send_kernel(
+    source_ref, target_ref, deficit_ref, v_hbm, u_hbm, out_ref, v_buf, u_buf, sems, total_ref
+):
+    far_stream(source_ref, target_ref, deficit_ref, v_hbm, u_hbm, total_ref, v_buf, u_buf, sems)
+    out_ref[...] = total_ref[...].astype(bf16)
+
+
+def near_kernel(near_source, near_target, columns_ref, tile_ref, out_ref, columns_buf):
+    out_ref[...] = near_part(
+        near_source, near_target, columns_ref, tile_ref, columns_buf, out_ref.shape[0]
+    )
+
+
+def near_send_kernel(
+    near_source, near_target, own_row, far_ref, columns_ref, tile_ref, out_ref, columns_buf, total_ref
+):
     count = out_ref.shape[1]
-    near = near_part(near_source, near_target, columns_ref, tile_buf, columns_buf, count)
+    near = near_part(near_source, near_target, columns_ref, tile_ref, columns_buf, count)
+    total_ref[...] = far_ref[...]
     own = pl.ds(pl.multiple_of(own_row[0] * count, count), count)
     total_ref[own, :] += near
-    out_ref[...] = jnp.broadcast_to(
-        total_ref[...].astype(bf16).reshape(1, -1, count, lanes), (out_ref.shape[0] // (total_ref.shape[0] // count), total_ref.shape[0] // count, count, lanes)
-    ).reshape(out_ref.shape)
-
-
-def far_kernel(
-    source_ref, target_ref, deficit_ref, v_hbm, u_hbm, out_ref, v_buf, u_buf, total_ref, sems
-):
-    copies = far_copies(v_hbm, u_hbm, v_buf, u_buf, sems)
-    for i in range(chunks):
-        for copy in copies(i):
-            copy.start()
-
-    def before(i):
-        for copy in copies(i):
-            copy.wait()
-
-    far_part(source_ref, target_ref, deficit_ref, v_buf, u_buf, total_ref, before)
-    out_ref[...] = total_ref[...].astype(bf16)
-
-
-def near_kernel(near_source, near_target, columns_ref, tile_buf, out_ref, columns_buf):
-    out_ref[...] = near_part(
-        near_source, near_target, columns_ref, tile_buf, columns_buf, out_ref.shape[0]
-    )
+    total = total_ref[...].astype(bf16).reshape(-1, count, lanes)
+    groups = total.shape[0]
+    for k in range(out_ref.shape[0] // groups):
+        out_ref[k * groups : (k + 1) * groups] = total
+
+
+def join_kernel(*refs):
+    parts, (columns_ref, send_ref) = refs[:-2], refs[-2:]
+    columns = jnp.concatenate([part[3] for part in parts], 0).astype(bf16)
+    columns_ref[...] = columns
+    for k in range(send_ref.shape[0]):
+        send_ref[k] = columns
+
+
+def update_kernel(recv_ref, stress_ref, *refs):
+    parts, (columns_ref, send_ref, own_ref) = refs[:-3], refs[-3:]
+    group = stress_ref.shape[0] // len(parts)
+    columns = []
+    for k, part in enumerate(parts):
+        first = (recv_ref[0] ^ k) * group
+        stress = stress_ref[first].astype(f32)
+        for b in range(1, group):
+            stress += stress_ref[first + b].astype(f32)
+        if k == 0:
+            own_ref[...] = stress
+        columns.append(part[2] - jnp.exp(part[0] + part[1] * stress))
+    columns = jnp.concatenate(columns, 0).astype(bf16)
+    columns_ref[...] = columns
+    for k in range(send_ref.shape[0]):
+        send_ref[k] = columns
 
 
 def final_kernel(own_ref, first_ref, second_ref, near_ref, order_ref, p_out, q_out):
@@ -238,92 +256,106 @@
     whole = (own_clusters, lanes)
 
     order = cluster_order.reshape(whole)
-    own, shared, deficit = pl.pallas_call(
+    own, shared = pl.pallas_call(
         order_kernel,
         out_shape=(
             jax.ShapeDtypeStruct((8,) + whole, f32),
-            jax.ShapeDtypeStruct((3,) + whole, f32),
-            jax.ShapeDtypeStruct(whole, bf16),
+            jax.ShapeDtypeStruct((4,) + whole, f32),
         ),
+        compiler_params=params,
     )(*[x.reshape(whole) for x in (log_rate, log_state, a_sigma, b_sigma, crit_slip, plate_rate)], order)
 
-    columns = lax.all_to_all(
-        jnp.broadcast_to(deficit[None], (device_count,) + whole),
-        ("recv", "src"), split_axis=0, concat_axis=0, tiled=True,
-    )
-    shared_columns = lax.all_gather(shared, "recv", axis=1, tiled=True)
+    parts = [shared] + [
+        lax.ppermute(shared, "recv", [(i, i ^ k) for i in range(recv_count)])
+        for k in range(1, recv_count)
+    ]
+    columns_shape = jax.ShapeDtypeStruct((source_rows, lanes), bf16)
+    send_shape = jax.ShapeDtypeStruct((src_count, source_rows, lanes), bf16)
+    first_columns, first_send = pl.pallas_call(
+        join_kernel, out_shape=(columns_shape, send_shape), compiler_params=params
+    )(*parts)
+    all_first = lax.all_to_all(first_send, "src", split_axis=0, concat_axis=0, tiled=True)
 
     near_own = lax.dynamic_slice_in_dim(near_pairs, src_index * tile_count, tile_count, 1)
     near_target = near_own[0] - (recv_index * group_rows + src_index * own_clusters)
-    near_source = near_own[1]
+
+    def group_place(cluster):
+        return ((cluster // group_rows) ^ recv_index) * own_clusters + cluster % own_clusters
+
+    near_source = near_own[1] // own_clusters % src_count * source_rows + group_place(near_own[1])
     far_target = far_pairs[0] - recv_index * group_rows
-    far_source = far_pairs[1] // group_rows * own_clusters + far_pairs[1] % own_clusters
+    far_source = group_place(far_pairs[1])
     table = (factor_rows // lanes, lanes)
     source_table, target_table = pl.pallas_call(
         functools.partial(table_kernel, rank=rank),
         out_shape=(jax.ShapeDtypeStruct(table, jnp.int32), jax.ShapeDtypeStruct(table, f32)),
+        compiler_params=params,
     )(*[x.reshape(far_count // lanes, lanes) for x in (far_source, far_target, far_ranks)])
 
     v_rows = far_v.reshape(factor_rows, lanes)
     u_rows = far_u.reshape(factor_rows, lanes)
+    far_specs = dict(
+        in_specs=[in_vmem] * 3 + [in_hbm] * 2,
+        out_specs=in_vmem,
+        compiler_params=pltpu.CompilerParams(vmem_limit_bytes=far_vmem_bytes),
+        cost_estimate=pl.CostEstimate(
+            flops=2 * factor_rows * lanes * (source_rows + group_rows), bytes_accessed=2**24, transcendentals=0
+        ),
+    )
     far_scratch = [
         pltpu.VMEM(v_rows.shape, bf16),
         pltpu.VMEM(u_rows.shape, bf16),
+        pltpu.SemaphoreType.DMA((2, chunks)),
     ]
+    columns_scratch = pltpu.VMEM((own_clusters * device_count, lanes), f32)
     total_scratch = pltpu.VMEM((group_rows, lanes), f32)
-    columns_scratch = pltpu.VMEM((own_clusters * device_count, lanes), f32)
-    far_sems = pltpu.SemaphoreType.DMA((2, chunks))
-
-    group_columns = lax.dynamic_index_in_dim(
-        columns.reshape((recv_count, src_count) + whole), src_index, 1, keepdims=False
-    ).reshape(source_rows, lanes)
+
+    first_far = pl.pallas_call(
+        far_kernel,
+        out_shape=jax.ShapeDtypeStruct((group_rows, lanes), f32),
+        scratch_shapes=far_scratch,
+        **far_specs,
+    )(source_table, target_table, first_columns, v_rows, u_rows)
     partial = pl.pallas_call(
-        both_kernel,
-        in_specs=[in_smem] * 3 + [in_vmem] * 4 + [anywhere] * 3,
+        near_send_kernel,
+        in_specs=[in_smem] * 3 + [in_vmem] * 3,
         out_specs=in_vmem,
         out_shape=jax.ShapeDtypeStruct((device_count,) + whole, bf16),
-        scratch_shapes=far_scratch
-        + [pltpu.VMEM(near_tiles.shape, bf16), columns_scratch, total_scratch, far_sems, pltpu.SemaphoreType.DMA],
-        compiler_params=params,
-    )(
-        near_source, near_target, src_index.reshape(1), source_table, target_table,
-        group_columns, columns.reshape(-1, lanes), v_rows, u_rows, near_tiles,
+        scratch_shapes=[columns_scratch, total_scratch],
+        compiler_params=params,
+    )(near_source, near_target, src_index.reshape(1), first_far, all_first.reshape(-1, lanes), near_tiles)
+    stress_parts = lax.all_to_all(partial, ("recv", "src"), split_axis=0, concat_axis=0, tiled=True)
+
+    second_columns, second_send, first_stress = pl.pallas_call(
+        update_kernel,
+        in_specs=[in_smem] + [in_vmem] * (1 + recv_count),
+        out_specs=(in_vmem, in_vmem, in_vmem),
+        out_shape=(columns_shape, send_shape, jax.ShapeDtypeStruct(whole, f32)),
+        compiler_params=params,
+    )(recv_index.reshape(1), stress_parts, *parts)
+    all_second = lax.all_to_all(second_send, "src", split_axis=0, concat_axis=0, tiled=True)
+    second_far = pl.pallas_call(
+        far_send_kernel,
+        out_shape=jax.ShapeDtypeStruct((group_rows, lanes), bf16),
+        scratch_shapes=far_scratch + [total_scratch],
+        **far_specs,
+    )(source_table, target_table, second_columns, v_rows, u_rows)
+    second_parts = lax.all_to_all(
+        second_far.reshape((src_count,) + whole), "src", split_axis=0, concat_axis=0, tiled=True
     )
-    stress_parts = lax.all_to_all(
-        partial, ("recv", "src"), split_axis=0, concat_axis=0, tiled=True
-    )
-    first_stress = jnp.sum(
-        stress_parts.reshape((recv_count, src_count) + whole).astype(f32), axis=1
-    )
-    second_deficit = (
-        shared_columns[2]
-        - jnp.exp(shared_columns[0] + shared_columns[1] * first_stress.reshape(-1, lanes))
-    ).astype(bf16)
-    own_stress = lax.dynamic_index_in_dim(first_stress, recv_index, 0, keepdims=False)
-
-    by_group = lax.all_gather(second_deficit.reshape((1, recv_count) + whole), "src", axis=0, tiled=True)
-    second_columns = by_group.transpose(1, 0, 2, 3).reshape(-1, lanes)
-    far_second = pl.pallas_call(
-        far_kernel,
-        in_specs=[in_vmem] * 3 + [anywhere] * 2,
-        out_specs=in_vmem,
-        out_shape=jax.ShapeDtypeStruct((group_rows, lanes), bf16),
-        scratch_shapes=far_scratch + [total_scratch, far_sems],
-        compiler_params=params,
-    )(source_table, target_table, second_deficit, v_rows, u_rows)
-    second_parts = lax.all_to_all(far_second, "src", split_axis=0, concat_axis=0, tiled=True)
-    near_second = pl.pallas_call(
+    second_near = pl.pallas_call(
         near_kernel,
         in_specs=[in_smem] * 2 + [in_vmem] * 2,
         out_specs=in_vmem,
         out_shape=jax.ShapeDtypeStruct(whole, f32),
         scratch_shapes=[columns_scratch],
         compiler_params=params,
-    )(near_source, near_target, second_columns, near_tiles)
+    )(near_source, near_target, all_second.reshape(-1, lanes), near_tiles)
     new_p, new_q = pl.pallas_call(
         final_kernel,
         out_shape=(jax.ShapeDtypeStruct(whole, f32), jax.ShapeDtypeStruct(whole, f32)),
-    )(own, own_stress, second_parts.reshape((src_count,) + whole), near_second, order)
+        compiler_params=params,
+    )(own, first_stress, second_parts, second_near, order)
     return new_p.reshape(-1), new_q.reshape(-1)
 
 

time: 86.1 us -> 72.6 us (0.84)
  blocking collectives: 24 us -> 13.6 us
  local copies, waits for them, and re-layouts: 13.8 us -> 8.98 us
  starting transfers between devices: 13.6 us -> 17 us
  other arithmetic: 2.04 us -> 0.82 us
  waiting for transfers between devices: 4.43 us -> 3.53 us
    all_gather x2 -> x0, blocking collectives: 24 us -> none  [the longest x1 14.3 us: on_device(): shared_columns = lax.all_gather(shared, 'recv', axis=1, tiled=True)]
    all_to_all x0 -> x1, blocking collectives: none -> 13.6 us  [on_device(): lax.all_to_all(partial, ('recv', 'src'), split_axis=0, concat_axis=0, til...]
    ppermute x0 -> x3, starting transfers between devices: none -> 5.76 us  [on_device(): lax.ppermute(shared, 'recv', [(i, i ^ k) for i in range(recv_count)])]
    pallas_call x2 -> x5, Pallas kernels: 19.2 us -> 22.9 us  [the longest x1 9.71 us: on_device(): pl.pallas_call(far_kernel, out_shape=jax.ShapeDtypeStruct((group_rows, la...]
    unnamed x24 -> x32, local copies, waits for them, and re-layouts: 11.7 us -> 8.9 us
    all_to_all x3, starting transfers between devices: 13.6 us -> 11.2 us  [the longest x1 4.14 us: on_device(): lax.all_to_all(second_far.reshape((src_count,) + whole), 'src', split_axi...]
    all_to_all x3, waiting for transfers between devices: 4.43 us -> 2.6 us  [the longest x1 2.59 us: on_device(): lax.all_to_all(second_far.reshape((src_count,) + whole), 'src', split_axi...]
    pallas_call x1, Pallas kernels: 1.73 us -> 0.28 us  [on_device(): pl.pallas_call(order_kernel, out_shape=(jax.ShapeDtypeStruct((8,) + whole...]
  transfers between devices with their start and end apart: 3 -> 6, of which waited for: 1 -> 2; matrix products, arithmetic and copies ran while one was open for 2% -> 1% of each run, Pallas kernels for 5% -> 31%
where the time goes in v2:
time: 72.6 us; the launch traced here: 71.6 us
  Pallas kernels  26.9 us (37%)
  starting transfers between devices  17 us (23%)
  blocking collectives  13.6 us (19%)
  local copies, waits for them, and re-layouts  8.98 us (12%)
  waiting for transfers between devices  3.53 us (5%)
  other arithmetic  0.82 us (1%)
  between operations  0.78 us (1%)
    all_to_all x1, blocking collectives, on_device(): lax.all_to_all(partial, ('recv', 'src'), split_axis=0, concat_axis=0, til...  13.6 us
    pallas_call x1, Pallas kernels, on_device(): pl.pallas_call(far_kernel, out_shape=jax.ShapeDtypeStruct((group_rows, la...  9.71 us
    pallas_call x1, Pallas kernels, on_device(): pl.pallas_call(far_send_kernel, out_shape=jax.ShapeDtypeStruct((group_row...  9.56 us
    unnamed x32, local copies, waits for them, and re-layouts  8.9 us
    ppermute x3, starting transfers between devices, on_device(): lax.ppermute(shared, 'recv', [(i, i ^ k) for i in range(recv_count)])  5.76 us
    all_to_all x1, starting transfers between devices, on_device(): lax.all_to_all(second_far.reshape((src_count,) + whole), 'src', split_axi...  4.14 us
    all_to_all x1, starting transfers between devices, on_device(): lax.all_to_all(first_send, 'src', split_axis=0, concat_axis=0, tiled=True)  3.72 us
    all_to_all x1, starting transfers between devices, on_device(): lax.all_to_all(second_send, 'src', split_axis=0, concat_axis=0, tiled=True)  3.37 us
  transfers between devices with their start and end apart: 6, of which 2 were waited for; matrix products, arithmetic and copies ran while one was open for 1% of the time, Pallas kernels for 31%

profile of v2, /device:TPU:0, one launch (start us, length us, event | category | flops | bytes accessed | tf_op | source)
XLA Modules:
  0.0 71.6 jit_solution(8063406885099043990)
XLA Ops:
  0.7 0.7 copy-done.5
  1.4 0.7 copy-done.9
  2.1 0.7 copy-done.10
  2.7 0.7 copy-done.11
  3.4 0.7 copy-done.12
  4.1 0.7 copy-done.13
  4.8 0.7 copy-done.14
  5.8 5.1 %collective-permute-start.2 = (f32[4,16,128]{2,1,0:T(8,128)S(1)}, f32[4,16,128]{2,1,0:T(8,128)S(1)}, u32[]{:S(2)}, u32[]{:S(2)}) collective-permute-start(f32[4,16,128]{2,1,0:T(8,128)S(1)} %get-tuple-element.16.refs_0_), channel_id=1, source_target_pairs={{0,24},{8,16},{16,8},{24,0},{1,25},{9,17},{17,9},{25,1},{2,26},{10... | collective-permute-start | bytes 98312 | tf_op jit(solution)/shard_map/ppermute | solution.py:269
  11.7 0.8 %slice_subtract_fusion = (s32[1,1024]{1,0:T(1,128)S(1)}, s32[1,1024]{1,0:T(1,128)S(1)}) fusion(s32[2,1024]{1,0:T(2,128)} %param.24, s32[]{:T(128)S(6)} %mul.31), kind=kLoop, calls=%fused_computation.10 | loop fusion | flops 1024 | bytes 16388 | tf_op jit(solution)/shard_map/sub | solution.py:286
  12.5 0.7 copy-done.15
  14.8 0.9 %collective-permute-done.1.refs_2_ = f32[4,16,128]{2,1,0:T(8,128)S(1)} collective-permute-done((f32[4,16,128]{2,1,0:T(8,128)S(1)}, f32[4,16,128]{2,1,0:T(8,128)S(1)}, u32[]{:S(2)}, u32[]{:S(2)}) %collective-permute-start.1) | collective-permute-done | bytes 32800 | tf_op jit(solution)/shard_map/ppermute | solution.py:269
  15.8 0.7 shard_map.142
  17.0 3.7 %all-to-all-start = ((bf16[8,64,128]{2,1,0:T(8,128)(2,1)}), bf16[8,64,128]{2,1,0:T(8,128)(2,1)S(1)}, u32[]{:S(2)}, u32[]{:S(2)}) async-start(bf16[8,64,128]{2,1,0:T(8,128)(2,1)} %get-tuple-element.18), calls=%async_computation | async-start | bytes 262144 | tf_op jit(solution)/shard_map/all_to_all | solution.py:277
  20.8 9.7 %shard_map.143.far_ref = f32[128,128]{1,0:T(8,128)} custom-call(s32[256,128]{1,0:T(8,128)} %copy-done.2, f32[256,128]{1,0:T(8,128)} %copy-done.3, bf16[64,128]{1,0:T(8,128)(2,1)} %copy-done.8, bf16[32768,128]{1,0:T(8,128)(2,1)} %bitcast.49, bf16[32768,128]{1,0:T(8,128)(2,1)} %bitcast.51), custom_call_target="tpu_custom_call" | custom-call | flops 1610612736 | bytes 16777216 | tf_op jit(solution)/shard_map/pallas_call | solution.py:313
  30.5 0.8 %copy-done.4 = f32[128,128]{1,0:T(8,128)S(1)} copy-done((f32[128,128]{1,0:T(8,128)S(1)}, f32[128,128]{1,0:T(8,128)}, u32[]{:S(2)}) %copy-start.4) | copy-done | bytes 65560
  31.3 2.3 %shard_map.144 = bf16[32,16,128]{2,1,0:T(8,128)(2,1)S(1)} custom-call(s32[96]{0:T(128)S(1)} %fusion.7.near_source, s32[96]{0:T(128)S(1)} %subtract_bitcast_fusion.near_target, s32[1]{0:T(128)} %bitcast.10.own_row, f32[128,128]{1,0:T(8,128)S(1)} %copy-done.4, bf16[512,128]{1,0:T(8,128)(2,1)S(1)} %bitcast.38, bf16[96,128,128]{2,1,0:T(8,128)(2,1)S(1)} %copy-done.1), custom_call_target="tpu_custom_call" | custom-call | tf_op jit(solution)/shard_map/pallas_call | solution.py:319
  33.6 13.6 %all_to_all.20.stress_ref = bf16[32,16,128]{2,1,0:T(8,128)(2,1)S(1)} all-to-all(bf16[32,16,128]{2,1,0:T(8,128)(2,1)S(1)} %shard_map.144), channel_id=1, replica_groups=mesh['recv'=4,'src'=8] {'recv','src'}, dimensions={0} | all-to-all | bytes 262144 | tf_op jit(solution)/shard_map/all_to_all | solution.py:327
  47.2 0.7 shard_map.145
  48.5 3.4 %all-to-all-start.3 = ((bf16[8,64,128]{2,1,0:T(8,128)(2,1)}), bf16[8,64,128]{2,1,0:T(8,128)(2,1)S(1)}, u32[]{:S(2)}, u32[]{:S(2)}) async-start(bf16[8,64,128]{2,1,0:T(8,128)(2,1)} %get-tuple-element.21), calls=%async_computation.3 | async-start | bytes 262144 | tf_op jit(solution)/shard_map/all_to_all | solution.py:336
  51.9 9.6 %shard_map.146 = bf16[128,128]{1,0:T(8,128)(2,1)} custom-call(s32[256,128]{1,0:T(8,128)} %copy-done.2, f32[256,128]{1,0:T(8,128)} %copy-done.3, bf16[64,128]{1,0:T(8,128)(2,1)} %copy-done.7, bf16[32768,128]{1,0:T(8,128)(2,1)} %bitcast.50, bf16[32768,128]{1,0:T(8,128)(2,1)} %bitcast.52), custom_call_target="tpu_custom_call" | custom-call | flops 1610612736 | bytes 16777216 | tf_op jit(solution)/shard_map/pallas_call | solution.py:337
  61.5 4.1 %all-to-all-start.2 = ((bf16[8,16,128]{2,1,0:T(8,128)(2,1)}), bf16[8,16,128]{2,1,0:T(8,128)(2,1)S(1)}, u32[]{:S(2)}, u32[]{:S(2)}) async-start(bf16[8,16,128]{2,1,0:T(8,128)(2,1)} %bitcast.53), calls=%async_computation.2 | async-start | bytes 65536 | tf_op jit(solution)/shard_map/all_to_all | solution.py:343
  65.6 2.2 %shard_map.147.near_ref = f32[16,128]{1,0:T(8,128)S(1)} custom-call(s32[96]{0:T(128)S(1)} %fusion.7.near_source, s32[96]{0:T(128)S(1)} %subtract_bitcast_fusion.near_target, bf16[512,128]{1,0:T(8,128)(2,1)S(1)} %bitcast.37, bf16[96,128,128]{2,1,0:T(8,128)(2,1)S(1)} %copy-done.1), custom_call_target="tpu_custom_call" | custom-call | tf_op jit(solution)/shard_map/pallas_call | solution.py:346
  67.9 2.6 %all-to-all-done.2.second_ref = bf16[8,16,128]{2,1,0:T(8,128)(2,1)S(1)} async-done(((bf16[8,16,128]{2,1,0:T(8,128)(2,1)}), bf16[8,16,128]{2,1,0:T(8,128)(2,1)S(1)}, u32[]{:S(2)}, u32[]{:S(2)}) %all-to-all-start.2) | async-done | bytes 32800 | tf_op jit(solution)/shard_map/all_to_all | solution.py:343
  70.5 1.1 %shard_map.148 = (f32[16,128]{1,0:T(8,128)}, f32[16,128]{1,0:T(8,128)}) custom-call(f32[8,16,128]{2,1,0:T(8,128)S(1)} %get-tuple-element.13.own_ref, f32[16,128]{1,0:T(8,128)S(1)} %get-tuple-element.19.first_ref, bf16[8,16,128]{2,1,0:T(8,128)(2,1)S(1)} %all-to-all-done.2.second_ref, f32[16,128]{1,0:T(8,128)S(1)} %shard_map.147.near_ref, s32[16,128]{1,0:T(8,128)S(1)} %bitcast.40), custom_call_target="tpu_custom_call" | custom-call | tf_op jit(solution)/shard_map/pallas_call | solution.py:354
  (35 shorter events, 3.9 us)
Async XLA Ops:
  0.6 11.0 %copy-start = (s32[2,768]{1,0:T(2,128)S(1)}, s32[2,768]{1,0:T(2,128)}, u32[]{:S(2)}) copy-start(s32[2,768]{1,0:T(2,128)} %param.21) | copy-start | bytes 18436
  0.6 0.7 copy-start.5
  1.4 0.7 copy-start.9
  2.0 0.7 copy-start.10
  2.7 0.7 copy-start.11
  3.4 0.7 copy-start.12
  4.1 0.7 copy-start.13
  4.8 0.7 copy-start.14
  5.8 9.0 %collective-permute-start.2 = (f32[4,16,128]{2,1,0:T(8,128)S(1)}, f32[4,16,128]{2,1,0:T(8,128)S(1)}, u32[]{:S(2)}, u32[]{:S(2)}) collective-permute-start(f32[4,16,128]{2,1,0:T(8,128)S(1)} %get-tuple-element.16.refs_0_), channel_id=1, source_target_pairs={{0,24},{8,16},{16,8},{24,0},{1,25},{9,17},{17,9},{25,1},{2,26},{10... | collective-permute-start | bytes 98312 | tf_op jit(solution)/shard_map/ppermute | solution.py:269
  10.9 4.8 %collective-permute-start.1 = (f32[4,16,128]{2,1,0:T(8,128)S(1)}, f32[4,16,128]{2,1,0:T(8,128)S(1)}, u32[]{:S(2)}, u32[]{:S(2)}) collective-permute-start(f32[4,16,128]{2,1,0:T(8,128)S(1)} %get-tuple-element.16.refs_0_), channel_id=1, source_target_pairs={{0,16},{8,24},{16,0},{24,8},{1,17},{9,25},{17,1},{25,9},{2,18},{10... | collective-permute-start | bytes 98312 | tf_op jit(solution)/shard_map/ppermute | solution.py:269
  10.9 4.8 %collective-permute-start = (f32[4,16,128]{2,1,0:T(8,128)S(1)}, f32[4,16,128]{2,1,0:T(8,128)S(1)}, u32[]{:S(2)}, u32[]{:S(2)}) collective-permute-start(f32[4,16,128]{2,1,0:T(8,128)S(1)} %get-tuple-element.16.refs_0_), channel_id=1, source_target_pairs={{0,8},{8,0},{16,24},{24,16},{1,9},{9,1},{17,25},{25,17},{2,10},{10... | collective-permute-start | bytes 98312 | tf_op jit(solution)/shard_map/ppermute | solution.py:269
  12.5 0.7 copy-start.15
  13.5 0.7 copy-start.2
  14.2 0.6 copy-start.3
  16.4 0.6 copy-start.8
  17.0 13.4 %all-to-all-start = ((bf16[8,64,128]{2,1,0:T(8,128)(2,1)}), bf16[8,64,128]{2,1,0:T(8,128)(2,1)S(1)}, u32[]{:S(2)}, u32[]{:S(2)}) async-start(bf16[8,64,128]{2,1,0:T(8,128)(2,1)} %get-tuple-element.18), calls=%async_computation | async-start | bytes 262144 | tf_op jit(solution)/shard_map/all_to_all | solution.py:277
  20.7 9.7 %copy-start.1 = (bf16[96,128,128]{2,1,0:T(8,128)(2,1)S(1)}, bf16[96,128,128]{2,1,0:T(8,128)(2,1)}, u32[]{:S(2)}) copy-start(bf16[96,128,128]{2,1,0:T(8,128)(2,1)} %tile_ref.3) | copy-start | bytes 9437188
  30.5 0.8 %copy-start.4 = (f32[128,128]{1,0:T(8,128)S(1)}, f32[128,128]{1,0:T(8,128)}, u32[]{:S(2)}) copy-start(f32[128,128]{1,0:T(8,128)} %shard_map.143.far_ref) | copy-start | bytes 196612
  47.9 0.6 copy-start.7
  48.5 13.0 %all-to-all-start.3 = ((bf16[8,64,128]{2,1,0:T(8,128)(2,1)}), bf16[8,64,128]{2,1,0:T(8,128)(2,1)S(1)}, u32[]{:S(2)}, u32[]{:S(2)}) async-start(bf16[8,64,128]{2,1,0:T(8,128)(2,1)} %get-tuple-element.21), calls=%async_computation.3 | async-start | bytes 262144 | tf_op jit(solution)/shard_map/all_to_all | solution.py:336
  51.9 18.6 %copy-start.6 = (s32[1,2048]{1,0:T(1,128)S(1)}, s32[1,2048]{1,0:T(1,128)}, u32[]{:S(2)}) copy-start(s32[1,2048]{1,0:T(1,128)} %param.19) | copy-start | bytes 24580
  61.5 9.0 %all-to-all-start.2 = ((bf16[8,16,128]{2,1,0:T(8,128)(2,1)}), bf16[8,16,128]{2,1,0:T(8,128)(2,1)S(1)}, u32[]{:S(2)}, u32[]{:S(2)}) async-start(bf16[8,16,128]{2,1,0:T(8,128)(2,1)} %bitcast.53), calls=%async_computation.2 | async-start | bytes 65536 | tf_op jit(solution)/shard_map/all_to_all | solution.py:343

commit v3 on v2

--- a/solution.py
+++ b/solution.py
@@ -13,24 +13,40 @@
 bf16 = jnp.bfloat16
 lanes = 128
 chunks = 8
+near_chunks = 4
 vmem_bytes = 8 * 2**20
-far_vmem_bytes = 58 * 2**20
+far_vmem_bytes = 28 * 2**20
+bodies = (1, 2, 2, 2, 1)
 by_row = (((1,), (1,)), ((), ()))
 in_vmem = pl.BlockSpec(memory_space=pltpu.VMEM)
-in_hbm = pl.BlockSpec(memory_space=pl.ANY)
+anywhere = pl.BlockSpec(memory_space=pl.ANY)
 in_smem = pl.BlockSpec(memory_space=pltpu.SMEM)
 
 
-def order_kernel(p_ref, q_ref, a_ref, b_ref, slip_ref, plate_ref, order_ref, own_ref, shared_ref):
-    order = order_ref[...]
+def in_hbm(x):
+    return pltpu.with_memory_space_constraint(x, pltpu.HBM)
+
+
+def order_kernel(*refs):
+    arguments, (own_ref, shared_ref, order_out, buf, order_buf, sems) = refs[:7], refs[7:]
+    count = len(arguments) - 1
+    copies = [
+        pltpu.make_async_copy(ref, order_buf if k == count else buf.at[k], sems.at[k])
+        for k, ref in enumerate(arguments)
+    ]
+    for copy in copies:
+        copy.start()
+    for copy in copies:
+        copy.wait()
+    order = order_buf[...]
+    order_out[...] = order
     row, lane = order // lanes, order % lanes
     rows = order.shape[0]
-    refs = (p_ref, q_ref, a_ref, b_ref, slip_ref, plate_ref)
-    sorted_values = [jnp.zeros(order.shape, f32)] * len(refs)
+    sorted_values = [jnp.zeros(order.shape, f32)] * count
     for r in range(rows):
         here = row == r
-        for k, ref in enumerate(refs):
-            spread = jnp.broadcast_to(ref[r : r + 1, :], order.shape)
+        for k in range(count):
+            spread = jnp.broadcast_to(buf[k, r : r + 1, :], order.shape)
             got = jnp.take_along_axis(spread, lane, axis=1)
             sorted_values[k] = jnp.where(here, got, sorted_values[k])
     p, q, a, b, slip, plate = sorted_values
@@ -45,19 +61,54 @@
     shared_ref[3] = (plate - speed).astype(bf16).astype(f32)
 
 
-def table_kernel(source_ref, target_ref, rank_ref, source_out, target_out, *, rank):
+def table_kernel(
+    near_pairs, far_pairs_hbm, rank_hbm, source_out, target_out, near_hot_out, near_target_out,
+    far_pairs, rank_ref, hot_buf, sems, *, rank, own_clusters, src_count,
+):
+    copies = (
+        pltpu.make_async_copy(far_pairs_hbm, far_pairs, sems.at[0]),
+        pltpu.make_async_copy(rank_hbm, rank_ref, sems.at[1]),
+    )
+    for copy in copies:
+        copy.start()
+    recv_index, src_index = lax.axis_index("recv"), lax.axis_index("src")
+    group_rows = own_clusters * src_count
+    source_rows = own_clusters * lax.axis_size("recv")
+
+    def group_place(cluster):
+        return ((cluster // group_rows) ^ recv_index) * own_clusters + cluster % own_clusters
+
+    tile_count, cluster_count = hot_buf.shape
+    cluster_ids = lax.broadcasted_iota(jnp.int32, (1, cluster_count), 1)
+    first_own = recv_index * group_rows + src_index * own_clusters
+    for t in range(tile_count):
+        source = near_pairs[1, src_index * tile_count + t]
+        place = (source // own_clusters) % src_count * source_rows + group_place(source)
+        hot_buf[t : t + 1, :] = jnp.where(cluster_ids == place, 1.0, 0.0)
+        near_target_out[t : t + 1, :] = jnp.full(
+            (1, lanes), near_pairs[0, src_index * tile_count + t] - first_own, jnp.int32
+        )
+    near_hot_out[...] = hot_buf[...].astype(bf16)
+
+    for copy in copies:
+        copy.wait()
     per_row = lanes // rank
     group = lanes // per_row
     shape = (group, lanes)
     lane = lax.broadcasted_iota(jnp.int32, shape, 1)
     pick = lax.broadcasted_iota(jnp.int32, shape, 0) * per_row + lane // rank
-    for a in range(source_ref.shape[0]):
-        def spread(ref):
-            return jnp.take_along_axis(jnp.broadcast_to(ref[a : a + 1, :], shape), pick, axis=1)
-
+
+    def spread(row):
+        return jnp.take_along_axis(jnp.broadcast_to(row, shape), pick, axis=1)
+
+    for a in range(rank_ref.shape[0]):
         where = slice(a * group, (a + 1) * group)
-        source_out[where, :] = jnp.where(lane % rank < spread(rank_ref), spread(source_ref), -1)
-        target_out[where, :] = spread(target_ref).astype(f32)
+        across = slice(a * lanes, (a + 1) * lanes)
+        source = group_place(far_pairs[1:2, across])
+        source_out[where, :] = jnp.where(
+            lane % rank < spread(rank_ref[a : a + 1, :]), spread(source), -1
+        )
+        target_out[where, :] = spread(far_pairs[0:1, across] - recv_index * group_rows).astype(f32)
 
 
 def far_part(source_ref, target_ref, deficit_ref, v_buf, u_buf, out_ref, before):
@@ -73,17 +124,19 @@
     ]
     out_ref[...] = jnp.zeros_like(out_ref)
 
-    def step(i, _):
-        before(i)
-        base = pl.multiple_of(i * part, part)
+    step = 0
+    for body in bodies:
+        for i in range(step, step + body):
+            before(i)
+        base, count = step * part, body * part
         products = lax.dot_general(
-            deficit, v_buf[pl.ds(base, part), :], by_row, preferred_element_type=f32
+            deficit, v_buf[base : base + count, :], by_row, preferred_element_type=f32
         )
         spread = []
-        for k in range(part // lanes):
-            row = i * (part // lanes) + k
-            source = source_ref[pl.ds(row, 1), :]
-            target = jnp.broadcast_to(target_ref[pl.ds(row, 1), :], (16, lanes)).astype(bf16)
+        for k in range(count // lanes):
+            row = base // lanes + k
+            source = source_ref[row : row + 1, :]
+            target = jnp.broadcast_to(target_ref[row : row + 1, :], (16, lanes)).astype(bf16)
             coef = jnp.sum(
                 jnp.where(source_ids == source, products[:, k * lanes : (k + 1) * lanes], 0.0),
                 axis=0,
@@ -96,22 +149,30 @@
                 )
             )
         out_ref[...] += jnp.dot(
-            jnp.concatenate(spread, 1), u_buf[pl.ds(base, part), :], preferred_element_type=f32
-        )
-        return 0
-
-    lax.fori_loop(0, chunks, step, 0)
-
-
-def near_part(source_ref, target_ref, columns_ref, tile_buf, columns_buf, count):
+            jnp.concatenate(spread, 1), u_buf[base : base + count, :], preferred_element_type=f32
+        )
+        step += body
+
+
+def near_part(hot_ref, target_ref, columns_ref, tiles_hbm, tile_buf, sems, count):
     tile_count = tile_buf.shape[0]
-    columns_buf[...] = columns_ref[...].astype(f32)
+    part = tile_count // near_chunks
+    copies = [
+        pltpu.make_async_copy(
+            tiles_hbm.at[i * part : (i + 1) * part], tile_buf.at[i * part : (i + 1) * part], sems.at[i]
+        )
+        for i in range(near_chunks)
+    ]
+    for copy in copies:
+        copy.start()
+    deficits = jnp.dot(hot_ref[...], columns_ref[...], preferred_element_type=f32)
     ids = lax.broadcasted_iota(jnp.int32, (count, lanes), 0)
     total = jnp.zeros((count, lanes), f32)
-    for t in range(tile_count):
-        deficit = jnp.broadcast_to(columns_buf[pl.ds(source_ref[t], 1), :], (count, lanes))
-        placed = jnp.where(ids == target_ref[t], deficit, 0.0).astype(bf16)
-        total += lax.dot_general(placed, tile_buf[t], by_row, preferred_element_type=f32)
+    for i, copy in enumerate(copies):
+        copy.wait()
+        for t in range(i * part, (i + 1) * part):
+            placed = jnp.where(ids == target_ref[t : t + 1, :], deficits[t : t + 1, :], 0.0).astype(bf16)
+            total += lax.dot_general(placed, tile_buf[t], by_row, preferred_element_type=f32)
     return total
 
 
@@ -147,19 +208,18 @@
     out_ref[...] = total_ref[...].astype(bf16)
 
 
-def near_kernel(near_source, near_target, columns_ref, tile_ref, out_ref, columns_buf):
-    out_ref[...] = near_part(
-        near_source, near_target, columns_ref, tile_ref, columns_buf, out_ref.shape[0]
-    )
+def near_kernel(hot_ref, target_ref, columns_ref, tiles_hbm, out_ref, tile_buf, sems):
+    count = out_ref.shape[0]
+    out_ref[...] = near_part(hot_ref, target_ref, columns_ref, tiles_hbm, tile_buf, sems, count)
 
 
 def near_send_kernel(
-    near_source, near_target, own_row, far_ref, columns_ref, tile_ref, out_ref, columns_buf, total_ref
+    hot_ref, target_ref, columns_ref, tiles_hbm, far_ref, out_ref, tile_buf, sems, total_ref
 ):
     count = out_ref.shape[1]
-    near = near_part(near_source, near_target, columns_ref, tile_ref, columns_buf, count)
+    near = near_part(hot_ref, target_ref, columns_ref, tiles_hbm, tile_buf, sems, count)
     total_ref[...] = far_ref[...]
-    own = pl.ds(pl.multiple_of(own_row[0] * count, count), count)
+    own = pl.ds(pl.multiple_of(lax.axis_index("src") * count, count), count)
     total_ref[own, :] += near
     total = total_ref[...].astype(bf16).reshape(-1, count, lanes)
     groups = total.shape[0]
@@ -175,12 +235,12 @@
         send_ref[k] = columns
 
 
-def update_kernel(recv_ref, stress_ref, *refs):
+def update_kernel(stress_ref, *refs):
     parts, (columns_ref, send_ref, own_ref) = refs[:-3], refs[-3:]
     group = stress_ref.shape[0] // len(parts)
     columns = []
     for k, part in enumerate(parts):
-        first = (recv_ref[0] ^ k) * group
+        first = (lax.axis_index("recv") ^ k) * group
         stress = stress_ref[first].astype(f32)
         for b in range(1, group):
             stress += stress_ref[first + b].astype(f32)
@@ -244,8 +304,6 @@
     src_count = lax.axis_size("src")
     recv_count = lax.axis_size("recv")
     device_count = src_count * recv_count
-    recv_index = lax.axis_index("recv")
-    src_index = lax.axis_index("src")
     tile_count = near_tiles.shape[0]
     own_clusters = log_rate.shape[0] // lanes
     group_rows = own_clusters * src_count
@@ -255,15 +313,23 @@
     params = pltpu.CompilerParams(vmem_limit_bytes=vmem_bytes)
     whole = (own_clusters, lanes)
 
-    order = cluster_order.reshape(whole)
-    own, shared = pl.pallas_call(
+    arguments = [x.reshape(whole) for x in (log_rate, log_state, a_sigma, b_sigma, crit_slip, plate_rate)]
+    own, shared, order = pl.pallas_call(
         order_kernel,
+        in_specs=[anywhere] * 7,
+        out_specs=(in_vmem,) * 3,
         out_shape=(
             jax.ShapeDtypeStruct((8,) + whole, f32),
             jax.ShapeDtypeStruct((4,) + whole, f32),
+            jax.ShapeDtypeStruct(whole, jnp.int32),
         ),
-        compiler_params=params,
-    )(*[x.reshape(whole) for x in (log_rate, log_state, a_sigma, b_sigma, crit_slip, plate_rate)], order)
+        scratch_shapes=[
+            pltpu.VMEM((6,) + whole, f32),
+            pltpu.VMEM(whole, jnp.int32),
+            pltpu.SemaphoreType.DMA((7,)),
+        ],
+        compiler_params=params,
+    )(*[in_hbm(x) for x in arguments + [cluster_order.reshape(whole)]])
 
     parts = [shared] + [
         lax.ppermute(shared, "recv", [(i, i ^ k) for i in range(recv_count)])
@@ -276,26 +342,31 @@
     )(*parts)
     all_first = lax.all_to_all(first_send, "src", split_axis=0, concat_axis=0, tiled=True)
 
-    near_own = lax.dynamic_slice_in_dim(near_pairs, src_index * tile_count, tile_count, 1)
-    near_target = near_own[0] - (recv_index * group_rows + src_index * own_clusters)
-
-    def group_place(cluster):
-        return ((cluster // group_rows) ^ recv_index) * own_clusters + cluster % own_clusters
-
-    near_source = near_own[1] // own_clusters % src_count * source_rows + group_place(near_own[1])
-    far_target = far_pairs[0] - recv_index * group_rows
-    far_source = group_place(far_pairs[1])
     table = (factor_rows // lanes, lanes)
-    source_table, target_table = pl.pallas_call(
-        functools.partial(table_kernel, rank=rank),
-        out_shape=(jax.ShapeDtypeStruct(table, jnp.int32), jax.ShapeDtypeStruct(table, f32)),
-        compiler_params=params,
-    )(*[x.reshape(far_count // lanes, lanes) for x in (far_source, far_target, far_ranks)])
-
-    v_rows = far_v.reshape(factor_rows, lanes)
-    u_rows = far_u.reshape(factor_rows, lanes)
+    hot = (tile_count, own_clusters * device_count)
+    source_table, target_table, near_hot, near_target = pl.pallas_call(
+        functools.partial(table_kernel, rank=rank, own_clusters=own_clusters, src_count=src_count),
+        in_specs=[in_smem, anywhere, anywhere],
+        out_specs=(in_vmem,) * 4,
+        out_shape=(
+            jax.ShapeDtypeStruct(table, jnp.int32),
+            jax.ShapeDtypeStruct(table, f32),
+            jax.ShapeDtypeStruct(hot, bf16),
+            jax.ShapeDtypeStruct((tile_count, lanes), jnp.int32),
+        ),
+        scratch_shapes=[
+            pltpu.VMEM(far_pairs.shape, jnp.int32),
+            pltpu.VMEM((far_count // lanes, lanes), jnp.int32),
+            pltpu.VMEM(hot, f32),
+            pltpu.SemaphoreType.DMA((2,)),
+        ],
+        compiler_params=params,
+    )(near_pairs, in_hbm(far_pairs), in_hbm(far_ranks.reshape(far_count // lanes, lanes)))
+
+    v_rows = in_hbm(far_v.reshape(factor_rows, lanes))
+    u_rows = in_hbm(far_u.reshape(factor_rows, lanes))
     far_specs = dict(
-        in_specs=[in_vmem] * 3 + [in_hbm] * 2,
+        in_specs=[in_vmem] * 3 + [anywhere] * 2,
         out_specs=in_vmem,
         compiler_params=pltpu.CompilerParams(vmem_limit_bytes=far_vmem_bytes),
         cost_estimate=pl.CostEstimate(
@@ -307,7 +378,8 @@
         pltpu.VMEM(u_rows.shape, bf16),
         pltpu.SemaphoreType.DMA((2, chunks)),
     ]
-    columns_scratch = pltpu.VMEM((own_clusters * device_count, lanes), f32)
+    tiles = in_hbm(near_tiles)
+    near_scratch = [pltpu.VMEM(near_tiles.shape, bf16), pltpu.SemaphoreType.DMA((near_chunks,))]
     total_scratch = pltpu.VMEM((group_rows, lanes), f32)
 
     first_far = pl.pallas_call(
@@ -318,21 +390,21 @@
     )(source_table, target_table, first_columns, v_rows, u_rows)
     partial = pl.pallas_call(
         near_send_kernel,
-        in_specs=[in_smem] * 3 + [in_vmem] * 3,
+        in_specs=[in_vmem] * 3 + [anywhere, in_vmem],
         out_specs=in_vmem,
         out_shape=jax.ShapeDtypeStruct((device_count,) + whole, bf16),
-        scratch_shapes=[columns_scratch, total_scratch],
-        compiler_params=params,
-    )(near_source, near_target, src_index.reshape(1), first_far, all_first.reshape(-1, lanes), near_tiles)
+        scratch_shapes=near_scratch + [total_scratch],
+        compiler_params=params,
+    )(near_hot, near_target, all_first.reshape(-1, lanes), tiles, first_far)
     stress_parts = lax.all_to_all(partial, ("recv", "src"), split_axis=0, concat_axis=0, tiled=True)
 
     second_columns, second_send, first_stress = pl.pallas_call(
         update_kernel,
-        in_specs=[in_smem] + [in_vmem] * (1 + recv_count),
+        in_specs=[in_vmem] * (1 + recv_count),
         out_specs=(in_vmem, in_vmem, in_vmem),
         out_shape=(columns_shape, send_shape, jax.ShapeDtypeStruct(whole, f32)),
         compiler_params=params,
-    )(recv_index.reshape(1), stress_parts, *parts)
+    )(stress_parts, *parts)
     all_second = lax.all_to_all(second_send, "src", split_axis=0, concat_axis=0, tiled=True)
     second_far = pl.pallas_call(
         far_send_kernel,
@@ -345,12 +417,12 @@
     )
     second_near = pl.pallas_call(
         near_kernel,
-        in_specs=[in_smem] * 2 + [in_vmem] * 2,
+        in_specs=[in_vmem] * 3 + [anywhere],
         out_specs=in_vmem,
         out_shape=jax.ShapeDtypeStruct(whole, f32),
-        scratch_shapes=[columns_scratch],
-        compiler_params=params,
-    )(near_source, near_target, all_second.reshape(-1, lanes), near_tiles)
+        scratch_shapes=near_scratch,
+        compiler_params=params,
+    )(near_hot, near_target, all_second.reshape(-1, lanes), tiles)
     new_p, new_q = pl.pallas_call(
         final_kernel,
         out_shape=(jax.ShapeDtypeStruct(whole, f32), jax.ShapeDtypeStruct(whole, f32)),

time: 72.6 us -> 64.2 us (0.88)
  local copies, waits for them, and re-layouts: 8.98 us -> 0.69 us
  Pallas kernels: 26.9 us -> 30.4 us
  waiting for transfers between devices: 3.53 us -> 1.32 us
  other arithmetic: 0.82 us -> 0 us
    unnamed x32 -> x2, local copies, waits for them, and re-layouts: 8.9 us -> 0.69 us
    pallas_call x5, Pallas kernels: 5.86 us -> 12.1 us  [the longest x1 4.64 us: on_device(): pl.pallas_call(near_kernel, in_specs=[in_vmem] * 3 + [anywhere], out_spec...]
    all_to_all x1, waiting for transfers between devices: 2.59 us -> 0.2 us  [on_device(): lax.all_to_all(second_far.reshape((src_count,) + whole), 'src', split_axi...]
    pallas_call x1, Pallas kernels: 9.71 us -> 7.98 us  [on_device(): pl.pallas_call(far_kernel, out_shape=jax.ShapeDtypeStruct((group_rows, la...]
    pallas_call x1, Pallas kernels: 9.56 us -> 8.59 us  [on_device(): pl.pallas_call(far_send_kernel, out_shape=jax.ShapeDtypeStruct((group_row...]
    sub x2 -> x0, other arithmetic: 0.79 us -> none  [the longest x1 0.78 us: on_device(): far_target = far_pairs[0] - recv_index * group_rows]
  transfers between devices with their start and end apart: 6 -> 6, of which waited for: 2 -> 2; matrix products, arithmetic and copies ran while one was open for 1% -> 0% of each run, Pallas kernels for 31% -> 37%
where the time goes in v3:
time: 64.2 us; the launch traced here: 63.6 us
  Pallas kernels  30.4 us (47%)
  starting transfers between devices  17 us (26%)
  blocking collectives  13.4 us (21%)
  waiting for transfers between devices  1.32 us (2%)
  between operations  0.72 us (1%)
  local copies, waits for them, and re-layouts  0.69 us (1%)
    all_to_all x1, blocking collectives, on_device(): lax.all_to_all(partial, ('recv', 'src'), split_axis=0, concat_axis=0, til...  13.4 us
    pallas_call x1, Pallas kernels, on_device(): pl.pallas_call(far_send_kernel, out_shape=jax.ShapeDtypeStruct((group_row...  8.59 us
    pallas_call x1, Pallas kernels, on_device(): pl.pallas_call(far_kernel, out_shape=jax.ShapeDtypeStruct((group_rows, la...  7.98 us
    ppermute x3, starting transfers between devices, on_device(): lax.ppermute(shared, 'recv', [(i, i ^ k) for i in range(recv_count)])  5.76 us
    pallas_call x1, Pallas kernels, on_device(): pl.pallas_call(near_kernel, in_specs=[in_vmem] * 3 + [anywhere], out_spec...  4.64 us
    all_to_all x1, starting transfers between devices, on_device(): lax.all_to_all(second_far.reshape((src_count,) + whole), 'src', split_axi...  3.97 us
    all_to_all x1, starting transfers between devices, on_device(): lax.all_to_all(first_send, 'src', split_axis=0, concat_axis=0, tiled=True)  3.72 us
    all_to_all x1, starting transfers between devices, on_device(): lax.all_to_all(second_send, 'src', split_axis=0, concat_axis=0, tiled=True)  3.55 us
  transfers between devices with their start and end apart: 6, of which 2 were waited for; matrix products, arithmetic and copies ran while one was open for 0% of the time, Pallas kernels for 37%

profile of v3, /device:TPU:0, one launch (start us, length us, event | category | flops | bytes accessed | tf_op | source)
XLA Modules:
  0.0 63.6 jit_solution(9841640603854363851)
XLA Ops:
  0.6 1.1 %shard_map.140 = (f32[8,16,128]{2,1,0:T(8,128)S(1)}, f32[4,16,128]{2,1,0:T(8,128)S(1)}, s32[16,128]{1,0:T(8,128)S(1)}) custom-call(f32[16,128]{1,0:T(8,128)} %bitcast.21, f32[16,128]{1,0:T(8,128)} %bitcast.22, f32[16,128]{1,0:T(8,128)} %bitcast.23, f32[16,128]{1,0:T(8,128)} %bitcast.24, f32[16,128]{1,0:T(8,128)} %bitcast.25, f32[16,128]{1,0:T(8,128)} %bitcast.26, ...), custom_call_target="tpu_custom_call" | custom-call | tf_op jit(solution)/shard_map/pallas_call | solution.py:317
  1.8 5.1 %collective-permute-start.2 = (f32[4,16,128]{2,1,0:T(8,128)S(1)}, f32[4,16,128]{2,1,0:T(8,128)S(1)}, u32[]{:S(2)}, u32[]{:S(2)}) collective-permute-start(f32[4,16,128]{2,1,0:T(8,128)S(1)} %get-tuple-element.19.refs_0_), channel_id=1, source_target_pairs={{0,24},{8,16},{16,8},{24,0},{1,25},{9,17},{17,9},{25,1},{2,26},{10... | collective-permute-start | bytes 98312 | tf_op jit(solution)/shard_map/ppermute | solution.py:335
  6.9 0.0 collective-permute-start.1
  6.9 0.6 %collective-permute-start = (f32[4,16,128]{2,1,0:T(8,128)S(1)}, f32[4,16,128]{2,1,0:T(8,128)S(1)}, u32[]{:S(2)}, u32[]{:S(2)}) collective-permute-start(f32[4,16,128]{2,1,0:T(8,128)S(1)} %get-tuple-element.19.refs_0_), channel_id=1, source_target_pairs={{0,8},{8,0},{16,24},{24,16},{1,9},{9,1},{17,25},{25,17},{2,10},{10... | collective-permute-start | bytes 98312 | tf_op jit(solution)/shard_map/ppermute | solution.py:335
  7.5 0.0 copy-start
  7.5 0.7 %copy-done = s32[2,768]{1,0:T(2,128)S(1)} copy-done((s32[2,768]{1,0:T(2,128)S(1)}, s32[2,768]{1,0:T(2,128)}, u32[]{:S(2)}) %copy-start) | copy-done | bytes 6168
  8.2 2.4 %shard_map.141 = (s32[256,128]{1,0:T(8,128)S(1)}, f32[256,128]{1,0:T(8,128)S(1)}, bf16[96,512]{1,0:T(8,128)(2,1)S(1)}, s32[96,128]{1,0:T(8,128)S(1)}) custom-call(s32[2,768]{1,0:T(2,128)S(1)} %copy-done, s32[2,1024]{1,0:T(2,128)} %far_pairs_hbm.1, s32[8,128]{1,0:T(8,128)} %bitcast.28), custom_call_target="tpu_custom_call" | custom-call | tf_op jit(solution)/shard_map/pallas_call | solution.py:347
  10.6 0.0 collective-permute-done.2.refs_3_
  10.6 1.1 %collective-permute-done.1.refs_2_ = f32[4,16,128]{2,1,0:T(8,128)S(1)} collective-permute-done((f32[4,16,128]{2,1,0:T(8,128)S(1)}, f32[4,16,128]{2,1,0:T(8,128)S(1)}, u32[]{:S(2)}, u32[]{:S(2)}) %collective-permute-start.1) | collective-permute-done | bytes 32800 | tf_op jit(solution)/shard_map/ppermute | solution.py:335
  11.7 0.0 collective-permute-done.refs_1_
  11.7 0.7 %shard_map.142 = (bf16[64,128]{1,0:T(8,128)(2,1)S(1)}, bf16[8,64,128]{2,1,0:T(8,128)(2,1)}) custom-call(f32[4,16,128]{2,1,0:T(8,128)S(1)} %get-tuple-element.19.refs_0_, f32[4,16,128]{2,1,0:T(8,128)S(1)} %collective-permute-done.refs_1_, f32[4,16,128]{2,1,0:T(8,128)S(1)} %collective-permute-done.1.refs_2_, f32[4,16,128]{2,1,0:T(8,128)S(1)} %collective-permute-done.2.refs_3_), custom_call_target="tpu_custom_call" | custom-call | tf_op jit(solution)/shard_map/pallas_call | solution.py:340
  12.4 3.7 %all-to-all-start = ((bf16[8,64,128]{2,1,0:T(8,128)(2,1)}), bf16[8,64,128]{2,1,0:T(8,128)(2,1)S(1)}, u32[]{:S(2)}, u32[]{:S(2)}) async-start(bf16[8,64,128]{2,1,0:T(8,128)(2,1)} %get-tuple-element.20), calls=%async_computation | async-start | bytes 262144 | tf_op jit(solution)/shard_map/all_to_all | solution.py:343
  16.1 8.0 %shard_map.143.far_ref = f32[128,128]{1,0:T(8,128)S(1)} custom-call(s32[256,128]{1,0:T(8,128)S(1)} %get-tuple-element.21.source_ref, f32[256,128]{1,0:T(8,128)S(1)} %get-tuple-element.22.target_ref, bf16[64,128]{1,0:T(8,128)(2,1)S(1)} %get-tuple-element.23.deficit_ref, bf16[32768,128]{1,0:T(8,128)(2,1)} %bitcast.17, bf16[32768,128]{1,0:T(8,128)(2,1)} %bitcast.19), custom_call_target="tpu_custom_call" | custom-call | flops 1610612736 | bytes 16777216 | tf_op jit(solution)/shard_map/pallas_call | solution.py:385
  24.1 0.0 all-to-all-done
  24.1 3.3 %shard_map.144 = bf16[32,16,128]{2,1,0:T(8,128)(2,1)S(1)} custom-call(bf16[96,512]{1,0:T(8,128)(2,1)S(1)} %get-tuple-element.17.hot_ref, s32[96,128]{1,0:T(8,128)S(1)} %get-tuple-element.18.target_ref, bf16[512,128]{1,0:T(8,128)(2,1)S(1)} %bitcast.15, bf16[96,128,128]{2,1,0:T(8,128)(2,1)} %tiles_hbm.3, f32[128,128]{1,0:T(8,128)S(1)} %shard_map.143.far_ref), custom_call_target="tpu_custom_call" | custom-call | tf_op jit(solution)/shard_map/pallas_call | solution.py:391
  27.4 13.4 %all_to_all.20.stress_ref = bf16[32,16,128]{2,1,0:T(8,128)(2,1)S(1)} all-to-all(bf16[32,16,128]{2,1,0:T(8,128)(2,1)S(1)} %shard_map.144), channel_id=1, replica_groups=mesh['recv'=4,'src'=8] {'recv','src'}, dimensions={0} | all-to-all | bytes 262144 | tf_op jit(solution)/shard_map/all_to_all | solution.py:399
  40.8 0.7 %shard_map.145 = (bf16[64,128]{1,0:T(8,128)(2,1)S(1)}, bf16[8,64,128]{2,1,0:T(8,128)(2,1)}, f32[16,128]{1,0:T(8,128)S(1)}) custom-call(bf16[32,16,128]{2,1,0:T(8,128)(2,1)S(1)} %all_to_all.20.stress_ref, f32[4,16,128]{2,1,0:T(8,128)S(1)} %get-tuple-element.19.refs_0_, f32[4,16,128]{2,1,0:T(8,128)S(1)} %collective-permute-done.refs_1_, ...), custom_call_target="tpu_custom_call" | custom-call | tf_op jit(solution)/shard_map/pallas_call | solution.py:401
  41.5 3.5 %all-to-all-start.3 = ((bf16[8,64,128]{2,1,0:T(8,128)(2,1)}), bf16[8,64,128]{2,1,0:T(8,128)(2,1)S(1)}, u32[]{:S(2)}, u32[]{:S(2)}) async-start(bf16[8,64,128]{2,1,0:T(8,128)(2,1)} %get-tuple-element.26), calls=%async_computation.3 | async-start | bytes 262144 | tf_op jit(solution)/shard_map/all_to_all | solution.py:408
  45.1 8.6 %shard_map.146 = bf16[128,128]{1,0:T(8,128)(2,1)} custom-call(s32[256,128]{1,0:T(8,128)S(1)} %get-tuple-element.21.source_ref, f32[256,128]{1,0:T(8,128)S(1)} %get-tuple-element.22.target_ref, bf16[64,128]{1,0:T(8,128)(2,1)S(1)} %get-tuple-element.25.deficit_ref, bf16[32768,128]{1,0:T(8,128)(2,1)} %bitcast.18, bf16[32768,128]{1,0:T(8,128)(2,1)} %bitcast.20), custom_call_target="tpu_custom_call" | custom-call | flops 1610612736 | bytes 16777216 | tf_op jit(solution)/shard_map/pallas_call | solution.py:409
  53.7 0.0 all-to-all-done.3
  53.7 4.0 %all-to-all-start.2 = ((bf16[8,16,128]{2,1,0:T(8,128)(2,1)}), bf16[8,16,128]{2,1,0:T(8,128)(2,1)S(1)}, u32[]{:S(2)}, u32[]{:S(2)}) async-start(bf16[8,16,128]{2,1,0:T(8,128)(2,1)} %bitcast.11), calls=%async_computation.2 | async-start | bytes 65536 | tf_op jit(solution)/shard_map/all_to_all | solution.py:415
  57.6 4.6 %shard_map.147.near_ref = f32[16,128]{1,0:T(8,128)S(1)} custom-call(bf16[96,512]{1,0:T(8,128)(2,1)S(1)} %get-tuple-element.17.hot_ref, s32[96,128]{1,0:T(8,128)S(1)} %get-tuple-element.18.target_ref, bf16[512,128]{1,0:T(8,128)(2,1)S(1)} %bitcast.16, bf16[96,128,128]{2,1,0:T(8,128)(2,1)} %tiles_hbm.3), custom_call_target="tpu_custom_call" | custom-call | tf_op jit(solution)/shard_map/pallas_call | solution.py:418
  62.3 0.2 all-to-all-done.2.second_ref
  62.5 1.1 %shard_map.148 = (f32[16,128]{1,0:T(8,128)}, f32[16,128]{1,0:T(8,128)}) custom-call(f32[8,16,128]{2,1,0:T(8,128)S(1)} %get-tuple-element.16.own_ref, f32[16,128]{1,0:T(8,128)S(1)} %get-tuple-element.24.first_ref, bf16[8,16,128]{2,1,0:T(8,128)(2,1)S(1)} %all-to-all-done.2.second_ref, f32[16,128]{1,0:T(8,128)S(1)} %shard_map.147.near_ref, ...), custom_call_target="tpu_custom_call" | custom-call | tf_op jit(solution)/shard_map/pallas_call | solution.py:426
Async XLA Ops:
  1.8 8.8 %collective-permute-start.2 = (f32[4,16,128]{2,1,0:T(8,128)S(1)}, f32[4,16,128]{2,1,0:T(8,128)S(1)}, u32[]{:S(2)}, u32[]{:S(2)}) collective-permute-start(f32[4,16,128]{2,1,0:T(8,128)S(1)} %get-tuple-element.19.refs_0_), channel_id=1, source_target_pairs={{0,24},{8,16},{16,8},{24,0},{1,25},{9,17},{17,9},{25,1},{2,26},{10... | collective-permute-start | bytes 98312 | tf_op jit(solution)/shard_map/ppermute | solution.py:335
  6.9 4.8 %collective-permute-start.1 = (f32[4,16,128]{2,1,0:T(8,128)S(1)}, f32[4,16,128]{2,1,0:T(8,128)S(1)}, u32[]{:S(2)}, u32[]{:S(2)}) collective-permute-start(f32[4,16,128]{2,1,0:T(8,128)S(1)} %get-tuple-element.19.refs_0_), channel_id=1, source_target_pairs={{0,16},{8,24},{16,0},{24,8},{1,17},{9,25},{17,1},{25,9},{2,18},{10... | collective-permute-start | bytes 98312 | tf_op jit(solution)/shard_map/ppermute | solution.py:335
  6.9 4.8 %collective-permute-start = (f32[4,16,128]{2,1,0:T(8,128)S(1)}, f32[4,16,128]{2,1,0:T(8,128)S(1)}, u32[]{:S(2)}, u32[]{:S(2)}) collective-permute-start(f32[4,16,128]{2,1,0:T(8,128)S(1)} %get-tuple-element.19.refs_0_), channel_id=1, source_target_pairs={{0,8},{8,0},{16,24},{24,16},{1,9},{9,1},{17,25},{25,17},{2,10},{10... | collective-permute-start | bytes 98312 | tf_op jit(solution)/shard_map/ppermute | solution.py:335
  7.5 0.7 %copy-start = (s32[2,768]{1,0:T(2,128)S(1)}, s32[2,768]{1,0:T(2,128)}, u32[]{:S(2)}) copy-start(s32[2,768]{1,0:T(2,128)} %near_pairs.1) | copy-start | bytes 18436
  12.4 11.7 %all-to-all-start = ((bf16[8,64,128]{2,1,0:T(8,128)(2,1)}), bf16[8,64,128]{2,1,0:T(8,128)(2,1)S(1)}, u32[]{:S(2)}, u32[]{:S(2)}) async-start(bf16[8,64,128]{2,1,0:T(8,128)(2,1)} %get-tuple-element.20), calls=%async_computation | async-start | bytes 262144 | tf_op jit(solution)/shard_map/all_to_all | solution.py:343
  41.5 12.2 %all-to-all-start.3 = ((bf16[8,64,128]{2,1,0:T(8,128)(2,1)}), bf16[8,64,128]{2,1,0:T(8,128)(2,1)S(1)}, u32[]{:S(2)}, u32[]{:S(2)}) async-start(bf16[8,64,128]{2,1,0:T(8,128)(2,1)} %get-tuple-element.26), calls=%async_computation.3 | async-start | bytes 262144 | tf_op jit(solution)/shard_map/all_to_all | solution.py:408
  53.7 8.8 %all-to-all-start.2 = ((bf16[8,16,128]{2,1,0:T(8,128)(2,1)}), bf16[8,16,128]{2,1,0:T(8,128)(2,1)S(1)}, u32[]{:S(2)}, u32[]{:S(2)}) async-start(bf16[8,16,128]{2,1,0:T(8,128)(2,1)} %bitcast.11), calls=%async_computation.2 | async-start | bytes 65536 | tf_op jit(solution)/shard_map/all_to_all | solution.py:415

commit v4 on v3

v4 whole, which is shorter than its diff:
```python
import functools

import jax
import jax.numpy as jnp
from jax import lax
from jax.experimental import pallas as pl
from jax.experimental.pallas import tpu as pltpu
from jax.sharding import PartitionSpec as P

time_step = 0.1
damping = 0.5
f32 = jnp.float32
bf16 = jnp.bfloat16
lanes = 128
chunks = 8
code_base = 4096
vmem_bytes = 8 * 2**20
far_vmem_bytes = 28 * 2**20
bodies = (1, 2, 2, 2, 1)
by_row = (((1,), (1,)), ((), ()))
in_vmem = pl.BlockSpec(memory_space=pltpu.VMEM)
anywhere = pl.BlockSpec(memory_space=pl.ANY)
in_smem = pl.BlockSpec(memory_space=pltpu.SMEM)


def in_hbm(x):
    return pltpu.with_memory_space_constraint(x, pltpu.HBM)


def order_kernel(*refs):
    arguments, (own_ref, deficit_ref, order_out, buf, order_buf, sems) = refs[:7], refs[7:]
    count = len(arguments) - 1
    copies = [
        pltpu.make_async_copy(ref, order_buf if k == count else buf.at[k], sems.at[k])
        for k, ref in enumerate(arguments)
    ]
    for copy in copies:
        copy.start()
    for copy in copies:
        copy.wait()
    order = order_buf[...]
    order_out[...] = order
    row, lane = order // lanes, order % lanes
    rows = order.shape[0]
    sorted_values = [jnp.zeros(order.shape, f32)] * count
    for r in range(rows):
        here = row == r
        for k in range(count):
            spread = jnp.broadcast_to(buf[k, r : r + 1, :], order.shape)
            got = jnp.take_along_axis(spread, lane, axis=1)
            sorted_values[k] = jnp.where(here, got, sorted_values[k])
    p, q, a, b, slip, plate = sorted_values
    speed = jnp.exp(p)
    theta_rate = jnp.exp(-q) - speed / slip
    gain = 1.0 / (a + damping * speed)
    for k, value in enumerate((p, q, a, b, slip, plate, theta_rate, gain)):
        own_ref[k] = value
    deficit_ref[...] = (plate - speed).astype(bf16)


def table_kernel(
    near_pairs, far_pairs_hbm, rank_hbm, far_out, near_out, far_pairs, rank_ref, sems, *, rank, own_clusters, src_count
):
    copies = (
        pltpu.make_async_copy(far_pairs_hbm, far_pairs, sems.at[0]),
        pltpu.make_async_copy(rank_hbm, rank_ref, sems.at[1]),
    )
    for copy in copies:
        copy.start()
    recv_index, src_index = lax.axis_index("recv"), lax.axis_index("src")
    group_rows = own_clusters * src_count
    source_rows = own_clusters * lax.axis_size("recv")

    def group_place(cluster):
        return ((cluster // group_rows) ^ recv_index) * own_clusters + cluster % own_clusters

    tile_count = near_out.shape[0]
    first_own = recv_index * group_rows + src_index * own_clusters
    for t in range(tile_count):
        target = near_pairs[0, src_index * tile_count + t] - first_own
        source = near_pairs[1, src_index * tile_count + t]
        place = (source // own_clusters) % src_count * source_rows + group_place(source)
        near_out[t : t + 1, :] = jnp.full((1, lanes), target * code_base + place, jnp.int32)

    for copy in copies:
        copy.wait()
    per_row = lanes // rank
    group = lanes // per_row
    shape = (group, lanes)
    lane = lax.broadcasted_iota(jnp.int32, shape, 1)
    pick = lax.broadcasted_iota(jnp.int32, shape, 0) * per_row + lane // rank

    def spread(row):
        return jnp.take_along_axis(jnp.broadcast_to(row, shape), pick, axis=1)

    for a in range(rank_ref.shape[0]):
        across = slice(a * lanes, (a + 1) * lanes)
        target = (far_pairs[0:1, across] - recv_index * group_rows) * code_base
        source = spread(target + group_place(far_pairs[1:2, across]))
        missing = spread(target + (code_base - 1))
        far_out[a * group : (a + 1) * group, :] = jnp.where(
            lane % rank < spread(rank_ref[a : a + 1, :]), source, missing
        )


def far_part(code_ref, deficit, v_buf, u_buf, out_ref, before):
    factor_rows = v_buf.shape[0]
    part = factor_rows // chunks
    source_count = deficit.shape[0]
    target_count = out_ref.shape[0]
    source_ids = lax.broadcasted_iota(jnp.int32, (source_count, lanes), 0)
    target_ids = [
        (lax.broadcasted_iota(jnp.int32, (16, lanes), 0) + 16 * k).astype(f32).astype(bf16)
        for k in range(target_count // 16)
    ]
    out_ref[...] = jnp.zeros_like(out_ref)

    step = 0
    for body in bodies:
        for i in range(step, step + body):
            before(i)
        base, count = step * part, body * part
        products = lax.dot_general(
            deficit, v_buf[base : base + count, :], by_row, preferred_element_type=f32
        )
        spread = []
        for k in range(count // lanes):
            row = base // lanes + k
            code = code_ref[row : row + 1, :]
            source = code % code_base
            target = jnp.broadcast_to((code // code_base).astype(f32), (16, lanes)).astype(bf16)
            coef = jnp.sum(
                jnp.where(source_ids == source, products[:, k * lanes : (k + 1) * lanes], 0.0),
                axis=0,
                keepdims=True,
            )
            coef = jnp.broadcast_to(coef, (16, lanes)).astype(bf16)
            spread.append(
                jnp.concatenate(
                    [jnp.where(ids == target, coef, jnp.zeros_like(coef)) for ids in target_ids], 0
                )
            )
        out_ref[...] += jnp.dot(
            jnp.concatenate(spread, 1), u_buf[base : base + count, :], preferred_element_type=f32
        )
        step += body


def far_kernel(code_ref, *refs):
    parts, (v_hbm, u_hbm, out_ref, v_buf, u_buf, sems, total_ref) = refs[:-7], refs[-7:]
    part = v_hbm.shape[0] // chunks

    def copies(i):
        where = slice(i * part, (i + 1) * part)
        return (
            pltpu.make_async_copy(v_hbm.at[where], v_buf.at[where], sems.at[0, i]),
            pltpu.make_async_copy(u_hbm.at[where], u_buf.at[where], sems.at[1, i]),
        )

    for i in range(chunks):
        for copy in copies(i):
            copy.start()

    def before(i):
        for copy in copies(i):
            copy.wait()

    deficit = jnp.concatenate([ref[...] for ref in parts], 0)
    count = parts[0].shape[0]
    for k in range(out_ref.shape[0]):
        out_ref[k, count:, :] = deficit
    far_part(code_ref, deficit, v_buf, u_buf, total_ref, before)
    for k in range(out_ref.shape[0]):
        out_ref[k, :count, :] = total_ref[k * count : (k + 1) * count, :].astype(bf16)


def whole_stress(code_ref, came_ref, tile_ref, count):
    senders = came_ref.shape[0]
    columns = jnp.concatenate([came_ref[k, count:, :] for k in range(senders)], 0)
    tile_count = tile_ref.shape[0]
    code = code_ref[...]
    place, target = code % code_base, code // code_base
    place_ids = lax.broadcasted_iota(jnp.int32, (tile_count, lanes), 1)
    deficits = jnp.zeros((tile_count, lanes), f32)
    for k in range(columns.shape[0] // lanes):
        hot = jnp.where(place_ids + k * lanes == place, 1.0, 0.0).astype(bf16)
        deficits += jnp.dot(hot, columns[k * lanes : (k + 1) * lanes, :], preferred_element_type=f32)
    ids = lax.broadcasted_iota(jnp.int32, (count, lanes), 0)
    placed = [
        jnp.where(ids == target[t : t + 1, :], deficits[t : t + 1, :], 0.0).astype(bf16)
        for t in range(tile_count)
    ]
    near = lax.dot_general(
        jnp.concatenate(placed, 1),
        jnp.concatenate([tile_ref[t] for t in range(tile_count)], 1),
        by_row,
        preferred_element_type=f32,
    )
    far = came_ref[0, :count, :].astype(f32)
    for k in range(1, senders):
        far += came_ref[k, :count, :].astype(f32)
    return far + near


def first_kernel(code_ref, came_ref, tile_ref, own_ref, stress_ref, deficit_ref):
    stress = whole_stress(code_ref, came_ref, tile_ref, stress_ref.shape[0])
    stress_ref[...] = stress
    p, b, plate, theta_rate, gain = [own_ref[k] for k in (0, 3, 5, 6, 7)]
    speed = jnp.exp(p + time_step * ((stress - b * theta_rate) * gain))
    deficit_ref[...] = (plate - speed).astype(bf16)


def final_kernel(code_ref, came_ref, tile_ref, own_ref, first_ref, order_ref, p_out, q_out):
    stress = whole_stress(code_ref, came_ref, tile_ref, first_ref.shape[0])
    p, q, a, b, slip, plate, theta_rate, gain = [own_ref[k] for k in range(8)]
    first_p = (first_ref[...] - b * theta_rate) * gain
    speed = jnp.exp(p + time_step * first_p)
    second_q = jnp.exp(-(q + time_step * theta_rate)) - speed / slip
    second_p = (stress - b * second_q) / (a + damping * speed)
    new_p = p + 0.5 * time_step * (first_p + second_p)
    new_q = q + 0.5 * time_step * (theta_rate + second_q)
    pieces = []
    for value in (new_p, new_q):
        for _ in range(3):
            piece = value.astype(bf16).astype(f32)
            value = value - piece
            pieces.append(piece)
    rows = p.shape[0]
    order = order_ref[...]
    row, lane = order // lanes, order % lanes
    row_ids = lax.broadcasted_iota(jnp.int32, (rows, lanes), 0)
    lane_ids = lax.broadcasted_iota(jnp.int32, (lanes, lanes), 0)
    total = jnp.zeros((len(pieces) * rows, lanes), f32)
    for r in range(rows):
        here = row_ids == row[r : r + 1, :]
        placed = jnp.concatenate(
            [jnp.where(here, piece[r : r + 1, :], 0.0) for piece in pieces], 0
        ).astype(bf16)
        spread = jnp.where(lane_ids == lane[r : r + 1, :], 1.0, 0.0).astype(bf16)
        total += lax.dot_general(placed, spread, by_row, preferred_element_type=f32)
    for k, out in enumerate((p_out, q_out)):
        high, mid, low = [total[(3 * k + j) * rows : (3 * k + j + 1) * rows, :] for j in range(3)]
        out[...] = (low + mid) + high


def on_device(
    log_rate,
    log_state,
    a_sigma,
    b_sigma,
    crit_slip,
    plate_rate,
    cluster_order,
    near_tiles,
    near_pairs,
    far_u,
    far_v,
    far_pairs,
    far_ranks,
):
    src_count = lax.axis_size("src")
    recv_count = lax.axis_size("recv")
    device_count = src_count * recv_count
    tile_count = near_tiles.shape[0]
    own_clusters = log_rate.shape[0] // lanes
    group_rows = own_clusters * src_count
    source_rows = own_clusters * recv_count
    far_count, rank = far_u.shape[:2]
    factor_rows = far_count * rank
    params = pltpu.CompilerParams(vmem_limit_bytes=vmem_bytes)
    whole = (own_clusters, lanes)

    arguments = [x.reshape(whole) for x in (log_rate, log_state, a_sigma, b_sigma, crit_slip, plate_rate)]
    own, first_deficit, order = pl.pallas_call(
        order_kernel,
        in_specs=[anywhere] * 7,
        out_specs=(in_vmem,) * 3,
        out_shape=(
            jax.ShapeDtypeStruct((8,) + whole, f32),
            jax.ShapeDtypeStruct(whole, bf16),
            jax.ShapeDtypeStruct(whole, jnp.int32),
        ),
        scratch_shapes=[
            pltpu.VMEM((6,) + whole, f32),
            pltpu.VMEM(whole, jnp.int32),
            pltpu.SemaphoreType.DMA((7,)),
        ],
        compiler_params=params,
    )(*[in_hbm(x) for x in arguments + [cluster_order.reshape(whole)]])

    far_codes, near_codes = pl.pallas_call(
        functools.partial(table_kernel, rank=rank, own_clusters=own_clusters, src_count=src_count),
        in_specs=[in_smem, anywhere, anywhere],
        out_specs=(in_vmem,) * 2,
        out_shape=(
            jax.ShapeDtypeStruct((factor_rows // lanes, lanes), jnp.int32),
            jax.ShapeDtypeStruct((tile_count, lanes), jnp.int32),
        ),
        scratch_shapes=[
            pltpu.VMEM(far_pairs.shape, jnp.int32),
            pltpu.VMEM((far_count // lanes, lanes), jnp.int32),
            pltpu.SemaphoreType.DMA((2,)),
        ],
        compiler_params=params,
    )(near_pairs, in_hbm(far_pairs), in_hbm(far_ranks.reshape(far_count // lanes, lanes)))

    v_rows = in_hbm(far_v.reshape(factor_rows, lanes))
    u_rows = in_hbm(far_u.reshape(factor_rows, lanes))

    def exchange(deficit):
        parts = [deficit] + [
            lax.ppermute(deficit, "recv", [(i, i ^ k) for i in range(recv_count)])
            for k in range(1, recv_count)
        ]
        send = pl.pallas_call(
            far_kernel,
            in_specs=[in_vmem] * (1 + recv_count) + [anywhere] * 2,
            out_specs=in_vmem,
            out_shape=jax.ShapeDtypeStruct((src_count, own_clusters + source_rows, lanes), bf16),
            scratch_shapes=[
                pltpu.VMEM(v_rows.shape, bf16),
                pltpu.VMEM(u_rows.shape, bf16),
                pltpu.SemaphoreType.DMA((2, chunks)),
                pltpu.VMEM((group_rows, lanes), f32),
            ],
            compiler_params=pltpu.CompilerParams(vmem_limit_bytes=far_vmem_bytes),
            cost_estimate=pl.CostEstimate(
                flops=2 * factor_rows * lanes * (source_rows + group_rows), bytes_accessed=2**24, transcendentals=0
            ),
        )(far_codes, *parts, v_rows, u_rows)
        return lax.all_to_all(send, "src", split_axis=0, concat_axis=0, tiled=True)

    first_stress, second_deficit = pl.pallas_call(
        first_kernel,
        in_specs=[in_vmem] * 4,
        out_specs=(in_vmem,) * 2,
        out_shape=(jax.ShapeDtypeStruct(whole, f32), jax.ShapeDtypeStruct(whole, bf16)),
        compiler_params=params,
    )(near_codes, exchange(first_deficit), near_tiles, own)
    new_p, new_q = pl.pallas_call(
        final_kernel,
        out_shape=(jax.ShapeDtypeStruct(whole, f32), jax.ShapeDtypeStruct(whole, f32)),
        compiler_params=params,
    )(near_codes, exchange(second_deficit), near_tiles, own, first_stress, order)
    return new_p.reshape(-1), new_q.reshape(-1)


def solution(mesh):
    return jax.shard_map(
        on_device,
        mesh=mesh,
        in_specs=(
            P(("recv", "src")),
            P(("recv", "src")),
            P(("recv", "src")),
            P(("recv", "src")),
            P(("recv", "src")),
            P(("recv", "src")),
            P(("recv", "src"), None),
            P(("recv", "src"), None, None),
            P(None, "recv"),
            P(("recv", "src"), None, None),
            P(("recv", "src"), None, None),
            P(None, ("recv", "src")),
            P(("recv", "src")),
        ),
        out_specs=(P(("recv", "src")), P(("recv", "src"))),
        check_vma=False,
    )
```

time: 64.2 us -> 57.1 us (0.89)
  starting transfers between devices: 17 us -> 10.2 us
  Pallas kernels: 30.4 us -> 23.6 us
  blocking collectives: 13.4 us -> 17.7 us
  waiting for transfers between devices: 1.32 us -> 3.9 us
    all_to_all x3 -> x0, starting transfers between devices: 11.2 us -> none  [the longest x1 3.97 us: on_device(): lax.all_to_all(second_far.reshape((src_count,) + whole), 'src', split_axi...]
    pallas_call x6 -> x3, Pallas kernels: 25.8 us -> 17.4 us  [the longest x2 16.3 us: exchange(): pl.pallas_call(far_kernel, in_specs=[in_vmem] * (1 + recv_count) + [anywh...]
    ppermute x3 -> x6, starting transfers between devices: 5.76 us -> 10.2 us  [exchange(): lax.ppermute(deficit, 'recv', [(i, i ^ k) for i in range(recv_count)])]
    all_to_all x1 -> x2, blocking collectives: 13.4 us -> 17.7 us  [exchange(): return lax.all_to_all(send, 'src', split_axis=0, concat_axis=0, tiled=True)]
    ppermute x3 -> x6, waiting for transfers between devices: 1.11 us -> 3.9 us  [exchange(): lax.ppermute(deficit, 'recv', [(i, i ^ k) for i in range(recv_count)])]
    pallas_call x1, Pallas kernels: 1.09 us -> 2.65 us  [on_device(): pl.pallas_call(final_kernel, out_shape=(jax.ShapeDtypeStruct(whole, f32),...]
  transfers between devices with their start and end apart: 6 -> 6, of which waited for: 2 -> 3; matrix products, arithmetic and copies ran while one was open for 0% -> 0% of each run, Pallas kernels for 37% -> 4%
where the time goes in v4:
time: 57.1 us; the launch traced here: 56.7 us
  Pallas kernels  23.6 us (41%)
  blocking collectives  17.7 us (31%)
  starting transfers between devices  10.2 us (18%)
  waiting for transfers between devices  3.9 us (7%)
  local copies, waits for them, and re-layouts  0.69 us (1%)
  between operations  0.68 us (1%)
    all_to_all x2, blocking collectives, exchange(): return lax.all_to_all(send, 'src', split_axis=0, concat_axis=0, tiled=True)  17.7 us
    pallas_call x2, Pallas kernels, exchange(): pl.pallas_call(far_kernel, in_specs=[in_vmem] * (1 + recv_count) + [anywh...  16.3 us
    ppermute x6, starting transfers between devices, exchange(): lax.ppermute(deficit, 'recv', [(i, i ^ k) for i in range(recv_count)])  10.2 us
    ppermute x6, waiting for transfers between devices, exchange(): lax.ppermute(deficit, 'recv', [(i, i ^ k) for i in range(recv_count)])  3.9 us
    pallas_call x1, Pallas kernels, on_device(): pl.pallas_call(final_kernel, out_shape=(jax.ShapeDtypeStruct(whole, f32),...  2.65 us
    pallas_call x1, Pallas kernels, on_device(): pl.pallas_call(functools.partial(table_kernel, rank=rank, own_clusters=ow...  2.42 us
  transfers between devices with their start and end apart: 6, of which 3 were waited for; matrix products, arithmetic and copies ran while one was open for 0% of the time, Pallas kernels for 4%

profile of v4, /device:TPU:0, one launch (start us, length us, event | category | flops | bytes accessed | tf_op | source)
XLA Modules:
  0.0 56.7 jit_solution(10694503888226093693)
XLA Ops:
  0.6 1.1 %shard_map.141 = (f32[8,16,128]{2,1,0:T(8,128)S(1)}, bf16[16,128]{1,0:T(8,128)(2,1)S(1)}, s32[16,128]{1,0:T(8,128)S(1)}) custom-call(f32[16,128]{1,0:T(8,128)} %bitcast.16, f32[16,128]{1,0:T(8,128)} %bitcast.17, f32[16,128]{1,0:T(8,128)} %bitcast.18, f32[16,128]{1,0:T(8,128)} %bitcast.19, f32[16,128]{1,0:T(8,128)} %bitcast.20, f32[16,128]{1,0:T(8,128)} %bitcast.21, ...), custom_call_target="tpu_custom_call" | custom-call | tf_op jit(solution)/shard_map/pallas_call | solution.py:274
  1.8 5.1 %collective-permute-start.2 = (bf16[16,128]{1,0:T(8,128)(2,1)S(1)}, bf16[16,128]{1,0:T(8,128)(2,1)S(1)}, u32[]{:S(2)}, u32[]{:S(2)}) collective-permute-start(bf16[16,128]{1,0:T(8,128)(2,1)S(1)} %get-tuple-element.13.refs_0_), channel_id=1, source_target_pairs={{0,24},{8,16},{16,8},{24,0},{1,25},{9,17},{17,9},{25,1},{2,26},{10... | collective-permute-start | bytes 12296 | tf_op jit(solution)/shard_map/ppermute | solution.py:312
  6.9 0.0 collective-permute-start.1
  6.9 0.6 %collective-permute-start = (bf16[16,128]{1,0:T(8,128)(2,1)S(1)}, bf16[16,128]{1,0:T(8,128)(2,1)S(1)}, u32[]{:S(2)}, u32[]{:S(2)}) collective-permute-start(bf16[16,128]{1,0:T(8,128)(2,1)S(1)} %get-tuple-element.13.refs_0_), channel_id=1, source_target_pairs={{0,8},{8,0},{16,24},{24,16},{1,9},{9,1},{17,25},{25,17},{2,10},{10... | collective-permute-start | bytes 12296 | tf_op jit(solution)/shard_map/ppermute | solution.py:312
  7.5 0.0 copy-start.1
  7.5 0.7 %copy-done.1 = s32[2,768]{1,0:T(2,128)S(1)} copy-done((s32[2,768]{1,0:T(2,128)S(1)}, s32[2,768]{1,0:T(2,128)}, u32[]{:S(2)}) %copy-start.1) | copy-done | bytes 6168
  8.2 2.4 %shard_map.140 = (s32[256,128]{1,0:T(8,128)S(1)}, s32[96,128]{1,0:T(8,128)S(1)}) custom-call(s32[2,768]{1,0:T(2,128)S(1)} %copy-done.1, s32[2,1024]{1,0:T(2,128)} %far_pairs_hbm.1, s32[8,128]{1,0:T(8,128)} %bitcast.23), custom_call_target="tpu_custom_call" | custom-call | tf_op jit(solution)/shard_map/pallas_call | solution.py:291
  10.7 0.0 collective-permute-done.2.refs_3_
  10.7 0.7 %collective-permute-done.1.refs_2_ = bf16[16,128]{1,0:T(8,128)(2,1)S(1)} collective-permute-done((bf16[16,128]{1,0:T(8,128)(2,1)S(1)}, bf16[16,128]{1,0:T(8,128)(2,1)S(1)}, u32[]{:S(2)}, u32[]{:S(2)}) %collective-permute-start.1) | collective-permute-done | bytes 4128 | tf_op jit(solution)/shard_map/ppermute | solution.py:312
  11.4 0.0 collective-permute-done.refs_1_
  11.4 0.0 copy-start
  11.4 8.2 %shard_map.142 = bf16[8,80,128]{2,1,0:T(8,128)(2,1)S(1)} custom-call(s32[256,128]{1,0:T(8,128)S(1)} %get-tuple-element.12.code_ref, bf16[16,128]{1,0:T(8,128)(2,1)S(1)} %get-tuple-element.13.refs_0_, bf16[16,128]{1,0:T(8,128)(2,1)S(1)} %collective-permute-done.refs_1_, bf16[16,128]{1,0:T(8,128)(2,1)S(1)} %collective-permute-done.1.refs_2_, ...), custom_call_target="tpu_custom_call" | custom-call | flops 1610612736 | bytes 16777216 | tf_op jit(solution)/shard_map/pallas_call | solution.py:315
  19.6 9.4 %all_to_all.10.came_ref = bf16[8,80,128]{2,1,0:T(8,128)(2,1)S(1)} all-to-all(bf16[8,80,128]{2,1,0:T(8,128)(2,1)S(1)} %shard_map.142), channel_id=1, replica_groups=mesh['recv'=4,'src'=8] {'src'}, dimensions={0} | all-to-all | bytes 327680 | tf_op jit(solution)/shard_map/all_to_all | solution.py:331
  29.0 0.0 copy-done
  29.0 1.1 %shard_map.143 = (f32[16,128]{1,0:T(8,128)S(1)}, bf16[16,128]{1,0:T(8,128)(2,1)S(1)}) custom-call(s32[96,128]{1,0:T(8,128)S(1)} %get-tuple-element.11.code_ref, bf16[8,80,128]{2,1,0:T(8,128)(2,1)S(1)} %all_to_all.10.came_ref, bf16[96,128,128]{2,1,0:T(8,128)(2,1)S(1)} %copy-done, f32[8,16,128]{2,1,0:T(8,128)S(1)} %get-tuple-element.14.own_ref), custom_call_target="tpu_custom_call" | custom-call | tf_op jit(solution)/shard_map/pallas_call | solution.py:333
  30.1 3.1 %collective-permute-start.5 = (bf16[16,128]{1,0:T(8,128)(2,1)S(1)}, bf16[16,128]{1,0:T(8,128)(2,1)S(1)}, u32[]{:S(2)}, u32[]{:S(2)}) collective-permute-start(bf16[16,128]{1,0:T(8,128)(2,1)S(1)} %get-tuple-element.15.refs_0_), channel_id=1, source_target_pairs={{0,24},{8,16},{16,8},{24,0},{1,25},{9,17},{17,9},{25,1},{2,26},{10... | collective-permute-start | bytes 12296 | tf_op jit(solution)/shard_map/ppermute | solution.py:312
  33.3 0.0 collective-permute-start.4
  33.3 1.3 %collective-permute-start.3 = (bf16[16,128]{1,0:T(8,128)(2,1)S(1)}, bf16[16,128]{1,0:T(8,128)(2,1)S(1)}, u32[]{:S(2)}, u32[]{:S(2)}) collective-permute-start(bf16[16,128]{1,0:T(8,128)(2,1)S(1)} %get-tuple-element.15.refs_0_), channel_id=1, source_target_pairs={{0,8},{8,0},{16,24},{24,16},{1,9},{9,1},{17,25},{25,17},{2,10},{10... | collective-permute-start | bytes 12296 | tf_op jit(solution)/shard_map/ppermute | solution.py:312
  34.6 1.0 %collective-permute-done.5.refs_3_ = bf16[16,128]{1,0:T(8,128)(2,1)S(1)} collective-permute-done((bf16[16,128]{1,0:T(8,128)(2,1)S(1)}, bf16[16,128]{1,0:T(8,128)(2,1)S(1)}, u32[]{:S(2)}, u32[]{:S(2)}) %collective-permute-start.5) | collective-permute-done | bytes 4128 | tf_op jit(solution)/shard_map/ppermute | solution.py:312
  35.6 2.1 %collective-permute-done.4.refs_2_ = bf16[16,128]{1,0:T(8,128)(2,1)S(1)} collective-permute-done((bf16[16,128]{1,0:T(8,128)(2,1)S(1)}, bf16[16,128]{1,0:T(8,128)(2,1)S(1)}, u32[]{:S(2)}, u32[]{:S(2)}) %collective-permute-start.4) | collective-permute-done | bytes 4128 | tf_op jit(solution)/shard_map/ppermute | solution.py:312
  37.8 0.0 collective-permute-done.3.refs_1_
  37.8 8.1 %shard_map.144 = bf16[8,80,128]{2,1,0:T(8,128)(2,1)S(1)} custom-call(s32[256,128]{1,0:T(8,128)S(1)} %get-tuple-element.12.code_ref, bf16[16,128]{1,0:T(8,128)(2,1)S(1)} %get-tuple-element.15.refs_0_, bf16[16,128]{1,0:T(8,128)(2,1)S(1)} %collective-permute-done.3.refs_1_, bf16[16,128]{1,0:T(8,128)(2,1)S(1)} %collective-permute-done.4.refs_2_, ...), custom_call_target="tpu_custom_call" | custom-call | flops 1610612736 | bytes 16777216 | tf_op jit(solution)/shard_map/pallas_call | solution.py:315
  45.8 8.3 %all_to_all.11.came_ref = bf16[8,80,128]{2,1,0:T(8,128)(2,1)S(1)} all-to-all(bf16[8,80,128]{2,1,0:T(8,128)(2,1)S(1)} %shard_map.144), channel_id=1, replica_groups=mesh['recv'=4,'src'=8] {'src'}, dimensions={0} | all-to-all | bytes 327680 | tf_op jit(solution)/shard_map/all_to_all | solution.py:331
  54.1 2.6 %shard_map.145 = (f32[16,128]{1,0:T(8,128)}, f32[16,128]{1,0:T(8,128)}) custom-call(s32[96,128]{1,0:T(8,128)S(1)} %get-tuple-element.11.code_ref, bf16[8,80,128]{2,1,0:T(8,128)(2,1)S(1)} %all_to_all.11.came_ref, bf16[96,128,128]{2,1,0:T(8,128)(2,1)S(1)} %copy-done, f32[8,16,128]{2,1,0:T(8,128)S(1)} %get-tuple-element.14.own_ref, ...), custom_call_target="tpu_custom_call" | custom-call | tf_op jit(solution)/shard_map/pallas_call | solution.py:340
Async XLA Ops:
  1.8 8.9 %collective-permute-start.2 = (bf16[16,128]{1,0:T(8,128)(2,1)S(1)}, bf16[16,128]{1,0:T(8,128)(2,1)S(1)}, u32[]{:S(2)}, u32[]{:S(2)}) collective-permute-start(bf16[16,128]{1,0:T(8,128)(2,1)S(1)} %get-tuple-element.13.refs_0_), channel_id=1, source_target_pairs={{0,24},{8,16},{16,8},{24,0},{1,25},{9,17},{17,9},{25,1},{2,26},{10... | collective-permute-start | bytes 12296 | tf_op jit(solution)/shard_map/ppermute | solution.py:312
  6.9 4.5 %collective-permute-start.1 = (bf16[16,128]{1,0:T(8,128)(2,1)S(1)}, bf16[16,128]{1,0:T(8,128)(2,1)S(1)}, u32[]{:S(2)}, u32[]{:S(2)}) collective-permute-start(bf16[16,128]{1,0:T(8,128)(2,1)S(1)} %get-tuple-element.13.refs_0_), channel_id=1, source_target_pairs={{0,16},{8,24},{16,0},{24,8},{1,17},{9,25},{17,1},{25,9},{2,18},{10... | collective-permute-start | bytes 12296 | tf_op jit(solution)/shard_map/ppermute | solution.py:312
  6.9 4.5 %collective-permute-start = (bf16[16,128]{1,0:T(8,128)(2,1)S(1)}, bf16[16,128]{1,0:T(8,128)(2,1)S(1)}, u32[]{:S(2)}, u32[]{:S(2)}) collective-permute-start(bf16[16,128]{1,0:T(8,128)(2,1)S(1)} %get-tuple-element.13.refs_0_), channel_id=1, source_target_pairs={{0,8},{8,0},{16,24},{24,16},{1,9},{9,1},{17,25},{25,17},{2,10},{10... | collective-permute-start | bytes 12296 | tf_op jit(solution)/shard_map/ppermute | solution.py:312
  7.5 0.7 %copy-start.1 = (s32[2,768]{1,0:T(2,128)S(1)}, s32[2,768]{1,0:T(2,128)}, u32[]{:S(2)}) copy-start(s32[2,768]{1,0:T(2,128)} %near_pairs.1) | copy-start | bytes 18436
  11.4 17.6 %copy-start = (bf16[96,128,128]{2,1,0:T(8,128)(2,1)S(1)}, bf16[96,128,128]{2,1,0:T(8,128)(2,1)}, u32[]{:S(2)}) copy-start(bf16[96,128,128]{2,1,0:T(8,128)(2,1)} %tile_ref.3) | copy-start | bytes 9437188
  30.1 5.5 %collective-permute-start.5 = (bf16[16,128]{1,0:T(8,128)(2,1)S(1)}, bf16[16,128]{1,0:T(8,128)(2,1)S(1)}, u32[]{:S(2)}, u32[]{:S(2)}) collective-permute-start(bf16[16,128]{1,0:T(8,128)(2,1)S(1)} %get-tuple-element.15.refs_0_), channel_id=1, source_target_pairs={{0,24},{8,16},{16,8},{24,0},{1,25},{9,17},{17,9},{25,1},{2,26},{10... | collective-permute-start | bytes 12296 | tf_op jit(solution)/shard_map/ppermute | solution.py:312
  33.3 4.5 %collective-permute-start.4 = (bf16[16,128]{1,0:T(8,128)(2,1)S(1)}, bf16[16,128]{1,0:T(8,128)(2,1)S(1)}, u32[]{:S(2)}, u32[]{:S(2)}) collective-permute-start(bf16[16,128]{1,0:T(8,128)(2,1)S(1)} %get-tuple-element.15.refs_0_), channel_id=1, source_target_pairs={{0,16},{8,24},{16,0},{24,8},{1,17},{9,25},{17,1},{25,9},{2,18},{10... | collective-permute-start | bytes 12296 | tf_op jit(solution)/shard_map/ppermute | solution.py:312
  33.3 4.5 %collective-permute-start.3 = (bf16[16,128]{1,0:T(8,128)(2,1)S(1)}, bf16[16,128]{1,0:T(8,128)(2,1)S(1)}, u32[]{:S(2)}, u32[]{:S(2)}) collective-permute-start(bf16[16,128]{1,0:T(8,128)(2,1)S(1)} %get-tuple-element.15.refs_0_), channel_id=1, source_target_pairs={{0,8},{8,0},{16,24},{24,16},{1,9},{9,1},{17,25},{25,17},{2,10},{10... | collective-permute-start | bytes 12296 | tf_op jit(solution)/shard_map/ppermute | solution.py:312

commit v5 on v4

--- a/solution.py
+++ b/solution.py
@@ -20,7 +20,6 @@
 by_row = (((1,), (1,)), ((), ()))
 in_vmem = pl.BlockSpec(memory_space=pltpu.VMEM)
 anywhere = pl.BlockSpec(memory_space=pl.ANY)
-in_smem = pl.BlockSpec(memory_space=pltpu.SMEM)
 
 
 def in_hbm(x):
@@ -59,12 +58,13 @@
 
 
 def table_kernel(
-    near_pairs, far_pairs_hbm, rank_hbm, far_out, near_out, far_pairs, rank_ref, sems, *, rank, own_clusters, src_count
+    near_hbm, far_hbm, rank_hbm, far_out, near_out, pick_out, near_pairs, far_pairs, rank_ref, sems, *,
+    rank, own_clusters, src_count, capacity,
 ):
-    copies = (
-        pltpu.make_async_copy(far_pairs_hbm, far_pairs, sems.at[0]),
-        pltpu.make_async_copy(rank_hbm, rank_ref, sems.at[1]),
-    )
+    copies = [
+        pltpu.make_async_copy(there, here, sems.at[k])
+        for k, (there, here) in enumerate(((near_hbm, near_pairs), (far_hbm, far_pairs), (rank_hbm, rank_ref)))
+    ]
     for copy in copies:
         copy.start()
     recv_index, src_index = lax.axis_index("recv"), lax.axis_index("src")
@@ -74,16 +74,49 @@
     def group_place(cluster):
         return ((cluster // group_rows) ^ recv_index) * own_clusters + cluster % own_clusters
 
-    tile_count = near_out.shape[0]
-    first_own = recv_index * group_rows + src_index * own_clusters
-    for t in range(tile_count):
-        target = near_pairs[0, src_index * tile_count + t] - first_own
-        source = near_pairs[1, src_index * tile_count + t]
-        place = (source // own_clusters) % src_count * source_rows + group_place(source)
-        near_out[t : t + 1, :] = jnp.full((1, lanes), target * code_base + place, jnp.int32)
-
     for copy in copies:
         copy.wait()
+    tile_count = near_out.shape[0]
+    padding = jnp.full((1, lanes - tile_count), -1, jnp.int32)
+
+    def by_device(row):
+        return jnp.concatenate(
+            [
+                jnp.concatenate([near_pairs[row : row + 1, k * tile_count : (k + 1) * tile_count], padding], 1)
+                for k in range(src_count)
+            ],
+            0,
+        )
+
+    target, source = by_device(0), by_device(1)
+    group = jnp.where(source < 0, -1, (source // own_clusters) % src_count)
+    place = jnp.where(source < 0, -1, group_place(source))
+    same = [group == g for g in range(src_count)]
+    before = lax.broadcasted_iota(jnp.int32, (lanes, lanes), 0) < lax.broadcasted_iota(jnp.int32, (lanes, lanes), 1)
+    counts = jnp.dot(
+        jnp.concatenate([jnp.where(here, 1.0, 0.0) for here in same], 0).astype(bf16),
+        jnp.where(before, 1.0, 0.0).astype(bf16),
+        preferred_element_type=f32,
+    )
+    slot = jnp.zeros(source.shape, f32)
+    for g, here in enumerate(same):
+        slot += jnp.where(here, counts[g * src_count : (g + 1) * src_count, :], 0.0)
+    slot = slot.astype(jnp.int32)
+    sent = jnp.where(group == src_index, slot, -1)
+    slot_ids = lax.broadcasted_iota(jnp.int32, (capacity, lanes), 0)
+    place_ids = lax.broadcasted_iota(jnp.int32, (source_rows, lanes), 0)
+    for k in range(src_count):
+        from_slot = jnp.where(slot_ids == sent[k : k + 1, :], 1.0, 0.0).astype(bf16)
+        from_place = jnp.where(place_ids == place[k : k + 1, :], 1.0, 0.0).astype(bf16)
+        pick_out[k * capacity : (k + 1) * capacity, :] = lax.dot_general(
+            from_slot, from_place, by_row, preferred_element_type=f32
+        ).astype(bf16)
+    first_own = recv_index * group_rows + src_index * own_clusters
+    code = (target - first_own) * code_base + group * capacity + slot
+    own = lax.broadcasted_iota(jnp.int32, code.shape, 0) == src_index
+    code = jnp.sum(jnp.where(own, code.astype(f32), 0.0), axis=0, keepdims=True)
+    near_out[...] = jnp.transpose(jnp.broadcast_to(code, (lanes, lanes))).astype(jnp.int32)[:tile_count, :]
+
     per_row = lanes // rank
     group = lanes // per_row
     shape = (group, lanes)
@@ -146,7 +179,7 @@
         step += body
 
 
-def far_kernel(code_ref, *refs):
+def far_kernel(code_ref, pick_ref, *refs):
     parts, (v_hbm, u_hbm, out_ref, v_buf, u_buf, sems, total_ref) = refs[:-7], refs[-7:]
     part = v_hbm.shape[0] // chunks
 
@@ -167,8 +200,10 @@
 
     deficit = jnp.concatenate([ref[...] for ref in parts], 0)
     count = parts[0].shape[0]
+    picked = jnp.dot(pick_ref[...], deficit, preferred_element_type=f32).astype(bf16)
+    capacity = out_ref.shape[1] - count
     for k in range(out_ref.shape[0]):
-        out_ref[k, count:, :] = deficit
+        out_ref[k, count:, :] = picked[k * capacity : (k + 1) * capacity, :]
     far_part(code_ref, deficit, v_buf, u_buf, total_ref, before)
     for k in range(out_ref.shape[0]):
         out_ref[k, :count, :] = total_ref[k * count : (k + 1) * count, :].astype(bf16)
@@ -288,21 +323,26 @@
         compiler_params=params,
     )(*[in_hbm(x) for x in arguments + [cluster_order.reshape(whole)]])
 
-    far_codes, near_codes = pl.pallas_call(
-        functools.partial(table_kernel, rank=rank, own_clusters=own_clusters, src_count=src_count),
-        in_specs=[in_smem, anywhere, anywhere],
-        out_specs=(in_vmem,) * 2,
+    capacity = -(-max(2, 2 * tile_count // src_count) // 16) * 16
+    far_codes, near_codes, picks = pl.pallas_call(
+        functools.partial(
+            table_kernel, rank=rank, own_clusters=own_clusters, src_count=src_count, capacity=capacity
+        ),
+        in_specs=[anywhere] * 3,
+        out_specs=(in_vmem,) * 3,
         out_shape=(
             jax.ShapeDtypeStruct((factor_rows // lanes, lanes), jnp.int32),
             jax.ShapeDtypeStruct((tile_count, lanes), jnp.int32),
+            jax.ShapeDtypeStruct((src_count * capacity, source_rows), bf16),
         ),
         scratch_shapes=[
+            pltpu.VMEM(near_pairs.shape, jnp.int32),
             pltpu.VMEM(far_pairs.shape, jnp.int32),
             pltpu.VMEM((far_count // lanes, lanes), jnp.int32),
-            pltpu.SemaphoreType.DMA((2,)),
+            pltpu.SemaphoreType.DMA((3,)),
         ],
         compiler_params=params,
-    )(near_pairs, in_hbm(far_pairs), in_hbm(far_ranks.reshape(far_count // lanes, lanes)))
+    )(*[in_hbm(x) for x in (near_pairs, far_pairs, far_ranks.reshape(far_count // lanes, lanes))])
 
     v_rows = in_hbm(far_v.reshape(factor_rows, lanes))
     u_rows = in_hbm(far_u.reshape(factor_rows, lanes))
@@ -314,9 +354,9 @@
         ]
         send = pl.pallas_call(
             far_kernel,
-            in_specs=[in_vmem] * (1 + recv_count) + [anywhere] * 2,
+            in_specs=[in_vmem] * (2 + recv_count) + [anywhere] * 2,
             out_specs=in_vmem,
-            out_shape=jax.ShapeDtypeStruct((src_count, own_clusters + source_rows, lanes), bf16),
+            out_shape=jax.ShapeDtypeStruct((src_count, own_clusters + capacity, lanes), bf16),
             scratch_shapes=[
                 pltpu.VMEM(v_rows.shape, bf16),
                 pltpu.VMEM(u_rows.shape, bf16),
@@ -327,7 +367,7 @@
             cost_estimate=pl.CostEstimate(
                 flops=2 * factor_rows * lanes * (source_rows + group_rows), bytes_accessed=2**24, transcendentals=0
             ),
-        )(far_codes, *parts, v_rows, u_rows)
+        )(far_codes, picks, *parts, v_rows, u_rows)
         return lax.all_to_all(send, "src", split_axis=0, concat_axis=0, tiled=True)
 
     first_stress, second_deficit = pl.pallas_call(

time: 57.1 us -> 54.1 us (0.947)
  Pallas kernels: 23.6 us -> 22.1 us
  blocking collectives: 17.7 us -> 16.3 us
  local copies, waits for them, and re-layouts: 0.69 us -> 0.01 us
    all_to_all x2, blocking collectives: 17.7 us -> 16.3 us  [exchange(): return lax.all_to_all(send, 'src', split_axis=0, concat_axis=0, tiled=True)]
    pallas_call x1, Pallas kernels: 2.42 us -> 1.15 us  [on_device(): pl.pallas_call(functools.partial(table_kernel, rank=rank, own_clusters=ow...]
    unnamed x4 -> x2, local copies, waits for them, and re-layouts: 0.69 us -> 0.01 us
  transfers between devices with their start and end apart: 6 -> 6, of which waited for: 3 -> 3; matrix products, arithmetic and copies ran while one was open for 0% -> 0% of each run, Pallas kernels for 4% -> 2%
where the time goes in v5:
time: 54.1 us; the launch traced here: 53.6 us
  Pallas kernels  22.1 us (41%)
  blocking collectives  16.3 us (30%)
  starting transfers between devices  10.2 us (19%)
  waiting for transfers between devices  4.32 us (8%)
  between operations  0.69 us (1%)
    all_to_all x2, blocking collectives, exchange(): return lax.all_to_all(send, 'src', split_axis=0, concat_axis=0, tiled=True)  16.3 us
    pallas_call x2, Pallas kernels, exchange(): pl.pallas_call(far_kernel, in_specs=[in_vmem] * (2 + recv_count) + [anywh...  16.2 us
    ppermute x6, starting transfers between devices, exchange(): lax.ppermute(deficit, 'recv', [(i, i ^ k) for i in range(recv_count)])  10.2 us
    ppermute x6, waiting for transfers between devices, exchange(): lax.ppermute(deficit, 'recv', [(i, i ^ k) for i in range(recv_count)])  4.32 us
    pallas_call x1, Pallas kernels, on_device(): pl.pallas_call(final_kernel, out_shape=(jax.ShapeDtypeStruct(whole, f32),...  2.55 us
    pallas_call x1, Pallas kernels, on_device(): pl.pallas_call(functools.partial(table_kernel, rank=rank, own_clusters=ow...  1.15 us
    pallas_call x1, Pallas kernels, on_device(): pl.pallas_call(order_kernel, in_specs=[anywhere] * 7, out_specs=(in_vmem,...  1.14 us
  transfers between devices with their start and end apart: 6, of which 3 were waited for; matrix products, arithmetic and copies ran while one was open for 0% of the time, Pallas kernels for 2%

profile of v5, /device:TPU:0, one launch (start us, length us, event | category | flops | bytes accessed | tf_op | source)
XLA Modules:
  0.0 53.6 jit_solution(7598447647771508027)
XLA Ops:
  0.6 1.1 %shard_map.141 = (f32[8,16,128]{2,1,0:T(8,128)S(1)}, bf16[16,128]{1,0:T(8,128)(2,1)S(1)}, s32[16,128]{1,0:T(8,128)S(1)}) custom-call(f32[16,128]{1,0:T(8,128)} %bitcast.16, f32[16,128]{1,0:T(8,128)} %bitcast.17, f32[16,128]{1,0:T(8,128)} %bitcast.18, f32[16,128]{1,0:T(8,128)} %bitcast.19, f32[16,128]{1,0:T(8,128)} %bitcast.20, f32[16,128]{1,0:T(8,128)} %bitcast.21, ...), custom_call_target="tpu_custom_call" | custom-call | tf_op jit(solution)/shard_map/pallas_call | solution.py:309
  1.8 5.1 %collective-permute-start.2 = (bf16[16,128]{1,0:T(8,128)(2,1)S(1)}, bf16[16,128]{1,0:T(8,128)(2,1)S(1)}, u32[]{:S(2)}, u32[]{:S(2)}) collective-permute-start(bf16[16,128]{1,0:T(8,128)(2,1)S(1)} %get-tuple-element.15.refs_0_), channel_id=1, source_target_pairs={{0,24},{8,16},{16,8},{24,0},{1,25},{9,17},{17,9},{25,1},{2,26},{10... | collective-permute-start | bytes 12296 | tf_op jit(solution)/shard_map/ppermute | solution.py:352
  6.9 0.0 collective-permute-start.1
  6.9 0.6 %collective-permute-start = (bf16[16,128]{1,0:T(8,128)(2,1)S(1)}, bf16[16,128]{1,0:T(8,128)(2,1)S(1)}, u32[]{:S(2)}, u32[]{:S(2)}) collective-permute-start(bf16[16,128]{1,0:T(8,128)(2,1)S(1)} %get-tuple-element.15.refs_0_), channel_id=1, source_target_pairs={{0,8},{8,0},{16,24},{24,16},{1,9},{9,1},{17,25},{25,17},{2,10},{10... | collective-permute-start | bytes 12296 | tf_op jit(solution)/shard_map/ppermute | solution.py:352
  7.5 1.1 %shard_map.140 = (s32[256,128]{1,0:T(8,128)S(1)}, s32[96,128]{1,0:T(8,128)S(1)}, bf16[256,64]{1,0:T(8,128)(2,1)S(1)}) custom-call(s32[2,768]{1,0:T(2,128)} %near_hbm.1, s32[2,1024]{1,0:T(2,128)} %far_hbm.1, s32[8,128]{1,0:T(8,128)} %bitcast.23), custom_call_target="tpu_custom_call" | custom-call | tf_op jit(solution)/shard_map/pallas_call | solution.py:327
  8.7 0.0 collective-permute-done.2.refs_3_
  8.7 2.7 %collective-permute-done.1.refs_2_ = bf16[16,128]{1,0:T(8,128)(2,1)S(1)} collective-permute-done((bf16[16,128]{1,0:T(8,128)(2,1)S(1)}, bf16[16,128]{1,0:T(8,128)(2,1)S(1)}, u32[]{:S(2)}, u32[]{:S(2)}) %collective-permute-start.1) | collective-permute-done | bytes 4128 | tf_op jit(solution)/shard_map/ppermute | solution.py:352
  11.4 0.0 collective-permute-done.refs_1_
  11.4 0.0 copy-start
  11.4 8.2 %shard_map.142 = bf16[8,48,128]{2,1,0:T(8,128)(2,1)S(1)} custom-call(s32[256,128]{1,0:T(8,128)S(1)} %get-tuple-element.13.code_ref, bf16[256,64]{1,0:T(8,128)(2,1)S(1)} %get-tuple-element.14.pick_ref, bf16[16,128]{1,0:T(8,128)(2,1)S(1)} %get-tuple-element.15.refs_0_, bf16[16,128]{1,0:T(8,128)(2,1)S(1)} %collective-permute-done.refs_1_, ...), custom_call_target="tpu_custom_call" | custom-call | flops 1610612736 | bytes 16777216 | tf_op jit(solution)/shard_map/pallas_call | solution.py:355
  19.6 8.7 %all_to_all.10.came_ref = bf16[8,48,128]{2,1,0:T(8,128)(2,1)S(1)} all-to-all(bf16[8,48,128]{2,1,0:T(8,128)(2,1)S(1)} %shard_map.142), channel_id=1, replica_groups=mesh['recv'=4,'src'=8] {'src'}, dimensions={0} | all-to-all | bytes 196608 | tf_op jit(solution)/shard_map/all_to_all | solution.py:371
  28.3 0.0 copy-done
  28.3 1.0 %shard_map.143 = (f32[16,128]{1,0:T(8,128)S(1)}, bf16[16,128]{1,0:T(8,128)(2,1)S(1)}) custom-call(s32[96,128]{1,0:T(8,128)S(1)} %get-tuple-element.12.code_ref, bf16[8,48,128]{2,1,0:T(8,128)(2,1)S(1)} %all_to_all.10.came_ref, bf16[96,128,128]{2,1,0:T(8,128)(2,1)S(1)} %copy-done, f32[8,16,128]{2,1,0:T(8,128)S(1)} %get-tuple-element.16.own_ref), custom_call_target="tpu_custom_call" | custom-call | tf_op jit(solution)/shard_map/pallas_call | solution.py:373
  29.4 1.5 %collective-permute-start.5 = (bf16[16,128]{1,0:T(8,128)(2,1)S(1)}, bf16[16,128]{1,0:T(8,128)(2,1)S(1)}, u32[]{:S(2)}, u32[]{:S(2)}) collective-permute-start(bf16[16,128]{1,0:T(8,128)(2,1)S(1)} %get-tuple-element.17.refs_0_), channel_id=1, source_target_pairs={{0,24},{8,16},{16,8},{24,0},{1,25},{9,17},{17,9},{25,1},{2,26},{10... | collective-permute-start | bytes 12296 | tf_op jit(solution)/shard_map/ppermute | solution.py:352
  30.9 0.6 %collective-permute-start.4 = (bf16[16,128]{1,0:T(8,128)(2,1)S(1)}, bf16[16,128]{1,0:T(8,128)(2,1)S(1)}, u32[]{:S(2)}, u32[]{:S(2)}) collective-permute-start(bf16[16,128]{1,0:T(8,128)(2,1)S(1)} %get-tuple-element.17.refs_0_), channel_id=1, source_target_pairs={{0,16},{8,24},{16,0},{24,8},{1,17},{9,25},{17,1},{25,9},{2,18},{10... | collective-permute-start | bytes 12296 | tf_op jit(solution)/shard_map/ppermute | solution.py:352
  31.5 2.3 %collective-permute-start.3 = (bf16[16,128]{1,0:T(8,128)(2,1)S(1)}, bf16[16,128]{1,0:T(8,128)(2,1)S(1)}, u32[]{:S(2)}, u32[]{:S(2)}) collective-permute-start(bf16[16,128]{1,0:T(8,128)(2,1)S(1)} %get-tuple-element.17.refs_0_), channel_id=1, source_target_pairs={{0,8},{8,0},{16,24},{24,16},{1,9},{9,1},{17,25},{25,17},{2,10},{10... | collective-permute-start | bytes 12296 | tf_op jit(solution)/shard_map/ppermute | solution.py:352
  33.8 1.0 %collective-permute-done.5.refs_3_ = bf16[16,128]{1,0:T(8,128)(2,1)S(1)} collective-permute-done((bf16[16,128]{1,0:T(8,128)(2,1)S(1)}, bf16[16,128]{1,0:T(8,128)(2,1)S(1)}, u32[]{:S(2)}, u32[]{:S(2)}) %collective-permute-start.5) | collective-permute-done | bytes 4128 | tf_op jit(solution)/shard_map/ppermute | solution.py:352
  34.8 0.6 %collective-permute-done.4.refs_2_ = bf16[16,128]{1,0:T(8,128)(2,1)S(1)} collective-permute-done((bf16[16,128]{1,0:T(8,128)(2,1)S(1)}, bf16[16,128]{1,0:T(8,128)(2,1)S(1)}, u32[]{:S(2)}, u32[]{:S(2)}) %collective-permute-start.4) | collective-permute-done | bytes 4128 | tf_op jit(solution)/shard_map/ppermute | solution.py:352
  35.4 0.0 collective-permute-done.3.refs_1_
  35.4 8.0 %shard_map.144 = bf16[8,48,128]{2,1,0:T(8,128)(2,1)S(1)} custom-call(s32[256,128]{1,0:T(8,128)S(1)} %get-tuple-element.13.code_ref, bf16[256,64]{1,0:T(8,128)(2,1)S(1)} %get-tuple-element.14.pick_ref, bf16[16,128]{1,0:T(8,128)(2,1)S(1)} %get-tuple-element.17.refs_0_, bf16[16,128]{1,0:T(8,128)(2,1)S(1)} %collective-permute-done.3.refs_1_, ...), custom_call_target="tpu_custom_call" | custom-call | flops 1610612736 | bytes 16777216 | tf_op jit(solution)/shard_map/pallas_call | solution.py:355
  43.5 7.6 %all_to_all.11.came_ref = bf16[8,48,128]{2,1,0:T(8,128)(2,1)S(1)} all-to-all(bf16[8,48,128]{2,1,0:T(8,128)(2,1)S(1)} %shard_map.144), channel_id=1, replica_groups=mesh['recv'=4,'src'=8] {'src'}, dimensions={0} | all-to-all | bytes 196608 | tf_op jit(solution)/shard_map/all_to_all | solution.py:371
  51.1 2.6 %shard_map.145 = (f32[16,128]{1,0:T(8,128)}, f32[16,128]{1,0:T(8,128)}) custom-call(s32[96,128]{1,0:T(8,128)S(1)} %get-tuple-element.12.code_ref, bf16[8,48,128]{2,1,0:T(8,128)(2,1)S(1)} %all_to_all.11.came_ref, bf16[96,128,128]{2,1,0:T(8,128)(2,1)S(1)} %copy-done, f32[8,16,128]{2,1,0:T(8,128)S(1)} %get-tuple-element.16.own_ref, ...), custom_call_target="tpu_custom_call" | custom-call | tf_op jit(solution)/shard_map/pallas_call | solution.py:380
Async XLA Ops:
  1.8 6.9 %collective-permute-start.2 = (bf16[16,128]{1,0:T(8,128)(2,1)S(1)}, bf16[16,128]{1,0:T(8,128)(2,1)S(1)}, u32[]{:S(2)}, u32[]{:S(2)}) collective-permute-start(bf16[16,128]{1,0:T(8,128)(2,1)S(1)} %get-tuple-element.15.refs_0_), channel_id=1, source_target_pairs={{0,24},{8,16},{16,8},{24,0},{1,25},{9,17},{17,9},{25,1},{2,26},{10... | collective-permute-start | bytes 12296 | tf_op jit(solution)/shard_map/ppermute | solution.py:352
  6.9 4.5 %collective-permute-start.1 = (bf16[16,128]{1,0:T(8,128)(2,1)S(1)}, bf16[16,128]{1,0:T(8,128)(2,1)S(1)}, u32[]{:S(2)}, u32[]{:S(2)}) collective-permute-start(bf16[16,128]{1,0:T(8,128)(2,1)S(1)} %get-tuple-element.15.refs_0_), channel_id=1, source_target_pairs={{0,16},{8,24},{16,0},{24,8},{1,17},{9,25},{17,1},{25,9},{2,18},{10... | collective-permute-start | bytes 12296 | tf_op jit(solution)/shard_map/ppermute | solution.py:352
  6.9 4.5 %collective-permute-start = (bf16[16,128]{1,0:T(8,128)(2,1)S(1)}, bf16[16,128]{1,0:T(8,128)(2,1)S(1)}, u32[]{:S(2)}, u32[]{:S(2)}) collective-permute-start(bf16[16,128]{1,0:T(8,128)(2,1)S(1)} %get-tuple-element.15.refs_0_), channel_id=1, source_target_pairs={{0,8},{8,0},{16,24},{24,16},{1,9},{9,1},{17,25},{25,17},{2,10},{10... | collective-permute-start | bytes 12296 | tf_op jit(solution)/shard_map/ppermute | solution.py:352
  11.4 16.9 %copy-start = (bf16[96,128,128]{2,1,0:T(8,128)(2,1)S(1)}, bf16[96,128,128]{2,1,0:T(8,128)(2,1)}, u32[]{:S(2)}) copy-start(bf16[96,128,128]{2,1,0:T(8,128)(2,1)} %tile_ref.3) | copy-start | bytes 9437188
  29.4 5.5 %collective-permute-start.5 = (bf16[16,128]{1,0:T(8,128)(2,1)S(1)}, bf16[16,128]{1,0:T(8,128)(2,1)S(1)}, u32[]{:S(2)}, u32[]{:S(2)}) collective-permute-start(bf16[16,128]{1,0:T(8,128)(2,1)S(1)} %get-tuple-element.17.refs_0_), channel_id=1, source_target_pairs={{0,24},{8,16},{16,8},{24,0},{1,25},{9,17},{17,9},{25,1},{2,26},{10... | collective-permute-start | bytes 12296 | tf_op jit(solution)/shard_map/ppermute | solution.py:352
  30.9 4.5 %collective-permute-start.4 = (bf16[16,128]{1,0:T(8,128)(2,1)S(1)}, bf16[16,128]{1,0:T(8,128)(2,1)S(1)}, u32[]{:S(2)}, u32[]{:S(2)}) collective-permute-start(bf16[16,128]{1,0:T(8,128)(2,1)S(1)} %get-tuple-element.17.refs_0_), channel_id=1, source_target_pairs={{0,16},{8,24},{16,0},{24,8},{1,17},{9,25},{17,1},{25,9},{2,18},{10... | collective-permute-start | bytes 12296 | tf_op jit(solution)/shard_map/ppermute | solution.py:352
  31.5 3.9 %collective-permute-start.3 = (bf16[16,128]{1,0:T(8,128)(2,1)S(1)}, bf16[16,128]{1,0:T(8,128)(2,1)S(1)}, u32[]{:S(2)}, u32[]{:S(2)}) collective-permute-start(bf16[16,128]{1,0:T(8,128)(2,1)S(1)} %get-tuple-element.17.refs_0_), channel_id=1, source_target_pairs={{0,8},{8,0},{16,24},{24,16},{1,9},{9,1},{17,25},{25,17},{2,10},{10... | collective-permute-start | bytes 12296 | tf_op jit(solution)/shard_map/ppermute | solution.py:352

commit v6 on v5

--- a/solution.py
+++ b/solution.py
@@ -57,8 +57,19 @@
     deficit_ref[...] = (plate - speed).astype(bf16)
 
 
+def head_copies(v_hbm, u_hbm, v_out, u_out, sems):
+    copies = [
+        pltpu.make_async_copy(there.at[: here.shape[0]], here, sems.at[k])
+        for k, (there, here) in enumerate(((v_hbm, v_out), (u_hbm, u_out)))
+    ]
+    for copy in copies:
+        copy.start()
+    return copies
+
+
 def table_kernel(
-    near_hbm, far_hbm, rank_hbm, far_out, near_out, pick_out, near_pairs, far_pairs, rank_ref, sems, *,
+    near_hbm, far_hbm, rank_hbm, v_hbm, u_hbm, far_out, near_out, pick_out, v_out, u_out,
+    near_pairs, far_pairs, rank_ref, sems, head_sems, *,
     rank, own_clusters, src_count, capacity,
 ):
     copies = [
@@ -67,6 +78,7 @@
     ]
     for copy in copies:
         copy.start()
+    heads = head_copies(v_hbm, u_hbm, v_out, u_out, head_sems)
     recv_index, src_index = lax.axis_index("recv"), lax.axis_index("src")
     group_rows = own_clusters * src_count
     source_rows = own_clusters * lax.axis_size("recv")
@@ -134,11 +146,12 @@
         far_out[a * group : (a + 1) * group, :] = jnp.where(
             lane % rank < spread(rank_ref[a : a + 1, :]), source, missing
         )
-
-
-def far_part(code_ref, deficit, v_buf, u_buf, out_ref, before):
-    factor_rows = v_buf.shape[0]
-    part = factor_rows // chunks
+    for copy in heads:
+        copy.wait()
+
+
+def far_part(code_ref, deficit, v_head, u_head, v_buf, u_buf, out_ref, before):
+    part = v_buf.shape[0] // chunks
     source_count = deficit.shape[0]
     target_count = out_ref.shape[0]
     source_ids = lax.broadcasted_iota(jnp.int32, (source_count, lanes), 0)
@@ -150,11 +163,13 @@
 
     step = 0
     for body in bodies:
-        for i in range(step, step + body):
-            before(i)
         base, count = step * part, body * part
+        v_ref, u_ref = (v_buf, u_buf) if step else (v_head, u_head)
+        if step:
+            for i in range(step, step + body):
+                before(i)
         products = lax.dot_general(
-            deficit, v_buf[base : base + count, :], by_row, preferred_element_type=f32
+            deficit, v_ref[base : base + count, :], by_row, preferred_element_type=f32
         )
         spread = []
         for k in range(count // lanes):
@@ -174,13 +189,13 @@
                 )
             )
         out_ref[...] += jnp.dot(
-            jnp.concatenate(spread, 1), u_buf[base : base + count, :], preferred_element_type=f32
+            jnp.concatenate(spread, 1), u_ref[base : base + count, :], preferred_element_type=f32
         )
         step += body
 
 
 def far_kernel(code_ref, pick_ref, *refs):
-    parts, (v_hbm, u_hbm, out_ref, v_buf, u_buf, sems, total_ref) = refs[:-7], refs[-7:]
+    parts, (v_head, u_head, v_hbm, u_hbm, out_ref, v_buf, u_buf, sems, total_ref) = refs[:-9], refs[-9:]
     part = v_hbm.shape[0] // chunks
 
     def copies(i):
@@ -190,7 +205,7 @@
             pltpu.make_async_copy(u_hbm.at[where], u_buf.at[where], sems.at[1, i]),
         )
 
-    for i in range(chunks):
+    for i in range(bodies[0], chunks):
         for copy in copies(i):
             copy.start()
 
@@ -204,7 +219,7 @@
     capacity = out_ref.shape[1] - count
     for k in range(out_ref.shape[0]):
         out_ref[k, count:, :] = picked[k * capacity : (k + 1) * capacity, :]
-    far_part(code_ref, deficit, v_buf, u_buf, total_ref, before)
+    far_part(code_ref, deficit, v_head, u_head, v_buf, u_buf, total_ref, before)
     for k in range(out_ref.shape[0]):
         out_ref[k, :count, :] = total_ref[k * count : (k + 1) * count, :].astype(bf16)
 
@@ -237,12 +252,17 @@
     return far + near
 
 
-def first_kernel(code_ref, came_ref, tile_ref, own_ref, stress_ref, deficit_ref):
+def first_kernel(
+    code_ref, came_ref, tile_ref, own_ref, v_hbm, u_hbm, stress_ref, deficit_ref, v_out, u_out, head_sems
+):
+    heads = head_copies(v_hbm, u_hbm, v_out, u_out, head_sems)
     stress = whole_stress(code_ref, came_ref, tile_ref, stress_ref.shape[0])
     stress_ref[...] = stress
     p, b, plate, theta_rate, gain = [own_ref[k] for k in (0, 3, 5, 6, 7)]
     speed = jnp.exp(p + time_step * ((stress - b * theta_rate) * gain))
     deficit_ref[...] = (plate - speed).astype(bf16)
+    for copy in heads:
+        copy.wait()
 
 
 def final_kernel(code_ref, came_ref, tile_ref, own_ref, first_ref, order_ref, p_out, q_out):
@@ -323,38 +343,41 @@
         compiler_params=params,
     )(*[in_hbm(x) for x in arguments + [cluster_order.reshape(whole)]])
 
+    v_rows = in_hbm(far_v.reshape(factor_rows, lanes))
+    u_rows = in_hbm(far_u.reshape(factor_rows, lanes))
+    head = jax.ShapeDtypeStruct((factor_rows // chunks * bodies[0], lanes), bf16)
     capacity = -(-max(2, 2 * tile_count // src_count) // 16) * 16
-    far_codes, near_codes, picks = pl.pallas_call(
+    far_codes, near_codes, picks, *first_heads = pl.pallas_call(
         functools.partial(
             table_kernel, rank=rank, own_clusters=own_clusters, src_count=src_count, capacity=capacity
         ),
-        in_specs=[anywhere] * 3,
-        out_specs=(in_vmem,) * 3,
+        in_specs=[anywhere] * 5,
+        out_specs=(in_vmem,) * 5,
         out_shape=(
             jax.ShapeDtypeStruct((factor_rows // lanes, lanes), jnp.int32),
             jax.ShapeDtypeStruct((tile_count, lanes), jnp.int32),
             jax.ShapeDtypeStruct((src_count * capacity, source_rows), bf16),
+            head,
+            head,
         ),
         scratch_shapes=[
             pltpu.VMEM(near_pairs.shape, jnp.int32),
             pltpu.VMEM(far_pairs.shape, jnp.int32),
             pltpu.VMEM((far_count // lanes, lanes), jnp.int32),
             pltpu.SemaphoreType.DMA((3,)),
+            pltpu.SemaphoreType.DMA((2,)),
         ],
         compiler_params=params,
-    )(*[in_hbm(x) for x in (near_pairs, far_pairs, far_ranks.reshape(far_count // lanes, lanes))])
-
-    v_rows = in_hbm(far_v.reshape(factor_rows, lanes))
-    u_rows = in_hbm(far_u.reshape(factor_rows, lanes))
-
-    def exchange(deficit):
+    )(*[in_hbm(x) for x in (near_pairs, far_pairs, far_ranks.reshape(far_count // lanes, lanes))], v_rows, u_rows)
+
+    def exchange(deficit, heads):
         parts = [deficit] + [
             lax.ppermute(deficit, "recv", [(i, i ^ k) for i in range(recv_count)])
             for k in range(1, recv_count)
         ]
         send = pl.pallas_call(
             far_kernel,
-            in_specs=[in_vmem] * (2 + recv_count) + [anywhere] * 2,
+            in_specs=[in_vmem] * (4 + recv_count) + [anywhere] * 2,
             out_specs=in_vmem,
             out_shape=jax.ShapeDtypeStruct((src_count, own_clusters + capacity, lanes), bf16),
             scratch_shapes=[
@@ -367,21 +390,22 @@
             cost_estimate=pl.CostEstimate(
                 flops=2 * factor_rows * lanes * (source_rows + group_rows), bytes_accessed=2**24, transcendentals=0
             ),
-        )(far_codes, picks, *parts, v_rows, u_rows)
+        )(far_codes, picks, *parts, *heads, v_rows, u_rows)
         return lax.all_to_all(send, "src", split_axis=0, concat_axis=0, tiled=True)
 
-    first_stress, second_deficit = pl.pallas_call(
+    first_stress, second_deficit, *second_heads = pl.pallas_call(
         first_kernel,
-        in_specs=[in_vmem] * 4,
-        out_specs=(in_vmem,) * 2,
-        out_shape=(jax.ShapeDtypeStruct(whole, f32), jax.ShapeDtypeStruct(whole, bf16)),
+        in_specs=[in_vmem] * 4 + [anywhere] * 2,
+        out_specs=(in_vmem,) * 4,
+        out_shape=(jax.ShapeDtypeStruct(whole, f32), jax.ShapeDtypeStruct(whole, bf16), head, head),
+        scratch_shapes=[pltpu.SemaphoreType.DMA((2,))],
         compiler_params=params,
-    )(near_codes, exchange(first_deficit), near_tiles, own)
+    )(near_codes, exchange(first_deficit, first_heads), near_tiles, own, v_rows, u_rows)
     new_p, new_q = pl.pallas_call(
         final_kernel,
         out_shape=(jax.ShapeDtypeStruct(whole, f32), jax.ShapeDtypeStruct(whole, f32)),
         compiler_params=params,
-    )(near_codes, exchange(second_deficit), near_tiles, own, first_stress, order)
+    )(near_codes, exchange(second_deficit, second_heads), near_tiles, own, first_stress, order)
     return new_p.reshape(-1), new_q.reshape(-1)
 
 

time: 54.1 us -> 53.4 us (0.987)
    pallas_call x3, Pallas kernels: 17.3 us -> 16.6 us  [the longest x2 15.1 us: exchange(): pl.pallas_call(far_kernel, in_specs=[in_vmem] * (4 + recv_count) + [anywh...]
  transfers between devices with their start and end apart: 6 -> 6, of which waited for: 3 -> 3; matrix products, arithmetic and copies ran while one was open for 0% -> 0% of each run, Pallas kernels for 2% -> 3%
where the time goes in v6:
time: 53.4 us; the launch traced here: 53.1 us
  Pallas kernels  22 us (41%)
  blocking collectives  16.3 us (31%)
  starting transfers between devices  10.2 us (19%)
  waiting for transfers between devices  3.91 us (7%)
  between operations  0.69 us (1%)
    all_to_all x2, blocking collectives, exchange(): return lax.all_to_all(send, 'src', split_axis=0, concat_axis=0, tiled=True)  16.3 us
    pallas_call x2, Pallas kernels, exchange(): pl.pallas_call(far_kernel, in_specs=[in_vmem] * (4 + recv_count) + [anywh...  15.1 us
    ppermute x6, starting transfers between devices, exchange(): lax.ppermute(deficit, 'recv', [(i, i ^ k) for i in range(recv_count)])  10.2 us
    ppermute x6, waiting for transfers between devices, exchange(): lax.ppermute(deficit, 'recv', [(i, i ^ k) for i in range(recv_count)])  3.91 us
    pallas_call x1, Pallas kernels, on_device(): pl.pallas_call(final_kernel, out_shape=(jax.ShapeDtypeStruct(whole, f32),...  2.55 us
    pallas_call x1, Pallas kernels, on_device(): pl.pallas_call(functools.partial(table_kernel, rank=rank, own_clusters=ow...  1.63 us
    pallas_call x1, Pallas kernels, on_device(): pl.pallas_call(first_kernel, in_specs=[in_vmem] * 4 + [anywhere] * 2, out...  1.56 us
    pallas_call x1, Pallas kernels, on_device(): pl.pallas_call(order_kernel, in_specs=[anywhere] * 7, out_specs=(in_vmem,...  1.14 us
  transfers between devices with their start and end apart: 6, of which 3 were waited for; matrix products, arithmetic and copies ran while one was open for 0% of the time, Pallas kernels for 3%

profile of v6, /device:TPU:0, one launch (start us, length us, event | category | flops | bytes accessed | tf_op | source)
XLA Modules:
  0.0 53.1 jit_solution(3260191974360814610)
XLA Ops:
  0.6 1.1 %shard_map.141 = (f32[8,16,128]{2,1,0:T(8,128)S(1)}, bf16[16,128]{1,0:T(8,128)(2,1)S(1)}, s32[16,128]{1,0:T(8,128)S(1)}) custom-call(f32[16,128]{1,0:T(8,128)} %bitcast.20, f32[16,128]{1,0:T(8,128)} %bitcast.21, f32[16,128]{1,0:T(8,128)} %bitcast.22, f32[16,128]{1,0:T(8,128)} %bitcast.23, f32[16,128]{1,0:T(8,128)} %bitcast.24, f32[16,128]{1,0:T(8,128)} %bitcast.25, ...), custom_call_target="tpu_custom_call" | custom-call | tf_op jit(solution)/shard_map/pallas_call | solution.py:329
  1.8 5.1 %collective-permute-start.2 = (bf16[16,128]{1,0:T(8,128)(2,1)S(1)}, bf16[16,128]{1,0:T(8,128)(2,1)S(1)}, u32[]{:S(2)}, u32[]{:S(2)}) collective-permute-start(bf16[16,128]{1,0:T(8,128)(2,1)S(1)} %get-tuple-element.19.refs_0_), channel_id=1, source_target_pairs={{0,24},{8,16},{16,8},{24,0},{1,25},{9,17},{17,9},{25,1},{2,26},{10... | collective-permute-start | bytes 12296 | tf_op jit(solution)/shard_map/ppermute | solution.py:375
  6.9 0.0 collective-permute-start.1
  6.9 0.6 %collective-permute-start = (bf16[16,128]{1,0:T(8,128)(2,1)S(1)}, bf16[16,128]{1,0:T(8,128)(2,1)S(1)}, u32[]{:S(2)}, u32[]{:S(2)}) collective-permute-start(bf16[16,128]{1,0:T(8,128)(2,1)S(1)} %get-tuple-element.19.refs_0_), channel_id=1, source_target_pairs={{0,8},{8,0},{16,24},{24,16},{1,9},{9,1},{17,25},{25,17},{2,10},{10... | collective-permute-start | bytes 12296 | tf_op jit(solution)/shard_map/ppermute | solution.py:375
  7.5 1.6 %shard_map.140 = (s32[256,128]{1,0:T(8,128)S(1)}, s32[96,128]{1,0:T(8,128)S(1)}, bf16[256,64]{1,0:T(8,128)(2,1)S(1)}, bf16[4096,128]{1,0:T(8,128)(2,1)S(1)}, bf16[4096,128]{1,0:T(8,128)(2,1)S(1)}) custom-call(s32[2,768]{1,0:T(2,128)} %near_hbm.1, s32[2,1024]{1,0:T(2,128)} %far_hbm.1, s32[8,128]{1,0:T(8,128)} %bitcast.27, bf16[32768,128]{1,0:T(8,128)(2,1)} %bitcast.12, ...), custom_call_target="tpu_custom_call" | custom-call | tf_op jit(solution)/shard_map/pallas_call | solution.py:350
  9.2 0.0 collective-permute-done.2.refs_3_
  9.2 2.2 %collective-permute-done.1.refs_2_ = bf16[16,128]{1,0:T(8,128)(2,1)S(1)} collective-permute-done((bf16[16,128]{1,0:T(8,128)(2,1)S(1)}, bf16[16,128]{1,0:T(8,128)(2,1)S(1)}, u32[]{:S(2)}, u32[]{:S(2)}) %collective-permute-start.1) | collective-permute-done | bytes 4128 | tf_op jit(solution)/shard_map/ppermute | solution.py:375
  11.4 0.0 collective-permute-done.refs_1_
  11.4 0.0 copy-start
  11.4 7.6 %shard_map.142 = bf16[8,48,128]{2,1,0:T(8,128)(2,1)S(1)} custom-call(s32[256,128]{1,0:T(8,128)S(1)} %get-tuple-element.17.code_ref, bf16[256,64]{1,0:T(8,128)(2,1)S(1)} %get-tuple-element.18.pick_ref, bf16[16,128]{1,0:T(8,128)(2,1)S(1)} %get-tuple-element.19.refs_0_, bf16[16,128]{1,0:T(8,128)(2,1)S(1)} %collective-permute-done.refs_1_, ...), custom_call_target="tpu_custom_call" | custom-call | flops 1610612736 | bytes 16777216 | tf_op jit(solution)/shard_map/pallas_call | solution.py:378
  19.0 8.7 %all_to_all.10.came_ref = bf16[8,48,128]{2,1,0:T(8,128)(2,1)S(1)} all-to-all(bf16[8,48,128]{2,1,0:T(8,128)(2,1)S(1)} %shard_map.142), channel_id=1, replica_groups=mesh['recv'=4,'src'=8] {'src'}, dimensions={0} | all-to-all | bytes 196608 | tf_op jit(solution)/shard_map/all_to_all | solution.py:394
  27.7 0.0 copy-done
  27.7 1.6 %shard_map.143 = (f32[16,128]{1,0:T(8,128)S(1)}, bf16[16,128]{1,0:T(8,128)(2,1)S(1)}, bf16[4096,128]{1,0:T(8,128)(2,1)S(1)}, bf16[4096,128]{1,0:T(8,128)(2,1)S(1)}) custom-call(s32[96,128]{1,0:T(8,128)S(1)} %get-tuple-element.16.code_ref, bf16[8,48,128]{2,1,0:T(8,128)(2,1)S(1)} %all_to_all.10.came_ref, bf16[96,128,128]{2,1,0:T(8,128)(2,1)S(1)} %copy-done, ...), custom_call_target="tpu_custom_call" | custom-call | tf_op jit(solution)/shard_map/pallas_call | solution.py:396
  29.3 1.6 %collective-permute-start.5 = (bf16[16,128]{1,0:T(8,128)(2,1)S(1)}, bf16[16,128]{1,0:T(8,128)(2,1)S(1)}, u32[]{:S(2)}, u32[]{:S(2)}) collective-permute-start(bf16[16,128]{1,0:T(8,128)(2,1)S(1)} %get-tuple-element.23.refs_0_), channel_id=1, source_target_pairs={{0,24},{8,16},{16,8},{24,0},{1,25},{9,17},{17,9},{25,1},{2,26},{10... | collective-permute-start | bytes 12296 | tf_op jit(solution)/shard_map/ppermute | solution.py:375
  30.9 0.5 collective-permute-start.4
  31.5 2.3 %collective-permute-start.3 = (bf16[16,128]{1,0:T(8,128)(2,1)S(1)}, bf16[16,128]{1,0:T(8,128)(2,1)S(1)}, u32[]{:S(2)}, u32[]{:S(2)}) collective-permute-start(bf16[16,128]{1,0:T(8,128)(2,1)S(1)} %get-tuple-element.23.refs_0_), channel_id=1, source_target_pairs={{0,8},{8,0},{16,24},{24,16},{1,9},{9,1},{17,25},{25,17},{2,10},{10... | collective-permute-start | bytes 12296 | tf_op jit(solution)/shard_map/ppermute | solution.py:375
  33.7 1.0 %collective-permute-done.5.refs_3_ = bf16[16,128]{1,0:T(8,128)(2,1)S(1)} collective-permute-done((bf16[16,128]{1,0:T(8,128)(2,1)S(1)}, bf16[16,128]{1,0:T(8,128)(2,1)S(1)}, u32[]{:S(2)}, u32[]{:S(2)}) %collective-permute-start.5) | collective-permute-done | bytes 4128 | tf_op jit(solution)/shard_map/ppermute | solution.py:375
  34.8 0.7 %collective-permute-done.4.refs_2_ = bf16[16,128]{1,0:T(8,128)(2,1)S(1)} collective-permute-done((bf16[16,128]{1,0:T(8,128)(2,1)S(1)}, bf16[16,128]{1,0:T(8,128)(2,1)S(1)}, u32[]{:S(2)}, u32[]{:S(2)}) %collective-permute-start.4) | collective-permute-done | bytes 4128 | tf_op jit(solution)/shard_map/ppermute | solution.py:375
  35.4 0.0 collective-permute-done.3.refs_1_
  35.4 7.5 %shard_map.144 = bf16[8,48,128]{2,1,0:T(8,128)(2,1)S(1)} custom-call(s32[256,128]{1,0:T(8,128)S(1)} %get-tuple-element.17.code_ref, bf16[256,64]{1,0:T(8,128)(2,1)S(1)} %get-tuple-element.18.pick_ref, bf16[16,128]{1,0:T(8,128)(2,1)S(1)} %get-tuple-element.23.refs_0_, bf16[16,128]{1,0:T(8,128)(2,1)S(1)} %collective-permute-done.3.refs_1_, ...), custom_call_target="tpu_custom_call" | custom-call | flops 1610612736 | bytes 16777216 | tf_op jit(solution)/shard_map/pallas_call | solution.py:378
  42.9 7.6 %all_to_all.11.came_ref = bf16[8,48,128]{2,1,0:T(8,128)(2,1)S(1)} all-to-all(bf16[8,48,128]{2,1,0:T(8,128)(2,1)S(1)} %shard_map.144), channel_id=1, replica_groups=mesh['recv'=4,'src'=8] {'src'}, dimensions={0} | all-to-all | bytes 196608 | tf_op jit(solution)/shard_map/all_to_all | solution.py:394
  50.5 2.6 %shard_map.145 = (f32[16,128]{1,0:T(8,128)}, f32[16,128]{1,0:T(8,128)}) custom-call(s32[96,128]{1,0:T(8,128)S(1)} %get-tuple-element.16.code_ref, bf16[8,48,128]{2,1,0:T(8,128)(2,1)S(1)} %all_to_all.11.came_ref, bf16[96,128,128]{2,1,0:T(8,128)(2,1)S(1)} %copy-done, f32[8,16,128]{2,1,0:T(8,128)S(1)} %get-tuple-element.22.own_ref, ...), custom_call_target="tpu_custom_call" | custom-call | tf_op jit(solution)/shard_map/pallas_call | solution.py:404
Async XLA Ops:
  1.8 7.4 %collective-permute-start.2 = (bf16[16,128]{1,0:T(8,128)(2,1)S(1)}, bf16[16,128]{1,0:T(8,128)(2,1)S(1)}, u32[]{:S(2)}, u32[]{:S(2)}) collective-permute-start(bf16[16,128]{1,0:T(8,128)(2,1)S(1)} %get-tuple-element.19.refs_0_), channel_id=1, source_target_pairs={{0,24},{8,16},{16,8},{24,0},{1,25},{9,17},{17,9},{25,1},{2,26},{10... | collective-permute-start | bytes 12296 | tf_op jit(solution)/shard_map/ppermute | solution.py:375
  6.9 4.5 %collective-permute-start.1 = (bf16[16,128]{1,0:T(8,128)(2,1)S(1)}, bf16[16,128]{1,0:T(8,128)(2,1)S(1)}, u32[]{:S(2)}, u32[]{:S(2)}) collective-permute-start(bf16[16,128]{1,0:T(8,128)(2,1)S(1)} %get-tuple-element.19.refs_0_), channel_id=1, source_target_pairs={{0,16},{8,24},{16,0},{24,8},{1,17},{9,25},{17,1},{25,9},{2,18},{10... | collective-permute-start | bytes 12296 | tf_op jit(solution)/shard_map/ppermute | solution.py:375
  6.9 4.5 %collective-permute-start = (bf16[16,128]{1,0:T(8,128)(2,1)S(1)}, bf16[16,128]{1,0:T(8,128)(2,1)S(1)}, u32[]{:S(2)}, u32[]{:S(2)}) collective-permute-start(bf16[16,128]{1,0:T(8,128)(2,1)S(1)} %get-tuple-element.19.refs_0_), channel_id=1, source_target_pairs={{0,8},{8,0},{16,24},{24,16},{1,9},{9,1},{17,25},{25,17},{2,10},{10... | collective-permute-start | bytes 12296 | tf_op jit(solution)/shard_map/ppermute | solution.py:375
  11.4 16.3 %copy-start = (bf16[96,128,128]{2,1,0:T(8,128)(2,1)S(1)}, bf16[96,128,128]{2,1,0:T(8,128)(2,1)}, u32[]{:S(2)}) copy-start(bf16[96,128,128]{2,1,0:T(8,128)(2,1)} %tile_ref.3) | copy-start | bytes 9437188
  29.3 5.5 %collective-permute-start.5 = (bf16[16,128]{1,0:T(8,128)(2,1)S(1)}, bf16[16,128]{1,0:T(8,128)(2,1)S(1)}, u32[]{:S(2)}, u32[]{:S(2)}) collective-permute-start(bf16[16,128]{1,0:T(8,128)(2,1)S(1)} %get-tuple-element.23.refs_0_), channel_id=1, source_target_pairs={{0,24},{8,16},{16,8},{24,0},{1,25},{9,17},{17,9},{25,1},{2,26},{10... | collective-permute-start | bytes 12296 | tf_op jit(solution)/shard_map/ppermute | solution.py:375
  30.9 4.5 %collective-permute-start.4 = (bf16[16,128]{1,0:T(8,128)(2,1)S(1)}, bf16[16,128]{1,0:T(8,128)(2,1)S(1)}, u32[]{:S(2)}, u32[]{:S(2)}) collective-permute-start(bf16[16,128]{1,0:T(8,128)(2,1)S(1)} %get-tuple-element.23.refs_0_), channel_id=1, source_target_pairs={{0,16},{8,24},{16,0},{24,8},{1,17},{9,25},{17,1},{25,9},{2,18},{10... | collective-permute-start | bytes 12296 | tf_op jit(solution)/shard_map/ppermute | solution.py:375
  31.5 4.0 %collective-permute-start.3 = (bf16[16,128]{1,0:T(8,128)(2,1)S(1)}, bf16[16,128]{1,0:T(8,128)(2,1)S(1)}, u32[]{:S(2)}, u32[]{:S(2)}) collective-permute-start(bf16[16,128]{1,0:T(8,128)(2,1)S(1)} %get-tuple-element.23.refs_0_), channel_id=1, source_target_pairs={{0,8},{8,0},{16,24},{24,16},{1,9},{9,1},{17,25},{25,17},{2,10},{10... | collective-permute-start | bytes 12296 | tf_op jit(solution)/shard_map/ppermute | solution.py:375

commit v7 on v6

--- a/solution.py
+++ b/solution.py
@@ -24,6 +24,16 @@
 
 def in_hbm(x):
     return pltpu.with_memory_space_constraint(x, pltpu.HBM)
+
+
+def gather_rows(arrays, row, lane):
+    out = [jnp.zeros(row.shape, f32)] * len(arrays)
+    for r in range(row.shape[0]):
+        here = row == r
+        for k, array in enumerate(arrays):
+            spread = jnp.broadcast_to(array[r : r + 1, :], row.shape)
+            out[k] = jnp.where(here, jnp.take_along_axis(spread, lane, axis=1), out[k])
+    return out
 
 
 def order_kernel(*refs):
@@ -40,15 +50,7 @@
     order = order_buf[...]
     order_out[...] = order
     row, lane = order // lanes, order % lanes
-    rows = order.shape[0]
-    sorted_values = [jnp.zeros(order.shape, f32)] * count
-    for r in range(rows):
-        here = row == r
-        for k in range(count):
-            spread = jnp.broadcast_to(buf[k, r : r + 1, :], order.shape)
-            got = jnp.take_along_axis(spread, lane, axis=1)
-            sorted_values[k] = jnp.where(here, got, sorted_values[k])
-    p, q, a, b, slip, plate = sorted_values
+    p, q, a, b, slip, plate = gather_rows([buf[k] for k in range(count)], row, lane)
     speed = jnp.exp(p)
     theta_rate = jnp.exp(-q) - speed / slip
     gain = 1.0 / (a + damping * speed)
@@ -252,50 +254,57 @@
     return far + near
 
 
-def first_kernel(
-    code_ref, came_ref, tile_ref, own_ref, v_hbm, u_hbm, stress_ref, deficit_ref, v_out, u_out, head_sems
-):
-    heads = head_copies(v_hbm, u_hbm, v_out, u_out, head_sems)
+def first_kernel(code_ref, came_ref, tile_ref, own_ref, stress_ref, deficit_ref):
     stress = whole_stress(code_ref, came_ref, tile_ref, stress_ref.shape[0])
     stress_ref[...] = stress
     p, b, plate, theta_rate, gain = [own_ref[k] for k in (0, 3, 5, 6, 7)]
     speed = jnp.exp(p + time_step * ((stress - b * theta_rate) * gain))
     deficit_ref[...] = (plate - speed).astype(bf16)
-    for copy in heads:
-        copy.wait()
-
-
-def final_kernel(code_ref, came_ref, tile_ref, own_ref, first_ref, order_ref, p_out, q_out):
-    stress = whole_stress(code_ref, came_ref, tile_ref, first_ref.shape[0])
+
+
+def ahead_kernel(own_ref, first_ref, order_ref, v_hbm, u_hbm, keep_ref, back_ref, q_out, v_out, u_out, head_sems):
+    heads = head_copies(v_hbm, u_hbm, v_out, u_out, head_sems)
+    order = order_ref[...]
+    rows = order.shape[0]
+    row, lane = order // lanes, order % lanes
+    row_ids = lax.broadcasted_iota(jnp.int32, (rows, lanes), 0)
+    position = lax.broadcasted_iota(jnp.int32, (rows, lanes), 1).astype(f32)
+    lane_ids = lax.broadcasted_iota(jnp.int32, (lanes, lanes), 0)
+    total = jnp.zeros((2 * rows, lanes), f32)
+    for r in range(rows):
+        here = row_ids == row[r : r + 1, :]
+        placed = jnp.concatenate([jnp.where(here, float(r), 0.0), jnp.where(here, position, 0.0)], 0)
+        spread = jnp.where(lane_ids == lane[r : r + 1, :], 1.0, 0.0).astype(bf16)
+        total += lax.dot_general(placed.astype(bf16), spread, by_row, preferred_element_type=f32)
+    back_row, back_lane = total[:rows].astype(jnp.int32), total[rows:].astype(jnp.int32)
+    back_ref[0] = back_row
+    back_ref[1] = back_lane
+
     p, q, a, b, slip, plate, theta_rate, gain = [own_ref[k] for k in range(8)]
     first_p = (first_ref[...] - b * theta_rate) * gain
     speed = jnp.exp(p + time_step * first_p)
     second_q = jnp.exp(-(q + time_step * theta_rate)) - speed / slip
-    second_p = (stress - b * second_q) / (a + damping * speed)
-    new_p = p + 0.5 * time_step * (first_p + second_p)
-    new_q = q + 0.5 * time_step * (theta_rate + second_q)
-    pieces = []
-    for value in (new_p, new_q):
-        for _ in range(3):
-            piece = value.astype(bf16).astype(f32)
-            value = value - piece
-            pieces.append(piece)
-    rows = p.shape[0]
-    order = order_ref[...]
-    row, lane = order // lanes, order % lanes
-    row_ids = lax.broadcasted_iota(jnp.int32, (rows, lanes), 0)
-    lane_ids = lax.broadcasted_iota(jnp.int32, (lanes, lanes), 0)
-    total = jnp.zeros((len(pieces) * rows, lanes), f32)
-    for r in range(rows):
-        here = row_ids == row[r : r + 1, :]
-        placed = jnp.concatenate(
-            [jnp.where(here, piece[r : r + 1, :], 0.0) for piece in pieces], 0
-        ).astype(bf16)
-        spread = jnp.where(lane_ids == lane[r : r + 1, :], 1.0, 0.0).astype(bf16)
-        total += lax.dot_general(placed, spread, by_row, preferred_element_type=f32)
-    for k, out in enumerate((p_out, q_out)):
-        high, mid, low = [total[(3 * k + j) * rows : (3 * k + j + 1) * rows, :] for j in range(3)]
-        out[...] = (low + mid) + high
+    second_gain = 0.5 * time_step / (a + damping * speed)
+    new_q, offset, factor = gather_rows(
+        (
+            q + 0.5 * time_step * (theta_rate + second_q),
+            p + 0.5 * time_step * first_p - b * second_q * second_gain,
+            second_gain,
+        ),
+        back_row,
+        back_lane,
+    )
+    q_out[...] = new_q
+    keep_ref[0] = offset
+    keep_ref[1] = factor
+    for copy in heads:
+        copy.wait()
+
+
+def final_kernel(code_ref, came_ref, tile_ref, keep_ref, back_ref, p_out):
+    stress = whole_stress(code_ref, came_ref, tile_ref, p_out.shape[0])
+    (stress,) = gather_rows((stress,), back_ref[0], back_ref[1])
+    p_out[...] = keep_ref[0] + keep_ref[1] * stress
 
 
 def on_device(
@@ -393,19 +402,35 @@
         )(far_codes, picks, *parts, *heads, v_rows, u_rows)
         return lax.all_to_all(send, "src", split_axis=0, concat_axis=0, tiled=True)
 
-    first_stress, second_deficit, *second_heads = pl.pallas_call(
+    state = jax.ShapeDtypeStruct(whole, f32)
+    first_stress, second_deficit = pl.pallas_call(
         first_kernel,
-        in_specs=[in_vmem] * 4 + [anywhere] * 2,
-        out_specs=(in_vmem,) * 4,
-        out_shape=(jax.ShapeDtypeStruct(whole, f32), jax.ShapeDtypeStruct(whole, bf16), head, head),
+        in_specs=[in_vmem] * 4,
+        out_specs=(in_vmem,) * 2,
+        out_shape=(state, jax.ShapeDtypeStruct(whole, bf16)),
+        compiler_params=params,
+    )(near_codes, exchange(first_deficit, first_heads), near_tiles, own)
+    keep, back, new_q, *second_heads = pl.pallas_call(
+        ahead_kernel,
+        in_specs=[in_vmem] * 3 + [anywhere] * 2,
+        out_specs=(in_vmem,) * 5,
+        out_shape=(
+            jax.ShapeDtypeStruct((2,) + whole, f32),
+            jax.ShapeDtypeStruct((2,) + whole, jnp.int32),
+            state,
+            head,
+            head,
+        ),
         scratch_shapes=[pltpu.SemaphoreType.DMA((2,))],
         compiler_params=params,
-    )(near_codes, exchange(first_deficit, first_heads), near_tiles, own, v_rows, u_rows)
-    new_p, new_q = pl.pallas_call(
+    )(own, first_stress, order, v_rows, u_rows)
+    new_p = pl.pallas_call(
         final_kernel,
-        out_shape=(jax.ShapeDtypeStruct(whole, f32), jax.ShapeDtypeStruct(whole, f32)),
+        in_specs=[in_vmem] * 5,
+        out_specs=in_vmem,
+        out_shape=state,
         compiler_params=params,
-    )(near_codes, exchange(second_deficit, second_heads), near_tiles, own, first_stress, order)
+    )(near_codes, exchange(second_deficit, second_heads), near_tiles, keep, back)
     return new_p.reshape(-1), new_q.reshape(-1)
 
 

time: 53.4 us -> 52.6 us (0.985)
  waiting for transfers between devices: 3.91 us -> 2.23 us
  Pallas kernels: 22 us -> 22.8 us
    ppermute x6, waiting for transfers between devices: 3.91 us -> 2.23 us  [exchange(): lax.ppermute(deficit, 'recv', [(i, i ^ k) for i in range(recv_count)])]
    pallas_call x2 -> x3, Pallas kernels: 4.11 us -> 4.94 us  [the longest x1 2.16 us: on_device(): pl.pallas_call(ahead_kernel, in_specs=[in_vmem] * 3 + [anywhere] * 2, out...]
  transfers between devices with their start and end apart: 6 -> 6, of which waited for: 3 -> 1; matrix products, arithmetic and copies ran while one was open for 0% -> 0% of each run, Pallas kernels for 3% -> 7%
where the time goes in v7:
time: 52.6 us; the launch traced here: 52.2 us
  Pallas kernels  22.8 us (43%)
  blocking collectives  16.3 us (31%)
  starting transfers between devices  10.2 us (19%)
  waiting for transfers between devices  2.23 us (4%)
  between operations  0.72 us (1%)
    all_to_all x2, blocking collectives, exchange(): return lax.all_to_all(send, 'src', split_axis=0, concat_axis=0, tiled=True)  16.3 us
    pallas_call x2, Pallas kernels, exchange(): pl.pallas_call(far_kernel, in_specs=[in_vmem] * (4 + recv_count) + [anywh...  15.1 us
    ppermute x6, starting transfers between devices, exchange(): lax.ppermute(deficit, 'recv', [(i, i ^ k) for i in range(recv_count)])  10.2 us
    ppermute x6, waiting for transfers between devices, exchange(): lax.ppermute(deficit, 'recv', [(i, i ^ k) for i in range(recv_count)])  2.23 us
    pallas_call x1, Pallas kernels, on_device(): pl.pallas_call(ahead_kernel, in_specs=[in_vmem] * 3 + [anywhere] * 2, out...  2.16 us
    pallas_call x1, Pallas kernels, on_device(): pl.pallas_call(final_kernel, in_specs=[in_vmem] * 5, out_specs=in_vmem, o...  1.74 us
    pallas_call x1, Pallas kernels, on_device(): pl.pallas_call(functools.partial(table_kernel, rank=rank, own_clusters=ow...  1.63 us
    pallas_call x1, Pallas kernels, on_device(): pl.pallas_call(order_kernel, in_specs=[anywhere] * 7, out_specs=(in_vmem,...  1.14 us
  transfers between devices with their start and end apart: 6, of which 1 were waited for; matrix products, arithmetic and copies ran while one was open for 0% of the time, Pallas kernels for 7%

profile of v7, /device:TPU:0, one launch (start us, length us, event | category | flops | bytes accessed | tf_op | source)
XLA Modules:
  0.0 52.2 jit_solution(1704614180897117236)
XLA Ops:
  0.6 1.1 %shard_map.141 = (f32[8,16,128]{2,1,0:T(8,128)S(1)}, bf16[16,128]{1,0:T(8,128)(2,1)S(1)}, s32[16,128]{1,0:T(8,128)S(1)}) custom-call(f32[16,128]{1,0:T(8,128)} %bitcast.21, f32[16,128]{1,0:T(8,128)} %bitcast.22, f32[16,128]{1,0:T(8,128)} %bitcast.23, f32[16,128]{1,0:T(8,128)} %bitcast.24, f32[16,128]{1,0:T(8,128)} %bitcast.25, f32[16,128]{1,0:T(8,128)} %bitcast.26, ...), custom_call_target="tpu_custom_call" | custom-call | tf_op jit(solution)/shard_map/pallas_call | solution.py:338
  1.8 5.1 %collective-permute-start.2 = (bf16[16,128]{1,0:T(8,128)(2,1)S(1)}, bf16[16,128]{1,0:T(8,128)(2,1)S(1)}, u32[]{:S(2)}, u32[]{:S(2)}) collective-permute-start(bf16[16,128]{1,0:T(8,128)(2,1)S(1)} %get-tuple-element.20.refs_0_), channel_id=1, source_target_pairs={{0,24},{8,16},{16,8},{24,0},{1,25},{9,17},{17,9},{25,1},{2,26},{10... | collective-permute-start | bytes 12296 | tf_op jit(solution)/shard_map/ppermute | solution.py:384
  6.9 0.0 collective-permute-start.1
  6.9 0.6 %collective-permute-start = (bf16[16,128]{1,0:T(8,128)(2,1)S(1)}, bf16[16,128]{1,0:T(8,128)(2,1)S(1)}, u32[]{:S(2)}, u32[]{:S(2)}) collective-permute-start(bf16[16,128]{1,0:T(8,128)(2,1)S(1)} %get-tuple-element.20.refs_0_), channel_id=1, source_target_pairs={{0,8},{8,0},{16,24},{24,16},{1,9},{9,1},{17,25},{25,17},{2,10},{10... | collective-permute-start | bytes 12296 | tf_op jit(solution)/shard_map/ppermute | solution.py:384
  7.5 1.6 %shard_map.140 = (s32[256,128]{1,0:T(8,128)S(1)}, s32[96,128]{1,0:T(8,128)S(1)}, bf16[256,64]{1,0:T(8,128)(2,1)S(1)}, bf16[4096,128]{1,0:T(8,128)(2,1)S(1)}, bf16[4096,128]{1,0:T(8,128)(2,1)S(1)}) custom-call(s32[2,768]{1,0:T(2,128)} %near_hbm.1, s32[2,1024]{1,0:T(2,128)} %far_hbm.1, s32[8,128]{1,0:T(8,128)} %bitcast.28, bf16[32768,128]{1,0:T(8,128)(2,1)} %bitcast.12, ...), custom_call_target="tpu_custom_call" | custom-call | tf_op jit(solution)/shard_map/pallas_call | solution.py:359
  9.2 0.0 collective-permute-done.2.refs_3_
  9.2 2.2 %collective-permute-done.1.refs_2_ = bf16[16,128]{1,0:T(8,128)(2,1)S(1)} collective-permute-done((bf16[16,128]{1,0:T(8,128)(2,1)S(1)}, bf16[16,128]{1,0:T(8,128)(2,1)S(1)}, u32[]{:S(2)}, u32[]{:S(2)}) %collective-permute-start.1) | collective-permute-done | bytes 4128 | tf_op jit(solution)/shard_map/ppermute | solution.py:384
  11.4 0.0 collective-permute-done.refs_1_
  11.4 0.0 copy-start
  11.4 7.6 %shard_map.142 = bf16[8,48,128]{2,1,0:T(8,128)(2,1)S(1)} custom-call(s32[256,128]{1,0:T(8,128)S(1)} %get-tuple-element.18.code_ref, bf16[256,64]{1,0:T(8,128)(2,1)S(1)} %get-tuple-element.19.pick_ref, bf16[16,128]{1,0:T(8,128)(2,1)S(1)} %get-tuple-element.20.refs_0_, bf16[16,128]{1,0:T(8,128)(2,1)S(1)} %collective-permute-done.refs_1_, ...), custom_call_target="tpu_custom_call" | custom-call | flops 1610612736 | bytes 16777216 | tf_op jit(solution)/shard_map/pallas_call | solution.py:387
  19.0 8.7 %all_to_all.10.came_ref = bf16[8,48,128]{2,1,0:T(8,128)(2,1)S(1)} all-to-all(bf16[8,48,128]{2,1,0:T(8,128)(2,1)S(1)} %shard_map.142), channel_id=1, replica_groups=mesh['recv'=4,'src'=8] {'src'}, dimensions={0} | all-to-all | bytes 196608 | tf_op jit(solution)/shard_map/all_to_all | solution.py:403
  27.7 0.0 copy-done
  27.7 1.0 %shard_map.143 = (f32[16,128]{1,0:T(8,128)S(1)}, bf16[16,128]{1,0:T(8,128)(2,1)S(1)}) custom-call(s32[96,128]{1,0:T(8,128)S(1)} %get-tuple-element.17.code_ref, bf16[8,48,128]{2,1,0:T(8,128)(2,1)S(1)} %all_to_all.10.came_ref, bf16[96,128,128]{2,1,0:T(8,128)(2,1)S(1)} %copy-done, f32[8,16,128]{2,1,0:T(8,128)S(1)} %get-tuple-element.23.own_ref), custom_call_target="tpu_custom_call" | custom-call | tf_op jit(solution)/shard_map/pallas_call | solution.py:406
  28.8 1.6 %collective-permute-start.5 = (bf16[16,128]{1,0:T(8,128)(2,1)S(1)}, bf16[16,128]{1,0:T(8,128)(2,1)S(1)}, u32[]{:S(2)}, u32[]{:S(2)}) collective-permute-start(bf16[16,128]{1,0:T(8,128)(2,1)S(1)} %get-tuple-element.24.refs_0_), channel_id=1, source_target_pairs={{0,24},{8,16},{16,8},{24,0},{1,25},{9,17},{17,9},{25,1},{2,26},{10... | collective-permute-start | bytes 12296 | tf_op jit(solution)/shard_map/ppermute | solution.py:384
  30.4 0.6 %collective-permute-start.4 = (bf16[16,128]{1,0:T(8,128)(2,1)S(1)}, bf16[16,128]{1,0:T(8,128)(2,1)S(1)}, u32[]{:S(2)}, u32[]{:S(2)}) collective-permute-start(bf16[16,128]{1,0:T(8,128)(2,1)S(1)} %get-tuple-element.24.refs_0_), channel_id=1, source_target_pairs={{0,16},{8,24},{16,0},{24,8},{1,17},{9,25},{17,1},{25,9},{2,18},{10... | collective-permute-start | bytes 12296 | tf_op jit(solution)/shard_map/ppermute | solution.py:384
  30.9 2.3 %collective-permute-start.3 = (bf16[16,128]{1,0:T(8,128)(2,1)S(1)}, bf16[16,128]{1,0:T(8,128)(2,1)S(1)}, u32[]{:S(2)}, u32[]{:S(2)}) collective-permute-start(bf16[16,128]{1,0:T(8,128)(2,1)S(1)} %get-tuple-element.24.refs_0_), channel_id=1, source_target_pairs={{0,8},{8,0},{16,24},{24,16},{1,9},{9,1},{17,25},{25,17},{2,10},{10... | collective-permute-start | bytes 12296 | tf_op jit(solution)/shard_map/ppermute | solution.py:384
  33.2 2.2 %shard_map.144 = (f32[2,16,128]{2,1,0:T(8,128)S(1)}, s32[2,16,128]{2,1,0:T(8,128)S(1)}, f32[16,128]{1,0:T(8,128)}, bf16[4096,128]{1,0:T(8,128)(2,1)S(1)}, bf16[4096,128]{1,0:T(8,128)(2,1)S(1)}) custom-call(f32[8,16,128]{2,1,0:T(8,128)S(1)} %get-tuple-element.23.own_ref, f32[16,128]{1,0:T(8,128)S(1)} %get-tuple-element.25.first_ref, ...), custom_call_target="tpu_custom_call" | custom-call | tf_op jit(solution)/shard_map/pallas_call | solution.py:413
  35.4 0.0 collective-permute-done.5.refs_3_
  35.4 0.0 collective-permute-done.4.refs_2_
  35.4 0.0 collective-permute-done.3.refs_1_
  35.4 7.5 %shard_map.145 = bf16[8,48,128]{2,1,0:T(8,128)(2,1)S(1)} custom-call(s32[256,128]{1,0:T(8,128)S(1)} %get-tuple-element.18.code_ref, bf16[256,64]{1,0:T(8,128)(2,1)S(1)} %get-tuple-element.19.pick_ref, bf16[16,128]{1,0:T(8,128)(2,1)S(1)} %get-tuple-element.24.refs_0_, bf16[16,128]{1,0:T(8,128)(2,1)S(1)} %collective-permute-done.3.refs_1_, ...), custom_call_target="tpu_custom_call" | custom-call | flops 1610612736 | bytes 16777216 | tf_op jit(solution)/shard_map/pallas_call | solution.py:387
  42.9 7.6 %all_to_all.11.came_ref = bf16[8,48,128]{2,1,0:T(8,128)(2,1)S(1)} all-to-all(bf16[8,48,128]{2,1,0:T(8,128)(2,1)S(1)} %shard_map.145), channel_id=1, replica_groups=mesh['recv'=4,'src'=8] {'src'}, dimensions={0} | all-to-all | bytes 196608 | tf_op jit(solution)/shard_map/all_to_all | solution.py:403
  50.5 1.7 %shard_map.146 = f32[16,128]{1,0:T(8,128)} custom-call(s32[96,128]{1,0:T(8,128)S(1)} %get-tuple-element.17.code_ref, bf16[8,48,128]{2,1,0:T(8,128)(2,1)S(1)} %all_to_all.11.came_ref, bf16[96,128,128]{2,1,0:T(8,128)(2,1)S(1)} %copy-done, f32[2,16,128]{2,1,0:T(8,128)S(1)} %get-tuple-element.29.keep_ref, s32[2,16,128]{2,1,0:T(8,128)S(1)} %get-tuple-element.30.back_ref), custom_call_target="tpu_custom_call" | custom-call | tf_op jit(solution)/shard_map/pallas_call | solution.py:427
Async XLA Ops:
  1.8 7.4 %collective-permute-start.2 = (bf16[16,128]{1,0:T(8,128)(2,1)S(1)}, bf16[16,128]{1,0:T(8,128)(2,1)S(1)}, u32[]{:S(2)}, u32[]{:S(2)}) collective-permute-start(bf16[16,128]{1,0:T(8,128)(2,1)S(1)} %get-tuple-element.20.refs_0_), channel_id=1, source_target_pairs={{0,24},{8,16},{16,8},{24,0},{1,25},{9,17},{17,9},{25,1},{2,26},{10... | collective-permute-start | bytes 12296 | tf_op jit(solution)/shard_map/ppermute | solution.py:384
  6.9 4.5 %collective-permute-start.1 = (bf16[16,128]{1,0:T(8,128)(2,1)S(1)}, bf16[16,128]{1,0:T(8,128)(2,1)S(1)}, u32[]{:S(2)}, u32[]{:S(2)}) collective-permute-start(bf16[16,128]{1,0:T(8,128)(2,1)S(1)} %get-tuple-element.20.refs_0_), channel_id=1, source_target_pairs={{0,16},{8,24},{16,0},{24,8},{1,17},{9,25},{17,1},{25,9},{2,18},{10... | collective-permute-start | bytes 12296 | tf_op jit(solution)/shard_map/ppermute | solution.py:384
  6.9 4.5 %collective-permute-start = (bf16[16,128]{1,0:T(8,128)(2,1)S(1)}, bf16[16,128]{1,0:T(8,128)(2,1)S(1)}, u32[]{:S(2)}, u32[]{:S(2)}) collective-permute-start(bf16[16,128]{1,0:T(8,128)(2,1)S(1)} %get-tuple-element.20.refs_0_), channel_id=1, source_target_pairs={{0,8},{8,0},{16,24},{24,16},{1,9},{9,1},{17,25},{25,17},{2,10},{10... | collective-permute-start | bytes 12296 | tf_op jit(solution)/shard_map/ppermute | solution.py:384
  11.4 16.3 %copy-start = (bf16[96,128,128]{2,1,0:T(8,128)(2,1)S(1)}, bf16[96,128,128]{2,1,0:T(8,128)(2,1)}, u32[]{:S(2)}) copy-start(bf16[96,128,128]{2,1,0:T(8,128)(2,1)} %tile_ref.3) | copy-start | bytes 9437188
  28.8 6.6 %collective-permute-start.5 = (bf16[16,128]{1,0:T(8,128)(2,1)S(1)}, bf16[16,128]{1,0:T(8,128)(2,1)S(1)}, u32[]{:S(2)}, u32[]{:S(2)}) collective-permute-start(bf16[16,128]{1,0:T(8,128)(2,1)S(1)} %get-tuple-element.24.refs_0_), channel_id=1, source_target_pairs={{0,24},{8,16},{16,8},{24,0},{1,25},{9,17},{17,9},{25,1},{2,26},{10... | collective-permute-start | bytes 12296 | tf_op jit(solution)/shard_map/ppermute | solution.py:384
  30.4 5.0 %collective-permute-start.4 = (bf16[16,128]{1,0:T(8,128)(2,1)S(1)}, bf16[16,128]{1,0:T(8,128)(2,1)S(1)}, u32[]{:S(2)}, u32[]{:S(2)}) collective-permute-start(bf16[16,128]{1,0:T(8,128)(2,1)S(1)} %get-tuple-element.24.refs_0_), channel_id=1, source_target_pairs={{0,16},{8,24},{16,0},{24,8},{1,17},{9,25},{17,1},{25,9},{2,18},{10... | collective-permute-start | bytes 12296 | tf_op jit(solution)/shard_map/ppermute | solution.py:384
  30.9 4.5 %collective-permute-start.3 = (bf16[16,128]{1,0:T(8,128)(2,1)S(1)}, bf16[16,128]{1,0:T(8,128)(2,1)S(1)}, u32[]{:S(2)}, u32[]{:S(2)}) collective-permute-start(bf16[16,128]{1,0:T(8,128)(2,1)S(1)} %get-tuple-element.24.refs_0_), channel_id=1, source_target_pairs={{0,8},{8,0},{16,24},{24,16},{1,9},{9,1},{17,25},{25,17},{2,10},{10... | collective-permute-start | bytes 12296 | tf_op jit(solution)/shard_map/ppermute | solution.py:384

commit v8 on v7

--- a/solution.py
+++ b/solution.py
@@ -14,9 +14,9 @@
 lanes = 128
 chunks = 8
 code_base = 4096
-vmem_bytes = 8 * 2**20
-far_vmem_bytes = 28 * 2**20
-bodies = (1, 2, 2, 2, 1)
+vmem_bytes = 16 * 2**20
+far_vmem_bytes = 40 * 2**20
+bodies = (3, 2, 2, 1)
 by_row = (((1,), (1,)), ((), ()))
 in_vmem = pl.BlockSpec(memory_space=pltpu.VMEM)
 anywhere = pl.BlockSpec(memory_space=pl.ANY)
@@ -270,12 +270,14 @@
     row_ids = lax.broadcasted_iota(jnp.int32, (rows, lanes), 0)
     position = lax.broadcasted_iota(jnp.int32, (rows, lanes), 1).astype(f32)
     lane_ids = lax.broadcasted_iota(jnp.int32, (lanes, lanes), 0)
-    total = jnp.zeros((2 * rows, lanes), f32)
+    placed, spread = [], []
     for r in range(rows):
         here = row_ids == row[r : r + 1, :]
-        placed = jnp.concatenate([jnp.where(here, float(r), 0.0), jnp.where(here, position, 0.0)], 0)
-        spread = jnp.where(lane_ids == lane[r : r + 1, :], 1.0, 0.0).astype(bf16)
-        total += lax.dot_general(placed.astype(bf16), spread, by_row, preferred_element_type=f32)
+        placed.append(jnp.concatenate([jnp.where(here, float(r), 0.0), jnp.where(here, position, 0.0)], 0).astype(bf16))
+        spread.append(jnp.where(lane_ids == lane[r : r + 1, :], 1.0, 0.0).astype(bf16))
+    total = lax.dot_general(
+        jnp.concatenate(placed, 1), jnp.concatenate(spread, 1), by_row, preferred_element_type=f32
+    )
     back_row, back_lane = total[:rows].astype(jnp.int32), total[rows:].astype(jnp.int32)
     back_ref[0] = back_row
     back_ref[1] = back_lane

time: 52.6 us -> 51.4 us (0.977)
  waiting for transfers between devices: 2.23 us -> 0.93 us
    pallas_call x2, Pallas kernels: 15.1 us -> 12.5 us  [exchange(): pl.pallas_call(far_kernel, in_specs=[in_vmem] * (4 + recv_count) + [anywh...]
    pallas_call x1, Pallas kernels: 2.16 us -> 3.46 us  [on_device(): pl.pallas_call(ahead_kernel, in_specs=[in_vmem] * 3 + [anywhere] * 2, out...]
    ppermute x6, waiting for transfers between devices: 2.23 us -> 0.93 us  [exchange(): lax.ppermute(deficit, 'recv', [(i, i ^ k) for i in range(recv_count)])]
    pallas_call x1, Pallas kernels: 1.63 us -> 2.93 us  [on_device(): pl.pallas_call(functools.partial(table_kernel, rank=rank, own_clusters=ow...]
  transfers between devices with their start and end apart: 6 -> 6, of which waited for: 1 -> 1; matrix products, arithmetic and copies ran while one was open for 0% -> 0% of each run, Pallas kernels for 7% -> 13%
where the time goes in v8:
time: 51.4 us; the launch traced here: 51 us
  Pallas kernels  22.8 us (44%)
  blocking collectives  16.3 us (32%)
  starting transfers between devices  10.2 us (20%)
  waiting for transfers between devices  0.93 us (2%)
  between operations  0.72 us (1%)
    all_to_all x2, blocking collectives, exchange(): return lax.all_to_all(send, 'src', split_axis=0, concat_axis=0, tiled=True)  16.3 us
    pallas_call x2, Pallas kernels, exchange(): pl.pallas_call(far_kernel, in_specs=[in_vmem] * (4 + recv_count) + [anywh...  12.5 us
    ppermute x6, starting transfers between devices, exchange(): lax.ppermute(deficit, 'recv', [(i, i ^ k) for i in range(recv_count)])  10.2 us
    pallas_call x1, Pallas kernels, on_device(): pl.pallas_call(ahead_kernel, in_specs=[in_vmem] * 3 + [anywhere] * 2, out...  3.46 us
    pallas_call x1, Pallas kernels, on_device(): pl.pallas_call(functools.partial(table_kernel, rank=rank, own_clusters=ow...  2.93 us
    pallas_call x1, Pallas kernels, on_device(): pl.pallas_call(final_kernel, in_specs=[in_vmem] * 5, out_specs=in_vmem, o...  1.74 us
    pallas_call x1, Pallas kernels, on_device(): pl.pallas_call(order_kernel, in_specs=[anywhere] * 7, out_specs=(in_vmem,...  1.14 us
    pallas_call x1, Pallas kernels, on_device(): pl.pallas_call(first_kernel, in_specs=[in_vmem] * 4, out_specs=(in_vmem,)...  1.04 us
  transfers between devices with their start and end apart: 6, of which 1 were waited for; matrix products, arithmetic and copies ran while one was open for 0% of the time, Pallas kernels for 13%

profile of v8, /device:TPU:0, one launch (start us, length us, event | category | flops | bytes accessed | tf_op | source)
XLA Modules:
  0.0 51.0 jit_solution(2389058636962961707)
XLA Ops:
  0.6 1.1 %shard_map.141 = (f32[8,16,128]{2,1,0:T(8,128)S(1)}, bf16[16,128]{1,0:T(8,128)(2,1)S(1)}, s32[16,128]{1,0:T(8,128)S(1)}) custom-call(f32[16,128]{1,0:T(8,128)} %bitcast.21, f32[16,128]{1,0:T(8,128)} %bitcast.22, f32[16,128]{1,0:T(8,128)} %bitcast.23, f32[16,128]{1,0:T(8,128)} %bitcast.24, f32[16,128]{1,0:T(8,128)} %bitcast.25, f32[16,128]{1,0:T(8,128)} %bitcast.26, ...), custom_call_target="tpu_custom_call" | custom-call | tf_op jit(solution)/shard_map/pallas_call | solution.py:340
  1.8 5.1 %collective-permute-start.2 = (bf16[16,128]{1,0:T(8,128)(2,1)S(1)}, bf16[16,128]{1,0:T(8,128)(2,1)S(1)}, u32[]{:S(2)}, u32[]{:S(2)}) collective-permute-start(bf16[16,128]{1,0:T(8,128)(2,1)S(1)} %get-tuple-element.20.refs_0_), channel_id=1, source_target_pairs={{0,24},{8,16},{16,8},{24,0},{1,25},{9,17},{17,9},{25,1},{2,26},{10... | collective-permute-start | bytes 12296 | tf_op jit(solution)/shard_map/ppermute | solution.py:386
  6.9 0.0 collective-permute-start.1
  6.9 0.6 %collective-permute-start = (bf16[16,128]{1,0:T(8,128)(2,1)S(1)}, bf16[16,128]{1,0:T(8,128)(2,1)S(1)}, u32[]{:S(2)}, u32[]{:S(2)}) collective-permute-start(bf16[16,128]{1,0:T(8,128)(2,1)S(1)} %get-tuple-element.20.refs_0_), channel_id=1, source_target_pairs={{0,8},{8,0},{16,24},{24,16},{1,9},{9,1},{17,25},{25,17},{2,10},{10... | collective-permute-start | bytes 12296 | tf_op jit(solution)/shard_map/ppermute | solution.py:386
  7.5 2.9 %shard_map.140 = (s32[256,128]{1,0:T(8,128)S(1)}, s32[96,128]{1,0:T(8,128)S(1)}, bf16[256,64]{1,0:T(8,128)(2,1)S(1)}, bf16[12288,128]{1,0:T(8,128)(2,1)S(1)}, bf16[12288,128]{1,0:T(8,128)(2,1)S(1)}) custom-call(s32[2,768]{1,0:T(2,128)} %near_hbm.1, s32[2,1024]{1,0:T(2,128)} %far_hbm.1, s32[8,128]{1,0:T(8,128)} %bitcast.28, bf16[32768,128]{1,0:T(8,128)(2,1)} %bitcast.12, ...), custom_call_target="tpu_custom_call" | custom-call | tf_op jit(solution)/shard_map/pallas_call | solution.py:361
  10.5 0.0 collective-permute-done.2.refs_3_
  10.5 0.9 %collective-permute-done.1.refs_2_ = bf16[16,128]{1,0:T(8,128)(2,1)S(1)} collective-permute-done((bf16[16,128]{1,0:T(8,128)(2,1)S(1)}, bf16[16,128]{1,0:T(8,128)(2,1)S(1)}, u32[]{:S(2)}, u32[]{:S(2)}) %collective-permute-start.1) | collective-permute-done | bytes 4128 | tf_op jit(solution)/shard_map/ppermute | solution.py:386
  11.4 0.0 collective-permute-done.refs_1_
  11.4 0.0 copy-start
  11.4 6.3 %shard_map.142 = bf16[8,48,128]{2,1,0:T(8,128)(2,1)S(1)} custom-call(s32[256,128]{1,0:T(8,128)S(1)} %get-tuple-element.18.code_ref, bf16[256,64]{1,0:T(8,128)(2,1)S(1)} %get-tuple-element.19.pick_ref, bf16[16,128]{1,0:T(8,128)(2,1)S(1)} %get-tuple-element.20.refs_0_, bf16[16,128]{1,0:T(8,128)(2,1)S(1)} %collective-permute-done.refs_1_, ...), custom_call_target="tpu_custom_call" | custom-call | flops 1610612736 | bytes 16777216 | tf_op jit(solution)/shard_map/pallas_call | solution.py:389
  17.7 8.7 %all_to_all.10.came_ref = bf16[8,48,128]{2,1,0:T(8,128)(2,1)S(1)} all-to-all(bf16[8,48,128]{2,1,0:T(8,128)(2,1)S(1)} %shard_map.142), channel_id=1, replica_groups=mesh['recv'=4,'src'=8] {'src'}, dimensions={0} | all-to-all | bytes 196608 | tf_op jit(solution)/shard_map/all_to_all | solution.py:405
  26.4 0.0 copy-done
  26.4 1.0 %shard_map.143 = (f32[16,128]{1,0:T(8,128)S(1)}, bf16[16,128]{1,0:T(8,128)(2,1)S(1)}) custom-call(s32[96,128]{1,0:T(8,128)S(1)} %get-tuple-element.17.code_ref, bf16[8,48,128]{2,1,0:T(8,128)(2,1)S(1)} %all_to_all.10.came_ref, bf16[96,128,128]{2,1,0:T(8,128)(2,1)S(1)} %copy-done, f32[8,16,128]{2,1,0:T(8,128)S(1)} %get-tuple-element.23.own_ref), custom_call_target="tpu_custom_call" | custom-call | tf_op jit(solution)/shard_map/pallas_call | solution.py:408
  27.5 2.9 %collective-permute-start.5 = (bf16[16,128]{1,0:T(8,128)(2,1)S(1)}, bf16[16,128]{1,0:T(8,128)(2,1)S(1)}, u32[]{:S(2)}, u32[]{:S(2)}) collective-permute-start(bf16[16,128]{1,0:T(8,128)(2,1)S(1)} %get-tuple-element.24.refs_0_), channel_id=1, source_target_pairs={{0,24},{8,16},{16,8},{24,0},{1,25},{9,17},{17,9},{25,1},{2,26},{10... | collective-permute-start | bytes 12296 | tf_op jit(solution)/shard_map/ppermute | solution.py:386
  30.4 0.0 collective-permute-start.4
  30.4 1.5 %collective-permute-start.3 = (bf16[16,128]{1,0:T(8,128)(2,1)S(1)}, bf16[16,128]{1,0:T(8,128)(2,1)S(1)}, u32[]{:S(2)}, u32[]{:S(2)}) collective-permute-start(bf16[16,128]{1,0:T(8,128)(2,1)S(1)} %get-tuple-element.24.refs_0_), channel_id=1, source_target_pairs={{0,8},{8,0},{16,24},{24,16},{1,9},{9,1},{17,25},{25,17},{2,10},{10... | collective-permute-start | bytes 12296 | tf_op jit(solution)/shard_map/ppermute | solution.py:386
  31.9 3.5 %shard_map.144 = (f32[2,16,128]{2,1,0:T(8,128)S(1)}, s32[2,16,128]{2,1,0:T(8,128)S(1)}, f32[16,128]{1,0:T(8,128)}, bf16[12288,128]{1,0:T(8,128)(2,1)S(1)}, bf16[12288,128]{1,0:T(8,128)(2,1)S(1)}) custom-call(f32[8,16,128]{2,1,0:T(8,128)S(1)} %get-tuple-element.23.own_ref, f32[16,128]{1,0:T(8,128)S(1)} %get-tuple-element.25.first_ref, ...), custom_call_target="tpu_custom_call" | custom-call | tf_op jit(solution)/shard_map/pallas_call | solution.py:415
  35.4 0.0 collective-permute-done.5.refs_3_
  35.4 0.0 collective-permute-done.4.refs_2_
  35.4 0.0 collective-permute-done.3.refs_1_
  35.4 6.2 %shard_map.145 = bf16[8,48,128]{2,1,0:T(8,128)(2,1)S(1)} custom-call(s32[256,128]{1,0:T(8,128)S(1)} %get-tuple-element.18.code_ref, bf16[256,64]{1,0:T(8,128)(2,1)S(1)} %get-tuple-element.19.pick_ref, bf16[16,128]{1,0:T(8,128)(2,1)S(1)} %get-tuple-element.24.refs_0_, bf16[16,128]{1,0:T(8,128)(2,1)S(1)} %collective-permute-done.3.refs_1_, ...), custom_call_target="tpu_custom_call" | custom-call | flops 1610612736 | bytes 16777216 | tf_op jit(solution)/shard_map/pallas_call | solution.py:389
  41.7 7.6 %all_to_all.11.came_ref = bf16[8,48,128]{2,1,0:T(8,128)(2,1)S(1)} all-to-all(bf16[8,48,128]{2,1,0:T(8,128)(2,1)S(1)} %shard_map.145), channel_id=1, replica_groups=mesh['recv'=4,'src'=8] {'src'}, dimensions={0} | all-to-all | bytes 196608 | tf_op jit(solution)/shard_map/all_to_all | solution.py:405
  49.2 1.7 %shard_map.146 = f32[16,128]{1,0:T(8,128)} custom-call(s32[96,128]{1,0:T(8,128)S(1)} %get-tuple-element.17.code_ref, bf16[8,48,128]{2,1,0:T(8,128)(2,1)S(1)} %all_to_all.11.came_ref, bf16[96,128,128]{2,1,0:T(8,128)(2,1)S(1)} %copy-done, f32[2,16,128]{2,1,0:T(8,128)S(1)} %get-tuple-element.29.keep_ref, s32[2,16,128]{2,1,0:T(8,128)S(1)} %get-tuple-element.30.back_ref), custom_call_target="tpu_custom_call" | custom-call | tf_op jit(solution)/shard_map/pallas_call | solution.py:429
Async XLA Ops:
  1.8 8.7 %collective-permute-start.2 = (bf16[16,128]{1,0:T(8,128)(2,1)S(1)}, bf16[16,128]{1,0:T(8,128)(2,1)S(1)}, u32[]{:S(2)}, u32[]{:S(2)}) collective-permute-start(bf16[16,128]{1,0:T(8,128)(2,1)S(1)} %get-tuple-element.20.refs_0_), channel_id=1, source_target_pairs={{0,24},{8,16},{16,8},{24,0},{1,25},{9,17},{17,9},{25,1},{2,26},{10... | collective-permute-start | bytes 12296 | tf_op jit(solution)/shard_map/ppermute | solution.py:386
  6.9 4.5 %collective-permute-start.1 = (bf16[16,128]{1,0:T(8,128)(2,1)S(1)}, bf16[16,128]{1,0:T(8,128)(2,1)S(1)}, u32[]{:S(2)}, u32[]{:S(2)}) collective-permute-start(bf16[16,128]{1,0:T(8,128)(2,1)S(1)} %get-tuple-element.20.refs_0_), channel_id=1, source_target_pairs={{0,16},{8,24},{16,0},{24,8},{1,17},{9,25},{17,1},{25,9},{2,18},{10... | collective-permute-start | bytes 12296 | tf_op jit(solution)/shard_map/ppermute | solution.py:386
  6.9 4.5 %collective-permute-start = (bf16[16,128]{1,0:T(8,128)(2,1)S(1)}, bf16[16,128]{1,0:T(8,128)(2,1)S(1)}, u32[]{:S(2)}, u32[]{:S(2)}) collective-permute-start(bf16[16,128]{1,0:T(8,128)(2,1)S(1)} %get-tuple-element.20.refs_0_), channel_id=1, source_target_pairs={{0,8},{8,0},{16,24},{24,16},{1,9},{9,1},{17,25},{25,17},{2,10},{10... | collective-permute-start | bytes 12296 | tf_op jit(solution)/shard_map/ppermute | solution.py:386
  11.4 15.0 %copy-start = (bf16[96,128,128]{2,1,0:T(8,128)(2,1)S(1)}, bf16[96,128,128]{2,1,0:T(8,128)(2,1)}, u32[]{:S(2)}) copy-start(bf16[96,128,128]{2,1,0:T(8,128)(2,1)} %tile_ref.3) | copy-start | bytes 9437188
  27.5 7.9 %collective-permute-start.5 = (bf16[16,128]{1,0:T(8,128)(2,1)S(1)}, bf16[16,128]{1,0:T(8,128)(2,1)S(1)}, u32[]{:S(2)}, u32[]{:S(2)}) collective-permute-start(bf16[16,128]{1,0:T(8,128)(2,1)S(1)} %get-tuple-element.24.refs_0_), channel_id=1, source_target_pairs={{0,24},{8,16},{16,8},{24,0},{1,25},{9,17},{17,9},{25,1},{2,26},{10... | collective-permute-start | bytes 12296 | tf_op jit(solution)/shard_map/ppermute | solution.py:386
  30.4 5.0 %collective-permute-start.4 = (bf16[16,128]{1,0:T(8,128)(2,1)S(1)}, bf16[16,128]{1,0:T(8,128)(2,1)S(1)}, u32[]{:S(2)}, u32[]{:S(2)}) collective-permute-start(bf16[16,128]{1,0:T(8,128)(2,1)S(1)} %get-tuple-element.24.refs_0_), channel_id=1, source_target_pairs={{0,16},{8,24},{16,0},{24,8},{1,17},{9,25},{17,1},{25,9},{2,18},{10... | collective-permute-start | bytes 12296 | tf_op jit(solution)/shard_map/ppermute | solution.py:386
  30.4 5.0 %collective-permute-start.3 = (bf16[16,128]{1,0:T(8,128)(2,1)S(1)}, bf16[16,128]{1,0:T(8,128)(2,1)S(1)}, u32[]{:S(2)}, u32[]{:S(2)}) collective-permute-start(bf16[16,128]{1,0:T(8,128)(2,1)S(1)} %get-tuple-element.24.refs_0_), channel_id=1, source_target_pairs={{0,8},{8,0},{16,24},{24,16},{1,9},{9,1},{17,25},{25,17},{2,10},{10... | collective-permute-start | bytes 12296 | tf_op jit(solution)/shard_map/ppermute | solution.py:386

commit v9 on v8

--- a/solution.py
+++ b/solution.py
@@ -36,27 +36,20 @@
     return out
 
 
-def order_kernel(*refs):
-    arguments, (own_ref, deficit_ref, order_out, buf, order_buf, sems) = refs[:7], refs[7:]
-    count = len(arguments) - 1
+def order_kernel(p_hbm, plate_hbm, order_hbm, own_ref, deficit_ref, order_ref, buf, sems):
     copies = [
-        pltpu.make_async_copy(ref, order_buf if k == count else buf.at[k], sems.at[k])
-        for k, ref in enumerate(arguments)
+        pltpu.make_async_copy(there, here, sems.at[k])
+        for k, (there, here) in enumerate(((p_hbm, buf.at[0]), (plate_hbm, buf.at[1]), (order_hbm, order_ref)))
     ]
     for copy in copies:
         copy.start()
     for copy in copies:
         copy.wait()
-    order = order_buf[...]
-    order_out[...] = order
-    row, lane = order // lanes, order % lanes
-    p, q, a, b, slip, plate = gather_rows([buf[k] for k in range(count)], row, lane)
-    speed = jnp.exp(p)
-    theta_rate = jnp.exp(-q) - speed / slip
-    gain = 1.0 / (a + damping * speed)
-    for k, value in enumerate((p, q, a, b, slip, plate, theta_rate, gain)):
-        own_ref[k] = value
-    deficit_ref[...] = (plate - speed).astype(bf16)
+    order = order_ref[...]
+    p, plate = gather_rows((buf[0], buf[1]), order // lanes, order % lanes)
+    own_ref[0] = p
+    own_ref[1] = plate
+    deficit_ref[...] = (plate - jnp.exp(p)).astype(bf16)
 
 
 def head_copies(v_hbm, u_hbm, v_out, u_out, sems):
@@ -70,14 +63,14 @@
 
 
 def table_kernel(
-    near_hbm, far_hbm, rank_hbm, v_hbm, u_hbm, far_out, near_out, pick_out, v_out, u_out,
-    near_pairs, far_pairs, rank_ref, sems, head_sems, *,
+    near_hbm, far_hbm, rank_hbm, q_hbm, a_hbm, b_hbm, slip_hbm, v_hbm, u_hbm, mine_ref, order_ref,
+    far_out, near_out, pick_out, own_out, v_out, u_out,
+    near_pairs, far_pairs, rank_ref, buf, sems, head_sems, *,
     rank, own_clusters, src_count, capacity,
 ):
-    copies = [
-        pltpu.make_async_copy(there, here, sems.at[k])
-        for k, (there, here) in enumerate(((near_hbm, near_pairs), (far_hbm, far_pairs), (rank_hbm, rank_ref)))
-    ]
+    ends = [(near_hbm, near_pairs), (far_hbm, far_pairs), (rank_hbm, rank_ref)]
+    ends += [(there, buf.at[k]) for k, there in enumerate((q_hbm, a_hbm, b_hbm, slip_hbm))]
+    copies = [pltpu.make_async_copy(there, here, sems.at[k]) for k, (there, here) in enumerate(ends)]
     for copy in copies:
         copy.start()
     heads = head_copies(v_hbm, u_hbm, v_out, u_out, head_sems)
@@ -148,6 +141,14 @@
         far_out[a * group : (a + 1) * group, :] = jnp.where(
             lane % rank < spread(rank_ref[a : a + 1, :]), source, missing
         )
+    order = order_ref[...]
+    q, a, b, slip = gather_rows([buf[k] for k in range(4)], order // lanes, order % lanes)
+    p, plate = mine_ref[0], mine_ref[1]
+    speed = jnp.exp(p)
+    theta_rate = jnp.exp(-q) - speed / slip
+    gain = 1.0 / (a + damping * speed)
+    for k, value in enumerate((p, q, a, b, slip, plate, theta_rate, gain)):
+        own_out[k] = value
     for copy in heads:
         copy.wait()
 
@@ -337,37 +338,35 @@
     whole = (own_clusters, lanes)
 
     arguments = [x.reshape(whole) for x in (log_rate, log_state, a_sigma, b_sigma, crit_slip, plate_rate)]
-    own, first_deficit, order = pl.pallas_call(
+    p_hbm, q_hbm, a_hbm, b_hbm, slip_hbm, plate_hbm = [in_hbm(x) for x in arguments]
+    mine, first_deficit, order = pl.pallas_call(
         order_kernel,
-        in_specs=[anywhere] * 7,
+        in_specs=[anywhere] * 3,
         out_specs=(in_vmem,) * 3,
         out_shape=(
-            jax.ShapeDtypeStruct((8,) + whole, f32),
+            jax.ShapeDtypeStruct((2,) + whole, f32),
             jax.ShapeDtypeStruct(whole, bf16),
             jax.ShapeDtypeStruct(whole, jnp.int32),
         ),
-        scratch_shapes=[
-            pltpu.VMEM((6,) + whole, f32),
-            pltpu.VMEM(whole, jnp.int32),
-            pltpu.SemaphoreType.DMA((7,)),
-        ],
+        scratch_shapes=[pltpu.VMEM((2,) + whole, f32), pltpu.SemaphoreType.DMA((3,))],
         compiler_params=params,
-    )(*[in_hbm(x) for x in arguments + [cluster_order.reshape(whole)]])
+    )(p_hbm, plate_hbm, in_hbm(cluster_order.reshape(whole)))
 
     v_rows = in_hbm(far_v.reshape(factor_rows, lanes))
     u_rows = in_hbm(far_u.reshape(factor_rows, lanes))
     head = jax.ShapeDtypeStruct((factor_rows // chunks * bodies[0], lanes), bf16)
     capacity = -(-max(2, 2 * tile_count // src_count) // 16) * 16
-    far_codes, near_codes, picks, *first_heads = pl.pallas_call(
+    far_codes, near_codes, picks, own, *first_heads = pl.pallas_call(
         functools.partial(
             table_kernel, rank=rank, own_clusters=own_clusters, src_count=src_count, capacity=capacity
         ),
-        in_specs=[anywhere] * 5,
-        out_specs=(in_vmem,) * 5,
+        in_specs=[anywhere] * 9 + [in_vmem] * 2,
+        out_specs=(in_vmem,) * 6,
         out_shape=(
             jax.ShapeDtypeStruct((factor_rows // lanes, lanes), jnp.int32),
             jax.ShapeDtypeStruct((tile_count, lanes), jnp.int32),
             jax.ShapeDtypeStruct((src_count * capacity, source_rows), bf16),
+            jax.ShapeDtypeStruct((8,) + whole, f32),
             head,
             head,
         ),
@@ -375,11 +374,12 @@
             pltpu.VMEM(near_pairs.shape, jnp.int32),
             pltpu.VMEM(far_pairs.shape, jnp.int32),
             pltpu.VMEM((far_count // lanes, lanes), jnp.int32),
-            pltpu.SemaphoreType.DMA((3,)),
+            pltpu.VMEM((4,) + whole, f32),
+            pltpu.SemaphoreType.DMA((7,)),
             pltpu.SemaphoreType.DMA((2,)),
         ],
         compiler_params=params,
-    )(*[in_hbm(x) for x in (near_pairs, far_pairs, far_ranks.reshape(far_count // lanes, lanes))], v_rows, u_rows)
+    )(*[in_hbm(x) for x in (near_pairs, far_pairs, far_ranks.reshape(far_count // lanes, lanes))], q_hbm, a_hbm, b_hbm, slip_hbm, v_rows, u_rows, mine, order)
 
     def exchange(deficit, heads):
         parts = [deficit] + [

time: 51.4 us -> 51.1 us (level)
  no operation moved by 1% of the time
where the time goes in v9:
time: 51.1 us; the launch traced here: 50.8 us
  Pallas kernels  22.7 us (44%)
  blocking collectives  16.3 us (32%)
  starting transfers between devices  10.2 us (20%)
  waiting for transfers between devices  0.82 us (2%)
  between operations  0.72 us (1%)
    all_to_all x2, blocking collectives, exchange(): return lax.all_to_all(send, 'src', split_axis=0, concat_axis=0, tiled=True)  16.3 us
    pallas_call x2, Pallas kernels, exchange(): pl.pallas_call(far_kernel, in_specs=[in_vmem] * (4 + recv_count) + [anywh...  12.5 us
    ppermute x6, starting transfers between devices, exchange(): lax.ppermute(deficit, 'recv', [(i, i ^ k) for i in range(recv_count)])  10.2 us
    pallas_call x1, Pallas kernels, on_device(): pl.pallas_call(ahead_kernel, in_specs=[in_vmem] * 3 + [anywhere] * 2, out...  3.46 us
    pallas_call x1, Pallas kernels, on_device(): pl.pallas_call(functools.partial(table_kernel, rank=rank, own_clusters=ow...  3.04 us
    pallas_call x1, Pallas kernels, on_device(): pl.pallas_call(final_kernel, in_specs=[in_vmem] * 5, out_specs=in_vmem, o...  1.74 us
    pallas_call x1, Pallas kernels, on_device(): pl.pallas_call(first_kernel, in_specs=[in_vmem] * 4, out_specs=(in_vmem,)...  1.04 us
  transfers between devices with their start and end apart: 6, of which 1 were waited for; matrix products, arithmetic and copies ran while one was open for 0% of the time, Pallas kernels for 13%

profile of v9, /device:TPU:0, one launch (start us, length us, event | category | flops | bytes accessed | tf_op | source)
XLA Modules:
  0.0 50.8 jit_solution(11130160351553485530)
XLA Ops:
  0.6 0.9 %shard_map.140 = (f32[2,16,128]{2,1,0:T(8,128)S(1)}, bf16[16,128]{1,0:T(8,128)(2,1)S(1)}, s32[16,128]{1,0:T(8,128)S(1)}) custom-call(f32[16,128]{1,0:T(8,128)} %bitcast.25, f32[16,128]{1,0:T(8,128)} %bitcast.26, s32[16,128]{1,0:T(8,128)} %bitcast.27), custom_call_target="tpu_custom_call" | custom-call | tf_op jit(solution)/shard_map/pallas_call | solution.py:342
  1.6 5.1 %collective-permute-start.2 = (bf16[16,128]{1,0:T(8,128)(2,1)S(1)}, bf16[16,128]{1,0:T(8,128)(2,1)S(1)}, u32[]{:S(2)}, u32[]{:S(2)}) collective-permute-start(bf16[16,128]{1,0:T(8,128)(2,1)S(1)} %get-tuple-element.23.refs_0_), channel_id=1, source_target_pairs={{0,24},{8,16},{16,8},{24,0},{1,25},{9,17},{17,9},{25,1},{2,26},{10... | collective-permute-start | bytes 12296 | tf_op jit(solution)/shard_map/ppermute | solution.py:386
  6.7 0.0 collective-permute-start.1
  6.7 0.6 %collective-permute-start = (bf16[16,128]{1,0:T(8,128)(2,1)S(1)}, bf16[16,128]{1,0:T(8,128)(2,1)S(1)}, u32[]{:S(2)}, u32[]{:S(2)}) collective-permute-start(bf16[16,128]{1,0:T(8,128)(2,1)S(1)} %get-tuple-element.23.refs_0_), channel_id=1, source_target_pairs={{0,8},{8,0},{16,24},{24,16},{1,9},{9,1},{17,25},{25,17},{2,10},{10... | collective-permute-start | bytes 12296 | tf_op jit(solution)/shard_map/ppermute | solution.py:386
  7.3 3.0 %shard_map.141 = (s32[256,128]{1,0:T(8,128)S(1)}, s32[96,128]{1,0:T(8,128)S(1)}, bf16[256,64]{1,0:T(8,128)(2,1)S(1)}, f32[8,16,128]{2,1,0:T(8,128)S(1)}, bf16[12...) custom-call(s32[2,768]{1,0:T(2,128)} %near_hbm.1, s32[2,1024]{1,0:T(2,128)} %far_hbm.1, s32[8,128]{1,0:T(8,128)} %bitcast.28, ...), custom_call_target="tpu_custom_call" | custom-call | tf_op jit(solution)/shard_map/pallas_call | solution.py:359
  10.4 0.0 collective-permute-done.2.refs_3_
  10.4 0.8 %collective-permute-done.1.refs_2_ = bf16[16,128]{1,0:T(8,128)(2,1)S(1)} collective-permute-done((bf16[16,128]{1,0:T(8,128)(2,1)S(1)}, bf16[16,128]{1,0:T(8,128)(2,1)S(1)}, u32[]{:S(2)}, u32[]{:S(2)}) %collective-permute-start.1) | collective-permute-done | bytes 4128 | tf_op jit(solution)/shard_map/ppermute | solution.py:386
  11.2 0.0 collective-permute-done.refs_1_
  11.2 0.0 copy-start
  11.2 6.3 %shard_map.142 = bf16[8,48,128]{2,1,0:T(8,128)(2,1)S(1)} custom-call(s32[256,128]{1,0:T(8,128)S(1)} %get-tuple-element.21.code_ref, bf16[256,64]{1,0:T(8,128)(2,1)S(1)} %get-tuple-element.22.pick_ref, bf16[16,128]{1,0:T(8,128)(2,1)S(1)} %get-tuple-element.23.refs_0_, bf16[16,128]{1,0:T(8,128)(2,1)S(1)} %collective-permute-done.refs_1_, ...), custom_call_target="tpu_custom_call" | custom-call | flops 1610612736 | bytes 16777216 | tf_op jit(solution)/shard_map/pallas_call | solution.py:389
  17.5 8.7 %all_to_all.10.came_ref = bf16[8,48,128]{2,1,0:T(8,128)(2,1)S(1)} all-to-all(bf16[8,48,128]{2,1,0:T(8,128)(2,1)S(1)} %shard_map.142), channel_id=1, replica_groups=mesh['recv'=4,'src'=8] {'src'}, dimensions={0} | all-to-all | bytes 196608 | tf_op jit(solution)/shard_map/all_to_all | solution.py:405
  26.2 0.0 copy-done
  26.2 1.0 %shard_map.143 = (f32[16,128]{1,0:T(8,128)S(1)}, bf16[16,128]{1,0:T(8,128)(2,1)S(1)}) custom-call(s32[96,128]{1,0:T(8,128)S(1)} %get-tuple-element.20.code_ref, bf16[8,48,128]{2,1,0:T(8,128)(2,1)S(1)} %all_to_all.10.came_ref, bf16[96,128,128]{2,1,0:T(8,128)(2,1)S(1)} %copy-done, f32[8,16,128]{2,1,0:T(8,128)S(1)} %get-tuple-element.26.own_ref), custom_call_target="tpu_custom_call" | custom-call | tf_op jit(solution)/shard_map/pallas_call | solution.py:408
  27.3 3.0 %collective-permute-start.5 = (bf16[16,128]{1,0:T(8,128)(2,1)S(1)}, bf16[16,128]{1,0:T(8,128)(2,1)S(1)}, u32[]{:S(2)}, u32[]{:S(2)}) collective-permute-start(bf16[16,128]{1,0:T(8,128)(2,1)S(1)} %get-tuple-element.27.refs_0_), channel_id=1, source_target_pairs={{0,24},{8,16},{16,8},{24,0},{1,25},{9,17},{17,9},{25,1},{2,26},{10... | collective-permute-start | bytes 12296 | tf_op jit(solution)/shard_map/ppermute | solution.py:386
  30.3 0.0 collective-permute-start.4
  30.3 1.4 %collective-permute-start.3 = (bf16[16,128]{1,0:T(8,128)(2,1)S(1)}, bf16[16,128]{1,0:T(8,128)(2,1)S(1)}, u32[]{:S(2)}, u32[]{:S(2)}) collective-permute-start(bf16[16,128]{1,0:T(8,128)(2,1)S(1)} %get-tuple-element.27.refs_0_), channel_id=1, source_target_pairs={{0,8},{8,0},{16,24},{24,16},{1,9},{9,1},{17,25},{25,17},{2,10},{10... | collective-permute-start | bytes 12296 | tf_op jit(solution)/shard_map/ppermute | solution.py:386
  31.7 3.5 %shard_map.144 = (f32[2,16,128]{2,1,0:T(8,128)S(1)}, s32[2,16,128]{2,1,0:T(8,128)S(1)}, f32[16,128]{1,0:T(8,128)}, bf16[12288,128]{1,0:T(8,128)(2,1)S(1)}, bf16[12288,128]{1,0:T(8,128)(2,1)S(1)}) custom-call(f32[8,16,128]{2,1,0:T(8,128)S(1)} %get-tuple-element.26.own_ref, f32[16,128]{1,0:T(8,128)S(1)} %get-tuple-element.28.first_ref, ...), custom_call_target="tpu_custom_call" | custom-call | tf_op jit(solution)/shard_map/pallas_call | solution.py:415
  35.2 0.0 collective-permute-done.5.refs_3_
  35.2 0.0 collective-permute-done.4.refs_2_
  35.2 0.0 collective-permute-done.3.refs_1_
  35.2 6.2 %shard_map.145 = bf16[8,48,128]{2,1,0:T(8,128)(2,1)S(1)} custom-call(s32[256,128]{1,0:T(8,128)S(1)} %get-tuple-element.21.code_ref, bf16[256,64]{1,0:T(8,128)(2,1)S(1)} %get-tuple-element.22.pick_ref, bf16[16,128]{1,0:T(8,128)(2,1)S(1)} %get-tuple-element.27.refs_0_, bf16[16,128]{1,0:T(8,128)(2,1)S(1)} %collective-permute-done.3.refs_1_, ...), custom_call_target="tpu_custom_call" | custom-call | flops 1610612736 | bytes 16777216 | tf_op jit(solution)/shard_map/pallas_call | solution.py:389
  41.4 7.6 %all_to_all.11.came_ref = bf16[8,48,128]{2,1,0:T(8,128)(2,1)S(1)} all-to-all(bf16[8,48,128]{2,1,0:T(8,128)(2,1)S(1)} %shard_map.145), channel_id=1, replica_groups=mesh['recv'=4,'src'=8] {'src'}, dimensions={0} | all-to-all | bytes 196608 | tf_op jit(solution)/shard_map/all_to_all | solution.py:405
  49.0 1.7 %shard_map.146 = f32[16,128]{1,0:T(8,128)} custom-call(s32[96,128]{1,0:T(8,128)S(1)} %get-tuple-element.20.code_ref, bf16[8,48,128]{2,1,0:T(8,128)(2,1)S(1)} %all_to_all.11.came_ref, bf16[96,128,128]{2,1,0:T(8,128)(2,1)S(1)} %copy-done, f32[2,16,128]{2,1,0:T(8,128)S(1)} %get-tuple-element.31.keep_ref, s32[2,16,128]{2,1,0:T(8,128)S(1)} %get-tuple-element.32.back_ref), custom_call_target="tpu_custom_call" | custom-call | tf_op jit(solution)/shard_map/pallas_call | solution.py:429
Async XLA Ops:
  1.6 8.8 %collective-permute-start.2 = (bf16[16,128]{1,0:T(8,128)(2,1)S(1)}, bf16[16,128]{1,0:T(8,128)(2,1)S(1)}, u32[]{:S(2)}, u32[]{:S(2)}) collective-permute-start(bf16[16,128]{1,0:T(8,128)(2,1)S(1)} %get-tuple-element.23.refs_0_), channel_id=1, source_target_pairs={{0,24},{8,16},{16,8},{24,0},{1,25},{9,17},{17,9},{25,1},{2,26},{10... | collective-permute-start | bytes 12296 | tf_op jit(solution)/shard_map/ppermute | solution.py:386
  6.7 4.5 %collective-permute-start.1 = (bf16[16,128]{1,0:T(8,128)(2,1)S(1)}, bf16[16,128]{1,0:T(8,128)(2,1)S(1)}, u32[]{:S(2)}, u32[]{:S(2)}) collective-permute-start(bf16[16,128]{1,0:T(8,128)(2,1)S(1)} %get-tuple-element.23.refs_0_), channel_id=1, source_target_pairs={{0,16},{8,24},{16,0},{24,8},{1,17},{9,25},{17,1},{25,9},{2,18},{10... | collective-permute-start | bytes 12296 | tf_op jit(solution)/shard_map/ppermute | solution.py:386
  6.7 4.5 %collective-permute-start = (bf16[16,128]{1,0:T(8,128)(2,1)S(1)}, bf16[16,128]{1,0:T(8,128)(2,1)S(1)}, u32[]{:S(2)}, u32[]{:S(2)}) collective-permute-start(bf16[16,128]{1,0:T(8,128)(2,1)S(1)} %get-tuple-element.23.refs_0_), channel_id=1, source_target_pairs={{0,8},{8,0},{16,24},{24,16},{1,9},{9,1},{17,25},{25,17},{2,10},{10... | collective-permute-start | bytes 12296 | tf_op jit(solution)/shard_map/ppermute | solution.py:386
  11.2 15.0 %copy-start = (bf16[96,128,128]{2,1,0:T(8,128)(2,1)S(1)}, bf16[96,128,128]{2,1,0:T(8,128)(2,1)}, u32[]{:S(2)}) copy-start(bf16[96,128,128]{2,1,0:T(8,128)(2,1)} %tile_ref.3) | copy-start | bytes 9437188
  27.3 7.9 %collective-permute-start.5 = (bf16[16,128]{1,0:T(8,128)(2,1)S(1)}, bf16[16,128]{1,0:T(8,128)(2,1)S(1)}, u32[]{:S(2)}, u32[]{:S(2)}) collective-permute-start(bf16[16,128]{1,0:T(8,128)(2,1)S(1)} %get-tuple-element.27.refs_0_), channel_id=1, source_target_pairs={{0,24},{8,16},{16,8},{24,0},{1,25},{9,17},{17,9},{25,1},{2,26},{10... | collective-permute-start | bytes 12296 | tf_op jit(solution)/shard_map/ppermute | solution.py:386
  30.3 4.9 %collective-permute-start.4 = (bf16[16,128]{1,0:T(8,128)(2,1)S(1)}, bf16[16,128]{1,0:T(8,128)(2,1)S(1)}, u32[]{:S(2)}, u32[]{:S(2)}) collective-permute-start(bf16[16,128]{1,0:T(8,128)(2,1)S(1)} %get-tuple-element.27.refs_0_), channel_id=1, source_target_pairs={{0,16},{8,24},{16,0},{24,8},{1,17},{9,25},{17,1},{25,9},{2,18},{10... | collective-permute-start | bytes 12296 | tf_op jit(solution)/shard_map/ppermute | solution.py:386
  30.3 4.9 %collective-permute-start.3 = (bf16[16,128]{1,0:T(8,128)(2,1)S(1)}, bf16[16,128]{1,0:T(8,128)(2,1)S(1)}, u32[]{:S(2)}, u32[]{:S(2)}) collective-permute-start(bf16[16,128]{1,0:T(8,128)(2,1)S(1)} %get-tuple-element.27.refs_0_), channel_id=1, source_target_pairs={{0,8},{8,0},{16,24},{24,16},{1,9},{9,1},{17,25},{25,17},{2,10},{10... | collective-permute-start | bytes 12296 | tf_op jit(solution)/shard_map/ppermute | solution.py:386
